TPU v7x, 32 devices: a whole 2x2x4 slice. The times are simulated.
32 devices in a mesh: fsdp: 32 (over z, y, x, core).
Axes of the slice: x: 2, y: 2, z: 4, core: 2. Of those that a mesh axis runs over, the one named last changes fastest.
Arguments:
- tokens: bfloat16 [8192, 2048], P('fsdp'), may hold values from -6 to 6
- cotangent: bfloat16 [8192, 2048], P('fsdp'), may hold values from -6 to 6
- block_first: int32 [64], P('fsdp'), may hold values from 0 to 1, as said below
- block_live: int32 [64], P('fsdp'), may hold values from 0 to 128, as said below
- w_qkv: float32 [2048, 6144], P('fsdp')
- w_attn_out: float32 [2048, 2048], P('fsdp'), may hold values from -1 to 1
- w_mlp_in: float32 [2048, 8192], P('fsdp'), may hold values from -0.125 to 0.125
- w_mlp_out: float32 [2048, 8192], P('fsdp'), may hold values from -0.0625 to 0.0625
- vectors: float32 [24576], P('fsdp')
- first_qkv: float32 [2048, 6144], P('fsdp'), may hold values from -6 to 6
- second_qkv: float32 [2048, 6144], P('fsdp'), may hold values from 204.8 to 3276.8
- first_attn_out: float32 [2048, 2048], P('fsdp'), may hold values from -6 to 6
- second_attn_out: float32 [2048, 2048], P('fsdp'), may hold values from 18.432 to 294.912
- first_mlp_in: float32 [2048, 8192], P('fsdp'), may hold values from -6 to 6
- second_mlp_in: float32 [2048, 8192], P('fsdp'), may hold values from 51.2 to 819.2
- first_mlp_out: float32 [2048, 8192], P('fsdp'), may hold values from -6 to 6
- second_mlp_out: float32 [2048, 8192], P('fsdp'), may hold values from 32.768 to 524.288
- first_vectors: float32 [24576], P('fsdp'), may hold values from -6 to 6
- second_vectors: float32 [24576], P('fsdp'), may hold values from 3276.8 to 52428.8
Outputs:
- out: bfloat16 [8192, 2048], P('fsdp')
- grad_tokens: bfloat16 [8192, 2048], P('fsdp')
- grad_qkv: float32 [2048, 6144], P('fsdp')
- grad_attn_out: float32 [2048, 2048], P('fsdp')
- grad_mlp_in: float32 [2048, 8192], P('fsdp')
- grad_mlp_out: float32 [2048, 8192], P('fsdp')
- grad_vectors: float32 [24576], P('fsdp')
- new_qkv: float32 [2048, 6144], P('fsdp')
- new_attn_out: float32 [2048, 2048], P('fsdp')
- new_mlp_in: float32 [2048, 8192], P('fsdp')
- new_mlp_out: float32 [2048, 8192], P('fsdp')
- new_vectors: float32 [24576], P('fsdp')
- new_first_qkv: float32 [2048, 6144], P('fsdp')
- new_second_qkv: float32 [2048, 6144], P('fsdp')
- new_first_attn_out: float32 [2048, 2048], P('fsdp')
- new_second_attn_out: float32 [2048, 2048], P('fsdp')
- new_first_mlp_in: float32 [2048, 8192], P('fsdp')
- new_second_mlp_in: float32 [2048, 8192], P('fsdp')
- new_first_mlp_out: float32 [2048, 8192], P('fsdp')
- new_second_mlp_out: float32 [2048, 8192], P('fsdp')
- new_first_vectors: float32 [24576], P('fsdp')
- new_second_vectors: float32 [24576], P('fsdp')
Inputs may be any that keep to these rules, and one draw needn't show every extreme that they name: Each device holds 2 blocks of 128 slots. A sequence fills consecutive blocks of one device, every block of it full but its last, which holds 1 to 128 live slots at its start; block_first gives its first block's index among the device's blocks. Blocks of no sequence follow the used ones of their device, with block_live 0 and block_first their own index. The first device holds one sequence of 256 live tokens. `block_live`: as for block_first.
All inputs are finite; a program needn't handle non-finite values.
Results may differ from a plain program's by a relative error of at most 0.012.
Values may be sent and summed in bfloat16 or wider, within the bound.
No kernel may reach another device: no remote copies, remote signals or barrier semaphores. Data moves between devices by JAX's collectives and lax.ppermute only.
A program may use at most 832 MiB of HBM per device.

v0:
```python
import jax
import jax.numpy as jnp
from jax import lax
from jax.sharding import PartitionSpec as P

D = 2048
HEADS = 8
HEAD = 256
FF = 8192
ROT = 64
BLOCK = 128
BLK_DEV = 2
STEP = 3
COLS = 24576
VEC = 24576


eps_norm = 1e-05
beta_one = 0.9
beta_two = 0.95
learn_rate = 0.03
vector_rate = 0.3
decay_matrix = 0.1
eps_adam = 1e-08
masked_score = -1e30
contract_rows = (((0,), (0,)), ((), ()))
contract_cols = (((1,), (1,)), ((), ()))


def layer_norm(values, gain_vec, shift_vec):
    row_mean = jnp.mean(values, axis=-1, keepdims=True)
    centred = values - row_mean
    spread = jnp.mean(centred * centred, axis=-1, keepdims=True)
    return centred * lax.rsqrt(spread + eps_norm) * gain_vec + shift_vec


def gelu_exact(values):
    return jax.nn.gelu(values, approximate=False)


def split_vectors(vec_all):
    boundaries = [D, 2 * D, 3 * D, 3 * D + FF, 4 * D + FF, 5 * D + FF, 6 * D + FF, 7 * D + FF]
    b_query, b_value, b_att, b_in, b_mlp, gain_one, shift_one, gain_two, shift_two = jnp.split(
        vec_all, boundaries
    )
    b_qkv = jnp.concatenate([b_query, jnp.zeros_like(b_query), b_value])
    return (b_qkv, b_att, b_in, b_mlp, gain_one, shift_one, gain_two, shift_two)


def slot_tables(first_blocks, live_blocks, slot_total):
    slot_index = jnp.arange(slot_total, dtype=jnp.int32)
    seq_of = jnp.broadcast_to(first_blocks[:, None], (BLK_DEV, BLOCK)).reshape(slot_total)
    live_of = jnp.broadcast_to(live_blocks[:, None], (BLK_DEV, BLOCK)).reshape(slot_total)
    offset = slot_index % BLOCK
    position = (slot_index - seq_of * BLOCK).astype(jnp.float32)
    alive_slot = offset < live_of
    allowed = (
        (seq_of[:, None] == seq_of[None, :])
        & (slot_index[None, :] <= slot_index[:, None])
        & (alive_slot[None, :] | (slot_index[None, :] == slot_index[:, None]))
    )
    return (position, alive_slot, allowed)


def rotary_tables(position):
    frequency = 10000.0 ** (-(2.0 * jnp.arange(ROT // 2, dtype=jnp.float32)) / ROT)
    angles = position[:, None] * frequency[None, :]
    cosine_table = jnp.concatenate([jnp.cos(angles), jnp.cos(angles)], axis=1)
    sine_table = jnp.concatenate([jnp.sin(angles), jnp.sin(angles)], axis=1)
    return (cosine_table, sine_table)


def apply_rotary(values, cosine_table, sine_table):
    rot_part = values[..., :ROT]
    turned = jnp.concatenate([-rot_part[..., ROT // 2 :], rot_part[..., : ROT // 2]], axis=-1)
    rotated = rot_part * cosine_table[:, None, :] + turned * sine_table[:, None, :]
    return jnp.concatenate([rotated, values[..., ROT:]], axis=-1)


def adamw_update(weight, grad, first_m, second_m, rate_value, decay_value):
    first_new = beta_one * first_m + (1.0 - beta_one) * grad
    second_new = beta_two * second_m + (1.0 - beta_two) * grad * grad
    fix_one = 1.0 - beta_one**STEP
    fix_two = 1.0 - beta_two**STEP
    direction = first_new / fix_one / (jnp.sqrt(second_new / fix_two) + eps_adam)
    return (weight - rate_value * (direction + decay_value * weight), first_new, second_new)


def masked_scores(queries, keys_rot, allowed):
    scores = jnp.einsum(
        "qhd,khd->hqk", queries, keys_rot, preferred_element_type=jnp.float32
    ) * HEAD ** (-0.5)
    return jnp.where(allowed[None], scores, masked_score)


def term_rows(pairs, width, vector_all, piece_len, share_rows, stride, row_count):
    blocks = row_count // stride
    products = []
    for left, right in pairs:
        products.append(
            lax.dot_general(left, right, contract_rows, preferred_element_type=jnp.float32)
        )
    product_rows = jnp.concatenate(products, axis=1).reshape(blocks, share_rows, width)
    vector_row = vector_all.reshape(blocks, 1, piece_len)
    vector_row = jnp.pad(vector_row, ((0, 0), (0, 0), (0, width - piece_len)))
    return jnp.concatenate([product_rows, vector_row], axis=1).reshape(row_count, width)


def body(
    tokens,
    cotangent,
    block_first,
    block_live,
    w_qkv,
    w_attn_out,
    w_mlp_in,
    w_mlp_out,
    vectors,
    first_qkv,
    second_qkv,
    first_attn_out,
    second_attn_out,
    first_mlp_in,
    second_mlp_in,
    first_mlp_out,
    second_mlp_out,
    first_vectors,
    second_vectors,
):
    device_count = lax.axis_size("fsdp")
    slot_total = tokens.shape[0]
    share_rows = D // device_count
    rows_dev = share_rows + 1
    piece_len = VEC // device_count
    bf16 = jnp.bfloat16
    f32 = jnp.float32
    attn_set = (
        lax.all_gather(w_qkv.astype(bf16), "fsdp", axis=0, tiled=True),
        lax.all_gather(w_attn_out.astype(bf16), "fsdp", axis=0, tiled=True),
        lax.all_gather(vectors.astype(bf16), "fsdp", axis=0, tiled=True),
    )
    mlp_set = (
        lax.all_gather(w_mlp_in.astype(bf16), "fsdp", axis=0, tiled=True),
        lax.all_gather(w_mlp_out.astype(bf16), "fsdp", axis=0, tiled=True),
    )
    wq_full, wo_full, vec_full = attn_set
    wi_full, wm_full = mlp_set
    inputs = tokens.astype(f32)
    position, alive_slot, allowed = slot_tables(block_first, block_live, slot_total)
    cosine_table, sine_table = rotary_tables(position)
    b_qkv, b_att, b_in, b_mlp, gain_one, shift_one, gain_two, shift_two = split_vectors(
        vec_full.astype(f32)
    )
    attn_norm, norm_one_back = jax.vjp(layer_norm, inputs, gain_one, shift_one)
    attn_in = attn_norm.astype(bf16)
    mixed_qkv = jnp.dot(attn_in, wq_full, preferred_element_type=f32) + b_qkv
    mixed_qkv = mixed_qkv.reshape(slot_total, 3, HEADS, HEAD)
    queries = apply_rotary(mixed_qkv[:, 0], cosine_table, sine_table).astype(bf16)
    keys_rot = apply_rotary(mixed_qkv[:, 1], cosine_table, sine_table).astype(bf16)
    values = mixed_qkv[:, 2].astype(bf16)
    scores = masked_scores(queries, keys_rot, allowed)
    row_max = jnp.max(scores, axis=-1, keepdims=True)
    raised = jnp.exp(scores - row_max)
    row_total = jnp.sum(raised, axis=-1, keepdims=True)
    log_total = row_max + jnp.log(row_total)
    weights_low = (raised / row_total).astype(bf16)
    attended = (
        jnp.einsum("hqk,khd->qhd", weights_low, values, preferred_element_type=f32)
        .reshape(slot_total, D)
        .astype(bf16)
    )
    attn_branch = (
        lax.dot_general(attended, wo_full, contract_cols, preferred_element_type=f32) + b_att
    )
    mlp_norm, norm_two_back = jax.vjp(layer_norm, inputs, gain_two, shift_two)
    mlp_in = mlp_norm.astype(bf16)
    hidden = jnp.dot(mlp_in, wi_full, preferred_element_type=f32) + b_in
    activated_f, gelu_back = jax.vjp(gelu_exact, hidden)
    activated = activated_f.astype(bf16)
    mlp_branch = (
        lax.dot_general(activated, wm_full, contract_cols, preferred_element_type=f32) + b_mlp
    )
    out = (inputs + attn_branch + mlp_branch).astype(bf16)
    again_attn = (
        lax.all_gather(w_qkv.astype(bf16), "fsdp", axis=0, tiled=True),
        lax.all_gather(w_attn_out.astype(bf16), "fsdp", axis=0, tiled=True),
        lax.all_gather(vectors.astype(bf16), "fsdp", axis=0, tiled=True),
    )
    again_mlp = (
        lax.all_gather(w_mlp_in.astype(bf16), "fsdp", axis=0, tiled=True),
        lax.all_gather(w_mlp_out.astype(bf16), "fsdp", axis=0, tiled=True),
    )
    wq_back, wo_back = (again_attn[0], again_attn[1])
    wi_back, wm_back = again_mlp
    grad_seed = jnp.where(alive_slot[:, None], cotangent, jnp.zeros_like(cotangent))
    seed_f = grad_seed.astype(f32)
    d_act = jnp.dot(grad_seed, wm_back, preferred_element_type=f32)
    d_hidden = gelu_back(d_act)[0].astype(bf16)
    d_mlp_in = lax.dot_general(d_hidden, wi_back, contract_cols, preferred_element_type=f32)
    mlp_pairs = [(mlp_in, d_hidden), (grad_seed, activated)]
    d_attended = (
        jnp.dot(grad_seed, wo_back, preferred_element_type=f32)
        .astype(bf16)
        .reshape(slot_total, HEADS, HEAD)
    )
    scores_again = masked_scores(queries, keys_rot, allowed)
    weights_soft = jnp.exp(scores_again - log_total)
    d_weights = jnp.einsum("qhd,khd->hqk", d_attended, values, preferred_element_type=f32)
    row_inner = jnp.sum(weights_soft * d_weights, axis=-1, keepdims=True)
    d_scores = (weights_soft * (d_weights - row_inner)).astype(bf16)
    d_queries = jnp.einsum(
        "hqk,khd->qhd", d_scores, keys_rot, preferred_element_type=f32
    ) * HEAD ** (-0.5)
    d_keys = jnp.einsum("hqk,qhd->khd", d_scores, queries, preferred_element_type=f32) * HEAD ** (
        -0.5
    )
    d_values = jnp.einsum("hqk,qhd->khd", weights_low, d_attended, preferred_element_type=f32)
    d_mixed = jnp.stack(
        [
            apply_rotary(d_queries, cosine_table, -sine_table),
            apply_rotary(d_keys, cosine_table, -sine_table),
            d_values,
        ],
        axis=1,
    )
    d_mixed = d_mixed.reshape(slot_total, 3 * D).astype(bf16)
    d_attn_in = lax.dot_general(d_mixed, wq_back, contract_cols, preferred_element_type=f32)
    d_in_one, d_gain_one, d_shift_one = norm_one_back(d_attn_in)
    d_in_two, d_gain_two, d_shift_two = norm_two_back(d_mlp_in)
    grad_tokens = (seed_f + d_in_one + d_in_two).astype(bf16)
    seed_sum = jnp.sum(seed_f, axis=0)
    mixed_sum = jnp.sum(d_mixed.astype(f32), axis=0)
    local_vec = jnp.concatenate(
        [
            mixed_sum[:D],
            mixed_sum[2 * D :],
            seed_sum,
            jnp.sum(d_hidden.astype(f32), axis=0),
            seed_sum,
            d_gain_one,
            d_shift_one,
            d_gain_two,
            d_shift_two,
        ]
    )
    attn_pairs = [(attn_in, d_mixed), (grad_seed, attended)]
    summed = lax.psum_scatter(
        term_rows(
            attn_pairs + mlp_pairs,
            COLS,
            local_vec,
            piece_len,
            share_rows,
            rows_dev,
            rows_dev * lax.axis_size("fsdp"),
        ),
        "fsdp",
        scatter_dimension=0,
        tiled=True,
    )
    grad_qkv = summed[:share_rows, : 3 * D]
    grad_attn_out = summed[:share_rows, 3 * D : 4 * D]
    grad_mlp_in = summed[:share_rows, 4 * D : 4 * D + FF]
    grad_mlp_out = summed[:share_rows, 4 * D + FF :]
    grad_vectors = summed[share_rows, :piece_len]
    new_qkv, m_qkv, u_qkv = adamw_update(
        w_qkv, grad_qkv, first_qkv, second_qkv, learn_rate, decay_matrix
    )
    new_att, m_att, u_att = adamw_update(
        w_attn_out, grad_attn_out, first_attn_out, second_attn_out, learn_rate, decay_matrix
    )
    new_in, m_in, u_in = adamw_update(
        w_mlp_in, grad_mlp_in, first_mlp_in, second_mlp_in, learn_rate, decay_matrix
    )
    new_out, m_out, u_out = adamw_update(
        w_mlp_out, grad_mlp_out, first_mlp_out, second_mlp_out, learn_rate, decay_matrix
    )
    new_vec, m_vec, u_vec = adamw_update(
        vectors, grad_vectors, first_vectors, second_vectors, vector_rate, 0.0
    )
    return (
        out,
        grad_tokens,
        grad_qkv,
        grad_attn_out,
        grad_mlp_in,
        grad_mlp_out,
        grad_vectors,
        new_qkv,
        new_att,
        new_in,
        new_out,
        new_vec,
        m_qkv,
        u_qkv,
        m_att,
        u_att,
        m_in,
        u_in,
        m_out,
        u_out,
        m_vec,
        u_vec,
    )


def solution(mesh):
    in_specs = (
        P("fsdp", None),
        P("fsdp", None),
        P("fsdp"),
        P("fsdp"),
        P("fsdp", None),
        P("fsdp", None),
        P("fsdp", None),
        P("fsdp", None),
        P("fsdp"),
        P("fsdp", None),
        P("fsdp", None),
        P("fsdp", None),
        P("fsdp", None),
        P("fsdp", None),
        P("fsdp", None),
        P("fsdp", None),
        P("fsdp", None),
        P("fsdp"),
        P("fsdp"),
    )
    out_specs = (
        P("fsdp", None),
        P("fsdp", None),
        P("fsdp", None),
        P("fsdp", None),
        P("fsdp", None),
        P("fsdp", None),
        P("fsdp"),
        P("fsdp", None),
        P("fsdp", None),
        P("fsdp", None),
        P("fsdp", None),
        P("fsdp"),
        P("fsdp", None),
        P("fsdp", None),
        P("fsdp", None),
        P("fsdp", None),
        P("fsdp", None),
        P("fsdp", None),
        P("fsdp", None),
        P("fsdp", None),
        P("fsdp"),
        P("fsdp"),
    )
    return jax.shard_map(body, mesh=mesh, in_specs=in_specs, out_specs=out_specs, check_vma=False)
```

profile of v0, /device:TPU:0, one launch (start us, length us, event | category | flops | bytes accessed | tf_op | source)
XLA Modules:
  0.0 4060.4 jit_solution(5006070805215017253)
XLA Ops:
  7.2 1.9 convert_element_type.104
  9.2 2.4 convert_element_type.97
  11.7 1.1 convert_element_type.106
  12.9 2.7 convert_element_type.108
  15.7 44.2 %all-gather = bf16[32,1,768]{2,1,0:T(2,128)(2,1)S(1)} all-gather(bf16[1,1,768]{2,1,0:T(2,128)(2,1)S(1)} %reshape.292), channel_id=1, replica_groups=mesh['fsdp'=32] {'fsdp'}, dimensions={0}, use_global_device_ids=true | all-gather | bytes 50688 | tf_op jit(solution)/shard_map/all_gather | solution.py:140
  64.1 0.8 fusion.46
  64.8 26.9 all-gather.8.cloned.1.call-done
  91.8 5.8 convolution_convert_fusion
  97.7 1.3 copy.104
  99.0 149.5 %all-gather.6.cloned.1.call-done = bf16[2048,6144]{1,0:T(8,128)(2,1)} async-done(((bf16[64,6144]{1,0:T(8,128)(2,1)}), bf16[2048,6144]{1,0:T(8,128)(2,1)}) %all-gather.6.cloned.1.call-update) | async-done | bytes 25165840 | tf_op jit(solution)/shard_map/all_gather | solution.py:138
  248.5 11.8 convolution_add_fusion.1
  260.3 2.6 copy.106
  262.9 2.6 copy-done.2
  265.6 1.7 copy.105
  267.3 2.5 fusion.74
  269.9 1.2 copy_bitcast_fusion
  272.6 0.7 fusion.38
  273.4 1.2 fusion.76
  275.0 0.9 copy-done.12
  276.2 0.7 multiply_reduce_fusion
  278.4 0.9 multiply_bitcast_fusion.1
  280.3 0.7 fusion.34
  282.7 2.3 convert_reduce_fusion.1
  285.0 4.6 copy.89
  290.8 2.0 convolution_convert_fusion.1
  292.9 8.3 fusion.64
  301.2 21.7 fusion.58
  322.9 122.0 %all-gather.10.cloned.1.call-done = bf16[2048,8192]{1,0:T(8,128)(2,1)} async-done(((bf16[64,8192]{1,0:T(8,128)(2,1)}), bf16[2048,8192]{1,0:T(8,128)(2,1)}) %all-gather.10.cloned.1.call-update) | async-done | bytes 33554448 | tf_op jit(solution)/shard_map/all_gather | solution.py:143
  444.9 33.3 multiply_convert_fusion
  478.2 163.0 %all-gather.12.cloned.1.call-done = bf16[2048,8192]{1,0:T(8,128)(2,1)} async-done(((bf16[64,8192]{1,0:T(8,128)(2,1)}), bf16[2048,8192]{1,0:T(8,128)(2,1)}) %all-gather.12.cloned.1.call-update) | async-done | bytes 33554448 | tf_op jit(solution)/shard_map/all_gather | solution.py:144
  641.2 26.5 convert_reduce_fusion
  667.7 25.6 fusion.55
  693.3 16.9 fusion.77
  710.2 14.3 fusion.67
  724.5 4.0 fusion.25
  728.6 2.9 convert_reduce_fusion.3
  731.5 25.6 fusion.63
  757.2 130.5 %pad_maximum_fusion = f32[2048,24576]{1,0:T(8,128)} fusion(f32[2048,8192]{1,0:T(8,128)} %fusion.63, f32[2048,8192]{1,0:T(8,128)} %fusion.55, f32[2048,2048]{1,0:T(8,128)} %fusion.64, f32[2048,6144]{1,0:T(8,128)} %fusion.58), kind=kLoop, calls=%fused_computation.2 | loop fusion | flops 150994944 | bytes 402653184 | tf_op jit(solution)/shard_map/concatenate | solution.py:103
  887.7 140.7 %select_maximum_fusion = f32[32,65,24576]{2,1,0:T(8,128)} fusion(f32[32,1,768]{2,1,0:T(1,128)S(1)} %bitcast.76, f32[32,64,24576]{2,1,0:T(8,128)} %bitcast.16), kind=kLoop, calls=%fused_computation | loop fusion | flops 153354240 | bytes 405897216 | tf_op jit(solution)/shard_map/concatenate | solution.py:106
  1028.4 180.0 %reshape.291 = f32[2080,24576]{1,0:T(8,128)} reshape(f32[32,65,24576]{2,1,0:T(8,128)} %select_maximum_fusion) | data formatting | bytes 408944640 | tf_op jit(solution)/shard_map/reshape | solution.py:106
  1208.5 1.2 copy-done.1
  1210.0 8.2 convert_add_fusion
  1218.2 18.8 fusion.17
  1237.0 2796.8 %all-reduce.4.cloned.1.call-done = f32[2080,24576]{1,0:T(8,128)} async-done(((f32[2080,24576]{1,0:T(8,128)}), f32[2080,24576]{1,0:T(8,128)}) %all-reduce.4.cloned.1.call-update) | async-done | bytes 204472336
  4033.7 0.8 dynamic-slice_reduce_fusion
  4035.2 5.7 multiply_subtract_fusion.2
  4041.0 3.2 multiply_subtract_fusion.3
  4044.2 9.2 multiply_subtract_fusion
  (155 shorter events, 13.3 us)
Async XLA Ops:
  7.2 4.5 copy-start.8
  7.2 84.6 %all-gather.8.cloned.1.call-start = ((), (), s32[]{:S(2)}) async-start(), calls=%async_computation.1 | async-start | bytes 8650752 | tf_op jit(solution)/shard_map/all_gather | solution.py:139
  9.2 239.3 %all-gather.6.cloned.1.call-start = ((), (), s32[]{:S(2)}) async-start(), calls=%async_computation | async-start | bytes 25952256 | tf_op jit(solution)/shard_map/all_gather | solution.py:138
  11.6 433.3 %all-gather.10.cloned.1.call-start = ((), (), s32[]{:S(2)}) async-start(), calls=%async_computation.2 | async-start | bytes 34603008 | tf_op jit(solution)/shard_map/all_gather | solution.py:143
  12.8 2.9 copy-start.38
  12.8 49.1 %copy-start.48 = (s32[2]{0:T(128)S(1)}, s32[2]{0:T(128)}, u32[]{:S(2)}) copy-start(s32[2]{0:T(128)} %param.21) | copy-start | bytes 28
  12.8 49.9 %copy-start = (bf16[256,2048]{1,0:T(8,128)(2,1)S(1)}, bf16[256,2048]{1,0:T(8,128)(2,1)}, u32[]{:S(2)}) copy-start(bf16[256,2048]{1,0:T(8,128)(2,1)} %param.19) | copy-start | bytes 3145732
  12.8 628.4 %all-gather.12.cloned.1.call-start = ((), (), s32[]{:S(2)}) async-start(), calls=%async_computation.3 | async-start | bytes 34603008 | tf_op jit(solution)/shard_map/all_gather | solution.py:144
  15.6 47.7 %copy-start.47 = (s32[2]{0:T(128)S(1)}, s32[2]{0:T(128)}, u32[]{:S(2)}) copy-start(s32[2]{0:T(128)} %param.22) | copy-start | bytes 28
  15.6 76.1 %copy-start.3 = (bf16[256,2048]{1,0:T(8,128)(2,1)S(1)}, bf16[256,2048]{1,0:T(8,128)(2,1)}, u32[]{:S(2)}) copy-start(bf16[256,2048]{1,0:T(8,128)(2,1)} %param.20) | copy-start | bytes 3145732
  15.7 4018.1 %all-reduce.4.cloned.1.call-start = ((), (), s32[]{:S(2)}) async-start(), calls=%async_computation.4 | async-start | bytes 408944640
  62.9 1.9 copy-start.27
  97.6 150.9 %copy-start.25 = (f32[2048]{0:T(1024)S(1)}, f32[2048]{0:T(1024)}, u32[]{:S(2)}) copy-start(f32[2048]{0:T(1024)} %get-tuple-element.87) | copy-start | bytes 24580
  97.6 150.9 %copy-start.28 = (f32[256]{0:T(256)S(1)}, f32[256]{0:T(256)}, u32[]{:S(2)}) copy-start(f32[256]{0:T(256)} %copy-done.27) | copy-start | bytes 3076
  97.6 150.9 %copy-start.30 = (f32[256]{0:T(256)S(1)}, f32[256]{0:T(256)}, u32[]{:S(2)}) copy-start(f32[256]{0:T(256)} %fusion.50) | copy-start | bytes 3076
  97.6 150.8 %copy-start.37 = (f32[6144]{0:T(1024)S(1)}, f32[6144]{0:T(1024)}, u32[]{:S(2)}) copy-start(f32[6144]{0:T(1024)} %pad_maximum_fusion.9) | copy-start | bytes 73732
  262.9 2.6 copy-start.2
  274.6 1.5 copy-start.13
  290.8 2.0 copy-start.4
  290.8 2.0 copy-start.35
  292.8 8.3 copy-start.20
  292.9 8.3 copy-start.26
  292.9 8.3 copy-start.29
  292.9 8.3 copy-start.31
  301.2 143.7 %copy-start.24 = (f32[2048]{0:T(1024)S(1)}, f32[2048]{0:T(1024)}, u32[]{:S(2)}) copy-start(f32[2048]{0:T(1024)} %get-tuple-element.82) | copy-start | bytes 24580
  301.2 143.7 %copy-start.36 = (f32[8192]{0:T(1024)S(1)}, f32[8192]{0:T(1024)}, u32[]{:S(2)}) copy-start(f32[8192]{0:T(1024)} %split.43) | copy-start | bytes 98308
  444.9 196.3 %copy-start.5 = (bf16[256,2048]{1,0:T(8,128)(2,1)S(1)}, bf16[256,2048]{1,0:T(8,128)(2,1)}, u32[]{:S(2)}) copy-start(bf16[256,2048]{1,0:T(8,128)(2,1)} %param.20) | copy-start | bytes 3145732
  710.2 14.3 copy-start.42
  724.5 4.1 copy-start.6
  724.5 4.1 copy-start.7
  728.6 3.0 copy-start.32
  1208.4 1.5 copy-start.21
  1210.0 8.2 copy-start.43
  1218.2 2816.3 %copy-start.39 = (f32[768]{0:T(1024)S(1)}, f32[768]{0:T(1024)}, u32[]{:S(2)}) copy-start(f32[768]{0:T(1024)} %param.27) | copy-start | bytes 9220
  1218.2 2816.3 %copy-start.45 = (f32[768]{0:T(1024)S(1)}, f32[768]{0:T(1024)}, u32[]{:S(2)}) copy-start(f32[768]{0:T(1024)} %param.36) | copy-start | bytes 9220
  1218.2 2816.4 %copy-start.46 = (f32[768]{0:T(1024)S(1)}, f32[768]{0:T(1024)}, u32[]{:S(2)}) copy-start(f32[768]{0:T(1024)} %param.37) | copy-start | bytes 9220
  1218.2 2817.0 %copy-start.11 = (f32[64,6144]{1,0:T(8,128)S(1)}, f32[64,6144]{1,0:T(8,128)}, u32[]{:S(2)}) copy-start(f32[64,6144]{1,0:T(8,128)} %param.23) | copy-start | bytes 4718596
  1218.2 2817.0 %copy-start.19 = (f32[64,6144]{1,0:T(8,128)S(1)}, f32[64,6144]{1,0:T(8,128)}, u32[]{:S(2)}) copy-start(f32[64,6144]{1,0:T(8,128)} %param.28) | copy-start | bytes 4718596
  4034.5 6.4 copy-start.40
  4035.2 5.8 copy-start.14
  4035.2 5.8 copy-start.22
  4035.2 5.8 copy-start.23
  4035.2 9.0 copy-start.15
  4035.2 9.0 copy-start.16
  4035.2 9.0 copy-start.17
  4035.2 9.0 copy-start.18
  4041.0 3.2 copy-start.9
  4041.0 3.2 copy-start.10
  (6 other events, 7.7 us)
Sparse Core Ops, SparseCore 0:
  11.5 80.2 all-gather.7
  95.2 153.2 all-gather.5
  251.9 192.9 all-gather.9
  448.2 192.9 all-gather.11
  1208.6 2825.1 all-reduce.3
where the time goes:
time: 4070 us; the launch traced here: 4060 us
  waiting for transfers between devices  3260 us (80%)
  other arithmetic  316 us (8%)
  matrix products  223 us (5%)
  local copies, waits for them, and re-layouts  205 us (5%)
  blocking collectives  44.2 us (1%)
    unnamed x6, waiting for transfers between devices  2800 us
    reshape x1, local copies, waits for them, and re-layouts, term_rows(): jnp.concatenate([product_rows, vector_row], axis=1)  180 us
    all_gather x1, waiting for transfers between devices, body(): lax.all_gather(w_mlp_out.astype(bf16), 'fsdp', axis=0, tiled=True)  163 us
    all_gather x1, waiting for transfers between devices, body(): lax.all_gather(w_qkv.astype(bf16), 'fsdp', axis=0, tiled=True)  150 us
    concatenate x1, other arithmetic, term_rows(): jnp.concatenate([product_rows, vector_row], axis=1)  141 us
    concatenate x1, other arithmetic, term_rows(): jnp.concatenate(products, axis=1).reshape(blocks, share_rows, width)  131 us
    all_gather x1, waiting for transfers between devices, body(): lax.all_gather(w_mlp_in.astype(bf16), 'fsdp', axis=0, tiled=True)  122 us
  transfers between devices with their start and end apart: 5, of which 5 were waited for; matrix products, arithmetic and copies ran while one was open for 4% of the time, Pallas kernels for 0%

commit v1 on v0

v1 whole, which is shorter than its diff:
```python
import jax
import jax.numpy as jnp
from jax import lax
from jax.sharding import Mesh, PartitionSpec as P

D = 2048
HEADS = 8
HEAD = 256
FF = 8192
ROT = 64
BLOCK = 128
BLK_DEV = 2
STEP = 3
VEC = 24576
TEAM = 8
SLICE_FF = FF // TEAM

eps_norm = 1e-05
beta_one = 0.9
beta_two = 0.95
learn_rate = 0.03
vector_rate = 0.3
decay_matrix = 0.1
eps_adam = 1e-08
masked_score = -1e30
contract_rows = (((0,), (0,)), ((), ()))
contract_cols = (((1,), (1,)), ((), ()))
bf16 = jnp.bfloat16
f32 = jnp.float32
PLANE = ("row", "col", "core")
EVERY = ("far", "row", "col", "core")


def dot(left, right, dims=(((1,), (0,)), ((), ()))):
    return lax.dot_general(left, right, dims, preferred_element_type=f32)


def split_vectors(vec_all):
    boundaries = [D, 2 * D, 3 * D, 3 * D + FF, 4 * D + FF, 5 * D + FF, 6 * D + FF, 7 * D + FF]
    return jnp.split(vec_all, boundaries)


def slot_tables(first_blocks, live_blocks, slot_total):
    slot_index = jnp.arange(slot_total, dtype=jnp.int32)
    seq_of = jnp.repeat(first_blocks, BLOCK, axis=-1)
    live_of = jnp.repeat(live_blocks, BLOCK, axis=-1)
    offset = slot_index % BLOCK
    position = (slot_index - seq_of * BLOCK).astype(f32)
    alive_slot = offset < live_of
    same = seq_of[..., :, None] == seq_of[..., None, :]
    causal = slot_index[None, :] <= slot_index[:, None]
    itself = slot_index[None, :] == slot_index[:, None]
    allowed = same & causal & (alive_slot[..., None, :] | itself)
    return (position, alive_slot, allowed)


def rotary_tables(position):
    frequency = 10000.0 ** (-(2.0 * jnp.arange(ROT // 2, dtype=f32)) / ROT)
    angles = position[:, None] * frequency[None, :]
    cosine_table = jnp.concatenate([jnp.cos(angles), jnp.cos(angles)], axis=1)
    sine_table = jnp.concatenate([jnp.sin(angles), jnp.sin(angles)], axis=1)
    return (cosine_table, sine_table)


def apply_rotary(values, cosine_table, sine_table):
    rot_part = values[..., :ROT]
    turned = jnp.concatenate([-rot_part[..., ROT // 2 :], rot_part[..., : ROT // 2]], axis=-1)
    rotated = rot_part * cosine_table + turned * sine_table
    return jnp.concatenate([rotated, values[..., ROT:]], axis=-1)


def adamw_update(weight, grad, first_m, second_m, rate_value, decay_value):
    first_new = beta_one * first_m + (1.0 - beta_one) * grad
    second_new = beta_two * second_m + (1.0 - beta_two) * grad * grad
    fix_one = 1.0 - beta_one**STEP
    fix_two = 1.0 - beta_two**STEP
    direction = first_new / fix_one / (jnp.sqrt(second_new / fix_two) + eps_adam)
    return (weight - rate_value * (direction + decay_value * weight), first_new, second_new)


def normalize(values):
    centred = values - jnp.mean(values, axis=-1, keepdims=True)
    spread = jnp.mean(centred * centred, axis=-1, keepdims=True)
    scale = lax.rsqrt(spread + eps_norm)
    return centred * scale, scale


def body(
    tokens,
    cotangent,
    block_first,
    block_live,
    w_qkv,
    w_attn_out,
    w_mlp_in,
    w_mlp_out,
    vectors,
    first_qkv,
    second_qkv,
    first_attn_out,
    second_attn_out,
    first_mlp_in,
    second_mlp_in,
    first_mlp_out,
    second_mlp_out,
    first_vectors,
    second_vectors,
):
    groups = lax.axis_size("far")
    slot_total = tokens.shape[0]
    rows_dev = w_qkv.shape[0]
    rows_group = rows_dev * TEAM
    team_slots = slot_total * TEAM
    me = lax.axis_index(PLANE)

    attn_send = jnp.concatenate(
        [
            w_qkv.astype(bf16).reshape(rows_dev, 3, TEAM, HEAD).transpose(2, 0, 1, 3).reshape(TEAM, rows_dev, 3 * HEAD),
            w_attn_out.astype(bf16).reshape(rows_dev, TEAM, HEAD).transpose(1, 0, 2),
        ],
        axis=2,
    )
    mlp_send = jnp.concatenate(
        [
            w_mlp_in.astype(bf16).reshape(rows_dev, TEAM, SLICE_FF).transpose(1, 0, 2),
            w_mlp_out.astype(bf16).reshape(rows_dev, TEAM, SLICE_FF).transpose(1, 0, 2),
        ],
        axis=2,
    )

    def fetch(block):
        got = lax.all_to_all(block, PLANE, 0, 0, tiled=True)
        return lax.all_gather(got.reshape(rows_group, block.shape[2]), "far", axis=0, tiled=True)

    attn_w = fetch(attn_send)
    mlp_w = fetch(mlp_send)
    wq, wo = attn_w[:, : 3 * HEAD], attn_w[:, 3 * HEAD :]
    wi, wm = mlp_w[:, :SLICE_FF], mlp_w[:, SLICE_FF:]
    vec_full = lax.all_gather(vectors.astype(bf16), EVERY, axis=0, tiled=True).astype(f32)
    b_query, b_value, b_att, b_in, b_mlp, gain_one, shift_one, gain_two, shift_two = split_vectors(vec_full)

    alive_own = jnp.repeat(
        jnp.arange(BLOCK, dtype=jnp.int32)[None, :] < block_live[:, None], 1, axis=0
    ).reshape(slot_total)
    seed_own = jnp.where(alive_own[:, None], cotangent, jnp.zeros_like(cotangent))
    x_team = lax.all_gather(tokens, PLANE, axis=0, tiled=True)
    seed = lax.all_gather(seed_own, PLANE, axis=0, tiled=True)
    blocks = lax.all_gather(jnp.stack([block_first, block_live]), PLANE, axis=0, tiled=False)
    position, alive_slot, allowed = slot_tables(blocks[:, 0], blocks[:, 1], slot_total)
    cosine_table, sine_table = rotary_tables(position.reshape(team_slots))

    xhat, _ = normalize(x_team.astype(f32))
    attn_in = (xhat * gain_one + shift_one).astype(bf16)
    mlp_in = (xhat * gain_two + shift_two).astype(bf16)

    bias_q = lax.dynamic_slice(b_query, (me * HEAD,), (HEAD,))
    bias_v = lax.dynamic_slice(b_value, (me * HEAD,), (HEAD,))
    mixed = dot(attn_in, wq)
    shape = (TEAM, slot_total, HEAD)
    queries = apply_rotary(mixed[:, :HEAD] + bias_q, cosine_table, sine_table).astype(bf16).reshape(shape)
    keys_rot = apply_rotary(mixed[:, HEAD : 2 * HEAD], cosine_table, sine_table).astype(bf16).reshape(shape)
    values = (mixed[:, 2 * HEAD :] + bias_v).astype(bf16).reshape(shape)
    scores = jnp.einsum("bqd,bkd->bqk", queries, keys_rot, preferred_element_type=f32) * HEAD ** (-0.5)
    scores = jnp.where(allowed, scores, masked_score)
    raised = jnp.exp(scores - jnp.max(scores, axis=-1, keepdims=True))
    weights_soft = raised / jnp.sum(raised, axis=-1, keepdims=True)
    weights_low = weights_soft.astype(bf16)
    attended = (
        jnp.einsum("bqk,bkd->bqd", weights_low, values, preferred_element_type=f32).astype(bf16).reshape(team_slots, HEAD)
    )
    bias_in = lax.dynamic_slice(b_in, (me * SLICE_FF,), (SLICE_FF,))
    hidden = dot(mlp_in, wi) + bias_in
    activated_f, gelu_back = jax.vjp(lambda v: jax.nn.gelu(v, approximate=False), hidden)
    activated = activated_f.astype(bf16)
    part_out = dot(attended, wo, contract_cols) + dot(activated, wm, contract_cols)
    branch = lax.psum_scatter(part_out.astype(bf16), PLANE, scatter_dimension=0, tiled=True)
    inputs = tokens.astype(f32)
    out = (inputs + branch.astype(f32) + (b_att + b_mlp)).astype(bf16)

    d_hidden = gelu_back(dot(seed, wm))[0].astype(bf16)
    d_attended = dot(seed, wo).astype(bf16).reshape(shape)
    d_weights = jnp.einsum("bqd,bkd->bqk", d_attended, values, preferred_element_type=f32)
    row_inner = jnp.sum(weights_soft * d_weights, axis=-1, keepdims=True)
    d_scores = (weights_soft * (d_weights - row_inner)).astype(bf16)
    d_queries = jnp.einsum("bqk,bkd->bqd", d_scores, keys_rot, preferred_element_type=f32) * HEAD ** (-0.5)
    d_keys = jnp.einsum("bqk,bqd->bkd", d_scores, queries, preferred_element_type=f32) * HEAD ** (-0.5)
    d_values = jnp.einsum("bqk,bqd->bkd", weights_low, d_attended, preferred_element_type=f32)
    d_mixed = jnp.concatenate(
        [
            apply_rotary(d_queries.reshape(team_slots, HEAD), cosine_table, -sine_table),
            apply_rotary(d_keys.reshape(team_slots, HEAD), cosine_table, -sine_table),
            d_values.reshape(team_slots, HEAD),
        ],
        axis=1,
    ).astype(bf16)
    d_attn_in = dot(d_mixed, wq, contract_cols)
    d_mlp_in = dot(d_hidden, wi, contract_cols)
    d_gain_one = jnp.sum(d_attn_in * xhat, axis=0)
    d_shift_one = jnp.sum(d_attn_in, axis=0)
    d_gain_two = jnp.sum(d_mlp_in * xhat, axis=0)
    d_shift_two = jnp.sum(d_mlp_in, axis=0)
    part_back = d_attn_in * gain_one + d_mlp_in * gain_two
    back = lax.psum_scatter(part_back.astype(bf16), PLANE, scatter_dimension=0, tiled=True).astype(f32)
    own_hat, own_scale = normalize(inputs)
    seed_f = seed_own.astype(f32)
    d_inputs = own_scale * (
        back
        - jnp.mean(back, axis=-1, keepdims=True)
        - own_hat * jnp.mean(back * own_hat, axis=-1, keepdims=True)
    )
    grad_tokens = (seed_f + d_inputs).astype(bf16)

    attn_term = jnp.concatenate(
        [dot(attn_in, d_mixed, contract_rows), dot(seed, attended, contract_rows)], axis=1
    ).astype(bf16)
    mlp_term = jnp.concatenate(
        [dot(mlp_in, d_hidden, contract_rows), dot(seed, activated, contract_rows)], axis=1
    ).astype(bf16)

    def deliver(term):
        width = term.shape[1]
        mine = lax.psum_scatter(term, "far", scatter_dimension=0, tiled=True)
        return lax.all_to_all(mine.reshape(TEAM, rows_dev, width), PLANE, 0, 0, tiled=True)

    attn_got = deliver(attn_term).astype(f32)
    mlp_got = deliver(mlp_term).astype(f32)
    grad_qkv = (
        attn_got[:, :, : 3 * HEAD].reshape(TEAM, rows_dev, 3, HEAD).transpose(1, 2, 0, 3).reshape(rows_dev, 3 * D)
    )
    grad_attn_out = attn_got[:, :, 3 * HEAD :].transpose(1, 0, 2).reshape(rows_dev, D)
    grad_mlp_in = mlp_got[:, :, :SLICE_FF].transpose(1, 0, 2).reshape(rows_dev, FF)
    grad_mlp_out = mlp_got[:, :, SLICE_FF:].transpose(1, 0, 2).reshape(rows_dev, FF)

    seed_sum = jnp.sum(seed_f, axis=0)
    mixed_sum = jnp.sum(d_mixed.astype(f32), axis=0)
    hidden_sum = jnp.sum(d_hidden.astype(f32), axis=0)

    def place(part, width):
        return lax.dynamic_update_slice(jnp.zeros((width,), f32), part, (me * part.shape[0],))

    local_vec = jnp.concatenate(
        [
            place(mixed_sum[:HEAD], D),
            place(mixed_sum[2 * HEAD :], D),
            seed_sum,
            place(hidden_sum, FF),
            seed_sum,
            d_gain_one,
            d_shift_one,
            d_gain_two,
            d_shift_two,
        ]
    )
    piece = vectors.shape[0]
    vec_terms = local_vec.reshape(groups, TEAM, piece).transpose(1, 0, 2)
    vec_plane = jnp.sum(lax.all_to_all(vec_terms, PLANE, 0, 0, tiled=True), axis=0)
    vec_line = lax.all_to_all(vec_plane, "far", 0, 0, tiled=True)
    grad_vectors = jnp.sum(vec_line, axis=0)

    new_qkv, m_qkv, u_qkv = adamw_update(w_qkv, grad_qkv, first_qkv, second_qkv, learn_rate, decay_matrix)
    new_att, m_att, u_att = adamw_update(
        w_attn_out, grad_attn_out, first_attn_out, second_attn_out, learn_rate, decay_matrix
    )
    new_in, m_in, u_in = adamw_update(w_mlp_in, grad_mlp_in, first_mlp_in, second_mlp_in, learn_rate, decay_matrix)
    new_out, m_out, u_out = adamw_update(
        w_mlp_out, grad_mlp_out, first_mlp_out, second_mlp_out, learn_rate, decay_matrix
    )
    new_vec, m_vec, u_vec = adamw_update(vectors, grad_vectors, first_vectors, second_vectors, vector_rate, 0.0)
    return (
        out,
        grad_tokens,
        grad_qkv,
        grad_attn_out,
        grad_mlp_in,
        grad_mlp_out,
        grad_vectors,
        new_qkv,
        new_att,
        new_in,
        new_out,
        new_vec,
        m_qkv,
        u_qkv,
        m_att,
        u_att,
        m_in,
        u_in,
        m_out,
        u_out,
        m_vec,
        u_vec,
    )


def solution(mesh):
    devices = mesh.devices.reshape(-1)
    layout = Mesh(devices.reshape(devices.size // TEAM, 2, 2, 2), EVERY)
    matrix, line = P(EVERY, None), P(EVERY)
    in_specs = (matrix, matrix, line, line) + (matrix,) * 4 + (line,) + (matrix,) * 8 + (line,) * 2
    out_specs = (matrix,) * 6 + (line,) + (matrix,) * 4 + (line,) + (matrix,) * 8 + (line,) * 2
    return jax.shard_map(body, mesh=layout, in_specs=in_specs, out_specs=out_specs, check_vma=False)
```

time: 4070 us -> 806 us (0.20)
  waiting for transfers between devices: 3260 us -> 325 us
  other arithmetic: 316 us -> 65.4 us
  local copies, waits for them, and re-layouts: 205 us -> 64.3 us
  blocking collectives: 44.2 us -> 125 us
    unnamed x6 -> x8, waiting for transfers between devices: 2800 us -> 0.8 us
    all_gather x4, waiting for transfers between devices: 461 us -> 141 us  [the longest x2 121 us: fetch(): lax.all_gather(got.reshape(rows_group, block.shape[2]), 'far', axis=0, ti...]
    concatenate x3 -> x4, other arithmetic: 272 us -> 11 us  [the longest x1 8.38 us: body(): jnp.concatenate([dot(mlp_in, d_hidden, contract_rows), dot(seed, activate...]
    reshape x2 -> x11, local copies, waits for them, and re-layouts: 181 us -> 8.13 us  [the longest x1 3.68 us: body(): attn_got[:, :, :3 * HEAD].reshape(TEAM, rows_dev, 3, HEAD)]
    reduce_scatter x0 -> x4, waiting for transfers between devices: none -> 165 us  [the longest x1 72.9 us: body(): lax.psum_scatter(part_out.astype(bf16), PLANE, scatter_dimension=0, tiled...]
    all_gather x1 -> x2, blocking collectives: 44.2 us -> 87.2 us  [the longest x1 45.4 us: body(): lax.all_gather(jnp.stack([block_first, block_live]), PLANE, axis=0, tiled...]
  transfers between devices with their start and end apart: 5 -> 12, of which waited for: 5 -> 8; matrix products, arithmetic and copies ran while one was open for 4% -> 36% of each run, Pallas kernels for 0% -> 0%
where the time goes in v1:
time: 806 us; the launch traced here: 800 us
  waiting for transfers between devices  325 us (40%)
  matrix products  188 us (23%)
  blocking collectives  125 us (16%)
  other arithmetic  65.4 us (8%)
  local copies, waits for them, and re-layouts  64.3 us (8%)
  starting transfers between devices  16 us (2%)
  between operations  15.6 us (2%)
    dot_general x12, matrix products, dot(): return lax.dot_general(left, right, dims, preferred_element_type=f32)  174 us
    all_gather x2, waiting for transfers between devices, fetch(): lax.all_gather(got.reshape(rows_group, block.shape[2]), 'far', axis=0, ti...  121 us
    reduce_scatter x1, waiting for transfers between devices, body(): lax.psum_scatter(part_out.astype(bf16), PLANE, scatter_dimension=0, tiled...  72.9 us
    reduce_scatter x1, waiting for transfers between devices, body(): lax.psum_scatter(part_back.astype(bf16), PLANE, scatter_dimension=0, tile...  67 us
    all_gather x1, blocking collectives, body(): lax.all_gather(jnp.stack([block_first, block_live]), PLANE, axis=0, tiled...  45.4 us
    all_gather x1, blocking collectives, body(): lax.all_gather(vectors.astype(bf16), EVERY, axis=0, tiled=True).astype(f32)  41.8 us
    all_to_all x1, blocking collectives, fetch(): got = lax.all_to_all(block, PLANE, 0, 0, tiled=True)  29.3 us
    reduce_scatter x2, waiting for transfers between devices, deliver(): mine = lax.psum_scatter(term, 'far', scatter_dimension=0, tiled=True)  25.1 us
  transfers between devices with their start and end apart: 12, of which 8 were waited for; matrix products, arithmetic and copies ran while one was open for 36% of the time, Pallas kernels for 0%

profile of v1, /device:TPU:0, one launch (start us, length us, event | category | flops | bytes accessed | tf_op | source)
XLA Modules:
  0.0 799.6 jit_solution(267213759487339527)
XLA Ops:
  12.2 29.3 %all_to_all.34 = bf16[8,64,1024]{2,1,0:T(8,128)(2,1)} all-to-all(bf16[8,64,1024]{2,1,0:T(8,128)(2,1)S(1)} %pad_maximum_fusion.3), channel_id=1, replica_groups=mesh['far'=4,'row'=2,'col'=2,'core'=2] {'row','col','core'}, dimensions={0} | all-to-all | bytes 2097152 | tf_op jit(solution)/shard_map/all_to_all | solution.py:132
  46.9 2.6 copy.182
  49.5 3.6 all-to-all-start.1
  53.1 45.4 %all-gather.1 = s32[8,2,2]{2,1,0:T(2,128)S(1)} all-gather(s32[1,2,2]{2,1,0:T(2,128)S(1)} %add_bitcast_fusion), channel_id=2, replica_groups=mesh['far'=4,'row'=2,'col'=2,'core'=2] {'row','col','core'}, dimensions={0}, use_global_device_ids=true | all-gather | bytes 144 | tf_op jit(solution)/shard_map/all_gather | solution.py:148
  98.9 41.8 %all-gather.2 = bf16[32,1,768]{2,1,0:T(2,128)(2,1)S(1)} all-gather(bf16[1,1,768]{2,1,0:T(2,128)(2,1)S(1)} %reshape.280), channel_id=1, replica_groups=mesh['far'=4,'row'=2,'col'=2,'core'=2] {'far','row','col','core'}, dimensions={0}, use_global_device_ids=true | all-gather | bytes 50688 | tf_op jit(solution)/shard_map/all_gather | solution.py:139
  148.4 4.7 convert_reduce_fusion
  154.2 2.3 fusion.13
  156.5 5.4 fusion.8
  161.9 18.6 %all-gather.10.cloned.1.call-done = bf16[2048,1024]{1,0:T(8,128)(2,1)} async-done(((bf16[512,1024]{1,0:T(8,128)(2,1)}), bf16[2048,1024]{1,0:T(8,128)(2,1)}) %all-gather.10.cloned.1.call-update) | async-done | bytes 4194320 | tf_op jit(solution)/shard_map/all_gather | solution.py:133
  180.5 10.4 %fusion.32 = f32[2048,768]{0,1:T(8,128)S(1)} fusion(bf16[2048,2048]{1,0:T(8,128)(2,1)} %fusion.8, bf16[2048,1024]{1,0:T(8,128)(2,1)} %all-gather.10.cloned.1.call-done), kind=kOutput, calls=%fused_computation.60 | convolution fusion | flops 6442450944 | bytes 17825792 | tf_op jit(solution)/shard_map/dot_general | solution.py:35
  191.0 2.6 copy-done.13
  194.2 3.4 slice_add_fusion.1
  209.8 2.9 multiply_select_fusion
  215.7 20.2 %all-gather.14.cloned.1.call-done = bf16[2048,2048]{1,0:T(8,128)(2,1)} async-done(((bf16[256,2048]{1,0:T(8,128)(2,1)}), bf16[2048,2048]{1,0:T(8,128)(2,1)}) %all-gather.14.cloned.1.call-update) | async-done | bytes 8388624 | tf_op jit(solution)/shard_map/all_gather | solution.py:147
  236.0 6.1 convolution_convert_fusion.4
  252.4 3.9 convolution_convert_fusion.5
  256.3 5.4 concatenate.71
  261.7 5.4 convolution_convert_fusion.6
  267.1 6.0 convolution_convert_fusion.3
  273.2 9.4 %convolution_convert_fusion.2 = bf16[2048,768]{0,1:T(8,128)(2,1)S(1)} fusion(bf16[2048,2048]{1,0:T(8,128)(2,1)} %fusion.8, bf16[2048,768]{1,0:T(8,128)(2,1)S(1)} %concatenate.71), kind=kOutput, calls=%fused_computation.49 | convolution fusion | flops 6444023808 | bytes 14680064 | tf_op jit(solution)/shard_map/dot_general | solution.py:35
  282.6 2.3 pad_maximum_fusion.1
  285.0 102.6 %all-gather.12.cloned.1.call-done = bf16[2048,2048]{1,0:T(8,128)(2,1)} async-done(((bf16[512,2048]{1,0:T(8,128)(2,1)}), bf16[2048,2048]{1,0:T(8,128)(2,1)}) %all-gather.12.cloned.1.call-update) | async-done | bytes 8388624 | tf_op jit(solution)/shard_map/all_gather | solution.py:133
  387.6 32.5 %multiply_convert_fusion = (bf16[2048,1024]{1,0:T(8,128)(2,1)S(1)}, f32[2048,1024]{1,0:T(8,128)}, f32[2048,1024]{1,0:T(8,128)}) fusion(f32[1024]{0:T(1024)S(1)} %copy-done.43, bf16[2048,2048]{1,0:T(8,128)(2,1)} %all-gather.12.cloned.1.call-done, bf16[2048,2048]{1,0:T(8,128)(2,1)} %all-gather.8.cloned.1.call-done, f32[2048]{0:T(1024)S(1)} %copy-done.40, ...), kind=kOutput, calls=%fused_computation.23 | convolution fusion | flops 8753512448 | bytes 33591296 | tf_op jit(solution)/shard_map/dot_general | solution.py:35
  420.2 15.1 %convolution_convert_fusion = bf16[2048,1024]{0,1:T(8,128)(2,1)} fusion(bf16[2048,2048]{1,0:T(8,128)(2,1)} %all-gather.14.cloned.1.call-done, bf16[2048,1024]{1,0:T(8,128)(2,1)S(1)} %get-tuple-element.45), kind=kOutput, calls=%fused_computation.39 | convolution fusion | flops 8592031744 | bytes 16777216 | tf_op jit(solution)/shard_map/dot_general | solution.py:35
  435.3 20.4 %convert_reduce_fusion.1 = (f32[1024]{0:T(1024)S(1)}, bf16[2048,1024]{1,0:T(8,128)(2,1)S(1)}) fusion(f32[2048,1024]{1,0:T(8,128)} %get-tuple-element.46, bf16[2048,2048]{1,0:T(8,128)(2,1)} %all-gather.14.cloned.1.call-done, bf16[2048,2048]{1,0:T(8,128)(2,1)} %all-gather.12.cloned.1.call-done, f32[2048,1024]{1,0:T(8,128)} %get-tuple-element.79, ...), kind=kOutput, calls=%fused_computation.21 | convolution fusion | flops 8625585152 | bytes 33562624 | tf_op jit(solution)/shard_map/dot_general | solution.py:35
  457.7 12.1 %convolution_convert_fusion.1 = bf16[2048,1024]{0,1:T(8,128)(2,1)} fusion(bf16[2048,1024]{1,0:T(8,128)(2,1)S(1)} %get-tuple-element.85, bf16[2048,2048]{1,0:T(8,128)(2,1)S(1)} %bitcast.98, f32[2048]{0:T(1024)S(1)} %copy-done.40, f32[2048]{0:T(1024)S(1)} %copy-done.39, f32[2048]{0:T(1024)S(1)} %add_rsqrt_fusion, f32[2048]{0:T(1024)S(1)} %broadcast_multiply_fusion), kind=kOutput, calls=%fused_computation.40 | convolution fusion | flops 8617197568 | bytes 16809984 | tf_op jit(solution)/shard_map/dot_general | solution.py:35
  469.8 8.4 %pad_maximum_fusion = bf16[2048,2048]{0,1:T(8,128)(2,1)} fusion(bf16[2048,1024]{0,1:T(8,128)(2,1)} %convolution_convert_fusion, bf16[2048,1024]{0,1:T(8,128)(2,1)} %convolution_convert_fusion.1), kind=kLoop, calls=%fused_computation.20 | loop fusion | flops 16777216 | bytes 16777216 | tf_op jit(solution)/shard_map/concatenate | solution.py:216
  480.1 11.7 %fusion.30 = f32[2048,2048]{1,0:T(8,128)} fusion(bf16[2048,768]{1,0:T(8,128)(2,1)S(1)} %copy-done.3, bf16[2048,1024]{1,0:T(8,128)(2,1)} %all-gather.10.cloned.1.call-done), kind=kOutput, calls=%fused_computation.58 | convolution fusion | flops 6442450944 | bytes 23068672 | tf_op jit(solution)/shard_map/dot_general | solution.py:35
  491.8 22.7 %fusion.71 = (f32[2048]{0:T(1024)S(1)}, f32[2048]{0:T(1024)S(1)}, bf16[2048,2048]{1,0:T(8,128)(2,1)}, f32[2048]{0:T(1024)S(1)}, f32[2048]{0:T(1024)S(1)}) fusion(f32[2048]{0:T(1024)S(1)} %add_rsqrt_fusion, f32[2048]{0:T(1024)S(1)} %broadcast_multiply_fusion, bf16[2048,2048]{1,0:T(8,128)(2,1)} %all-gather.8.cloned.1.call-done, f32[2048]{0:T(1024)S(1)} %copy-done.39, ...), kind=kOutput, calls=%fused_computation.181 | convolution fusion | flops 8644452352 | bytes 42008576 | tf_op jit(solution)/shard_map/dot_general | solution.py:35
  514.6 15.5 %fusion.22 = f32[2048,2048]{1,0:T(8,128)} fusion(bf16[2048,1024]{1,0:T(8,128)(2,1)} %copy-done.48, bf16[2048,2048]{1,0:T(8,128)(2,1)} %all-gather.12.cloned.1.call-done), kind=kOutput, calls=%fused_computation.43 | convolution fusion | flops 8589934592 | bytes 25165824 | tf_op jit(solution)/shard_map/dot_general | solution.py:35
  530.1 11.8 %add_convert_fusion.1 = bf16[2048,2048]{1,0:T(8,128)(2,1)} fusion(f32[2048,2048]{1,0:T(8,128)} %fusion.22, bf16[2048,256]{1,0:T(8,128)(2,1)S(1)} %bitcast.139, bf16[2048,1024]{1,0:T(8,128)(2,1)} %all-gather.10.cloned.1.call-done), kind=kOutput, calls=%fused_computation.17 | convolution fusion | flops 2155872256 | bytes 27262976 | tf_op jit(solution)/shard_map/dot_general | solution.py:35
  542.2 2.5 convert_reduce_fusion.2
  545.2 8.6 %all_to_all.35 = f32[8,4,768]{2,1,0:T(4,128)S(1)} all-to-all(f32[8,4,768]{2,1,0:T(4,128)S(1)} %copy.199), channel_id=1, replica_groups=mesh['far'=4,'row'=2,'col'=2,'core'=2] {'row','col','core'}, dimensions={0} | all-to-all | bytes 196608 | tf_op jit(solution)/shard_map/all_to_all | solution.py:256
  554.5 3.3 all-to-all-start.5
  560.0 3.3 all-to-all-done.5
  563.3 3.9 all-to-all-start.2
  568.6 14.0 %all-to-all-done.2 = bf16[8,64,1024]{2,1,0:T(8,128)(2,1)S(1)} async-done(((bf16[8,64,1024]{2,1,0:T(8,128)(2,1)}), bf16[8,64,1024]{2,1,0:T(8,128)(2,1)S(1)}, u32[]{:S(2)}, u32[]{:S(2)}) %all-to-all-start.2) | async-done | bytes 1048608 | tf_op jit(solution)/shard_map/all_to_all | solution.py:223
  583.9 3.7 reshape.270
  587.5 2.5 copy.194
  593.2 3.0 multiply_subtract_fusion.2
  596.2 25.1 %reduce-scatter.11.cloned.1.call-done = bf16[512,2048]{0,1:T(8,128)(2,1)} async-done(((bf16[2048,2048]{0,1:T(8,128)(2,1)}), bf16[512,2048]{0,1:T(8,128)(2,1)}) %reduce-scatter.11.cloned.1.call-update) | async-done | bytes 2097168 | tf_op jit(solution)/shard_map/reduce_scatter | solution.py:222
  621.3 3.9 copy.196
  625.2 4.5 all-to-all-start.3
  629.7 2.6 multiply_subtract_fusion.3
  632.3 67.0 %reduce-scatter.7.cloned.1.call-done = bf16[256,2048]{1,0:T(8,128)(2,1)} async-done(((bf16[2048,2048]{1,0:T(8,128)(2,1)}), bf16[256,2048]{1,0:T(8,128)(2,1)}) %reduce-scatter.7.cloned.1.call-update) | async-done | bytes 1048592 | tf_op jit(solution)/shard_map/reduce_scatter | solution.py:203
  701.3 72.9 %reduce-scatter.5.cloned.1.call-done = bf16[256,2048]{1,0:T(8,128)(2,1)} async-done(((bf16[2048,2048]{1,0:T(8,128)(2,1)}), bf16[256,2048]{1,0:T(8,128)(2,1)}) %reduce-scatter.5.cloned.1.call-update) | async-done | bytes 1048592 | tf_op jit(solution)/shard_map/reduce_scatter | solution.py:176
  774.1 4.0 fusion.40
  786.6 5.6 multiply_subtract_fusion
  (227 shorter events, 68.9 us)
Async XLA Ops:
  7.2 141.2 %all-gather.8.cloned.1.call-start = ((), (), s32[]{:S(2)}) async-start(), calls=%async_computation.10 | async-start | bytes 9437184 | tf_op jit(solution)/shard_map/all_gather | solution.py:146
  7.9 172.6 %all-gather.10.cloned.1.call-start = ((), (), s32[]{:S(2)}) async-start(), calls=%async_computation.11 | async-start | bytes 5242880 | tf_op jit(solution)/shard_map/all_gather | solution.py:133
  10.7 30.9 %copy-start.44 = (s32[2]{0:T(128)S(1)}, s32[2]{0:T(128)}, u32[]{:S(2)}) copy-start(s32[2]{0:T(128)} %param.22) | copy-start | bytes 28
  10.7 31.0 %copy-start.29 = (bf16[256,2048]{1,0:T(8,128)(2,1)S(1)}, bf16[256,2048]{1,0:T(8,128)(2,1)}, u32[]{:S(2)}) copy-start(bf16[256,2048]{1,0:T(8,128)(2,1)} %param.20) | copy-start | bytes 3145732
  41.6 194.4 %all-gather.14.cloned.1.call-start = ((), (), s32[]{:S(2)}) async-start(), calls=%async_computation.14 | async-start | bytes 9437184 | tf_op jit(solution)/shard_map/all_gather | solution.py:147
  41.7 4.2 copy-start.5
  46.7 2.8 copy-start.45
  46.9 51.7 %copy-start.36 = (f32[768]{0:T(1024)S(1)}, f32[768]{0:T(1024)}, u32[]{:S(2)}) copy-start(f32[768]{0:T(1024)} %param.27) | copy-start | bytes 9220
  49.5 97.0 %all-to-all-start.1 = ((bf16[8,64,2048]{2,1,0:T(8,128)(2,1)}), bf16[8,64,2048]{2,1,0:T(8,128)(2,1)S(1)}, u32[]{:S(2)}, u32[]{:S(2)}) async-start(bf16[8,64,2048]{2,1,0:T(8,128)(2,1)} %copy.182), calls=%async_computation.1 | async-start | bytes 4194304 | tf_op jit(solution)/shard_map/all_to_all | solution.py:132
  53.1 334.5 %all-gather.12.cloned.1.call-start = ((), (), s32[]{:S(2)}) async-start(), calls=%async_computation.12 | async-start | bytes 10485760 | tf_op jit(solution)/shard_map/all_gather | solution.py:133
  141.4 15.1 %copy-start.34 = (f32[2048]{0:T(1024)}, f32[2048]{0:T(1024)S(1)}, u32[]{:S(2)}) copy-start(f32[2048]{0:T(1024)S(1)} %get-tuple-element.74) | copy-start | bytes 24580
  147.8 409.9 %reduce-scatter.9.cloned.1.call-start = ((), (), s32[]{:S(2)}) async-start(), calls=%async_computation.16 | async-start | bytes 5242880 | tf_op jit(solution)/shard_map/reduce_scatter | solution.py:222
  148.4 5.8 copy-start
  236.0 6.1 copy-start.30
  247.8 4.6 copy-start.47
  261.7 11.5 %copy-start.2 = (bf16[2048,768]{1,0:T(8,128)(2,1)}, bf16[2048,768]{1,0:T(8,128)(2,1)S(1)}, u32[]{:S(2)}) copy-start(bf16[2048,768]{1,0:T(8,128)(2,1)S(1)} %concatenate.71) | copy-start | bytes 9437188
  284.9 102.7 %copy-start.39 = (f32[2048]{0:T(1024)S(1)}, f32[2048]{0:T(1024)}, u32[]{:S(2)}) copy-start(f32[2048]{0:T(1024)} %get-tuple-element.70) | copy-start | bytes 24580
  284.9 102.7 %copy-start.40 = (f32[2048]{0:T(1024)S(1)}, f32[2048]{0:T(1024)}, u32[]{:S(2)}) copy-start(f32[2048]{0:T(1024)} %get-tuple-element.69) | copy-start | bytes 24580
  284.9 102.7 %copy-start.43 = (f32[1024]{0:T(1024)S(1)}, f32[1024]{0:T(1024)}, u32[]{:S(2)}) copy-start(f32[1024]{0:T(1024)} %dynamic_slice.11) | copy-start | bytes 12292
  284.9 336.4 %reduce-scatter.11.cloned.1.call-start = ((), (), s32[]{:S(2)}) async-start(), calls=%async_computation.17 | async-start | bytes 10485760 | tf_op jit(solution)/shard_map/reduce_scatter | solution.py:222
  420.2 15.1 %copy-start.48 = (bf16[2048,1024]{1,0:T(8,128)(2,1)}, bf16[2048,1024]{1,0:T(8,128)(2,1)S(1)}, u32[]{:S(2)}) copy-start(bf16[2048,1024]{1,0:T(8,128)(2,1)S(1)} %get-tuple-element.45) | copy-start | bytes 12582916
  420.2 37.5 %slice-start = ((s8[8388608]{0:T(1024)(128)(4,1)}), s8[4194304]{0:T(1024)(128)(4,1)S(1)}, s32[]{:S(2)}) async-start(s8[8388608]{0:T(1024)(128)(4,1)} %bitcast.97), calls=%async_computation.18 | async-start | bytes 8388608
  435.3 22.4 %slice-start.1 = ((s8[8388608]{0:T(1024)(128)(4,1)}), s8[4194304]{0:T(1024)(128)(4,1)S(1)}, s32[]{:S(2)}) async-start(s8[8388608]{0:T(1024)(128)(4,1)} %bitcast.97), calls=%async_computation.19 | async-start | bytes 8388608
  478.2 13.6 %copy-start.35 = (f32[2048]{0:T(1024)S(1)}, f32[2048]{0:T(1024)}, u32[]{:S(2)}) copy-start(f32[2048]{0:T(1024)} %copy-done.34) | copy-start | bytes 24580
  478.2 221.1 %reduce-scatter.7.cloned.1.call-start = ((), (), s32[]{:S(2)}) async-start(), calls=%async_computation.15 | async-start | bytes 9437184 | tf_op jit(solution)/shard_map/reduce_scatter | solution.py:203
  514.6 15.5 %copy-start.31 = (bf16[8,256,256]{2,1,0:T(8,128)(2,1)S(1)}, bf16[8,256,256]{2,1,0:T(8,128)(2,1)}, u32[]{:S(2)}) copy-start(bf16[8,256,256]{2,1,0:T(8,128)(2,1)} %convolution_convert_fusion.6) | copy-start | bytes 3145732
  514.6 259.6 %reduce-scatter.5.cloned.1.call-start = ((), (), s32[]{:S(2)}) async-start(), calls=%async_computation.13 | async-start | bytes 9437184 | tf_op jit(solution)/shard_map/reduce_scatter | solution.py:176
  541.9 3.2 copy-start.32
  541.9 25.3 %copy-start.1 = (bf16[256,2048]{1,0:T(8,128)(2,1)S(1)}, bf16[256,2048]{1,0:T(8,128)(2,1)}, u32[]{:S(2)}) copy-start(bf16[256,2048]{1,0:T(8,128)(2,1)} %param.19) | copy-start | bytes 3145732
  544.8 23.1 %copy-start.37 = (f32[768]{0:T(1024)S(1)}, f32[768]{0:T(1024)}, u32[]{:S(2)}) copy-start(f32[768]{0:T(1024)} %param.27) | copy-start | bytes 9220
  544.8 23.1 %copy-start.41 = (f32[768]{0:T(1024)S(1)}, f32[768]{0:T(1024)}, u32[]{:S(2)}) copy-start(f32[768]{0:T(1024)} %param.36) | copy-start | bytes 9220
  544.8 23.1 %copy-start.42 = (f32[768]{0:T(1024)S(1)}, f32[768]{0:T(1024)}, u32[]{:S(2)}) copy-start(f32[768]{0:T(1024)} %param.37) | copy-start | bytes 9220
  554.5 8.9 %all-to-all-start.5 = ((f32[4,1,768]{2,1,0:T(1,128)}), f32[4,1,768]{2,1,0:T(1,128)S(1)}, u32[]{:S(2)}, u32[]{:S(2)}) async-start(f32[4,1,768]{2,1,0:T(1,128)} %all_to_all.26), calls=%async_computation.9 | async-start | bytes 24576 | tf_op jit(solution)/shard_map/all_to_all | solution.py:257
  563.3 19.2 %all-to-all-start.2 = ((bf16[8,64,1024]{2,1,0:T(8,128)(2,1)}), bf16[8,64,1024]{2,1,0:T(8,128)(2,1)S(1)}, u32[]{:S(2)}, u32[]{:S(2)}) async-start(bf16[8,64,1024]{2,1,0:T(8,128)(2,1)} %bitcast.23), calls=%async_computation.5 | async-start | bytes 2097152 | tf_op jit(solution)/shard_map/all_to_all | solution.py:223
  567.9 22.1 %copy-start.38 = (f32[768]{0:T(1024)}, f32[768]{0:T(1024)S(1)}, u32[]{:S(2)}) copy-start(f32[768]{0:T(1024)S(1)} %reduce_sum.169) | copy-start | bytes 9220
  590.1 3.1 copy-start.28
  590.9 38.8 %copy-start.21 = (f32[8,8,8,256]{3,2,0,1:T(8,128)}, f32[8,8,8,256]{3,2,0,1:T(8,128)S(1)}, u32[]{:S(2)}) copy-start(f32[8,8,8,256]{3,2,0,1:T(8,128)S(1)} %copy.212) | copy-start | bytes 1572868
  596.2 33.5 %copy-start.20 = (f32[64,2048]{1,0:T(8,128)S(1)}, f32[64,2048]{1,0:T(8,128)}, u32[]{:S(2)}) copy-start(f32[64,2048]{1,0:T(8,128)} %param.24) | copy-start | bytes 1572868
  625.2 148.9 %copy-start.4 = (bf16[256,2048]{1,0:T(8,128)(2,1)S(1)}, bf16[256,2048]{1,0:T(8,128)(2,1)}, u32[]{:S(2)}) copy-start(bf16[256,2048]{1,0:T(8,128)(2,1)} %get-tuple-element.44) | copy-start | bytes 3145732
  625.2 148.9 %copy-start.33 = (f32[2048]{0:T(1024)S(1)}, f32[2048]{0:T(1024)}, u32[]{:S(2)}) copy-start(f32[2048]{0:T(1024)} %get-tuple-element.68) | copy-start | bytes 24580
  625.2 152.9 %all-to-all-start.3 = ((bf16[8,64,2048]{2,1,0:T(8,128)(2,1)}), bf16[8,64,2048]{2,1,0:T(8,128)(2,1)}, u32[]{:S(2)}, u32[]{:S(2)}) async-start(bf16[8,64,2048]{2,1,0:T(8,128)(2,1)} %bitcast.105), calls=%async_computation.7 | async-start | bytes 4194304 | tf_op jit(solution)/shard_map/all_to_all | solution.py:223
  780.3 3.3 copy-start.19
  780.9 3.9 copy-start.6
  780.9 4.5 copy-start.7
  780.9 5.1 copy-start.16
  780.9 5.7 copy-start.17
  781.1 11.2 %copy-start.8 = (f32[8,8,8,1024]{3,2,0,1:T(8,128)}, f32[8,8,8,1024]{3,2,0,1:T(8,128)S(1)}, u32[]{:S(2)}) copy-start(f32[8,8,8,1024]{3,2,0,1:T(8,128)S(1)} %copy.214) | copy-start | bytes 6291460
  781.2 11.0 %copy-start.9 = (f32[8,8,8,1024]{3,2,0,1:T(8,128)}, f32[8,8,8,1024]{3,2,0,1:T(8,128)S(1)}, u32[]{:S(2)}) copy-start(f32[8,8,8,1024]{3,2,0,1:T(8,128)S(1)} %copy.213) | copy-start | bytes 6291460
  (16 other events, 24.3 us)
Sparse Core Ops, SparseCore 0:
  9.9 82.2 all-gather.7
  93.8 86.6 all-gather.9
  183.0 52.9 all-gather.13
  238.0 149.6 all-gather.11
  389.8 74.9 reduce-scatter.8
  478.4 142.9 reduce-scatter.10
  625.2 74.1 reduce-scatter.6
  702.8 71.2 reduce-scatter.4

commit v2 on v1

v2 whole, which is shorter than its diff:
```python
import jax
import jax.numpy as jnp
from jax import lax
from jax.experimental import pallas as pl
from jax.experimental.pallas import tpu as pltpu
from jax.sharding import Mesh, PartitionSpec as P

D = 2048
HEADS = 8
HEAD = 256
FF = 8192
ROT = 64
BLOCK = 128
BLK_DEV = 2
STEP = 3
VEC = 24576
TEAM = 8
SLICE_FF = FF // TEAM
CHUNKS = ((0, 256), None, (512, 1024), (256, 512))
PACK_ROWS = 16
FENCE = 20000
LANES = 128

eps_norm = 1e-05
beta_one = 0.9
beta_two = 0.95
learn_rate = 0.03
vector_rate = 0.3
decay_matrix = 0.1
eps_adam = 1e-08
masked_score = -1e30
plain = (((1,), (0,)), ((), ()))
contract_rows = (((0,), (0,)), ((), ()))
contract_cols = (((1,), (1,)), ((), ()))
bf16 = jnp.bfloat16
f32 = jnp.float32
VMEM_BYTES = 56 * 1024 * 1024
NEAR = ("low", "row", "core")
CROSS = ("col", "far")
EVERY = ("far", "low", "row", "col", "core")
SWAP = [(0, 1), (1, 0)]
COST_UNIT = 115000000
ANYWHERE = pl.BlockSpec(memory_space=pl.ANY)


def dot(left, right, dims=plain):
    return lax.dot_general(left, right, dims, preferred_element_type=f32)


def after(value, *others):
    return lax.optimization_barrier((value, *others))[0]


def params(cost):
    return dict(
        compiler_params=pltpu.CompilerParams(vmem_limit_bytes=VMEM_BYTES),
        cost_estimate=pl.CostEstimate(flops=int(cost * COST_UNIT), bytes_accessed=1024, transcendentals=0),
    )


def shaped(shape, dtype):
    return jax.ShapeDtypeStruct(shape, dtype)


def blocks(shape, index):
    return pl.BlockSpec(shape, index)


def split_vectors(vec_all):
    boundaries = [D, 2 * D, 3 * D, 3 * D + FF, 4 * D + FF, 5 * D + FF, 6 * D + FF, 7 * D + FF]
    return jnp.split(vec_all, boundaries)


def adamw_update(weight, grad, first_m, second_m, rate_value, decay_value):
    first_new = beta_one * first_m + (1.0 - beta_one) * grad
    second_new = beta_two * second_m + (1.0 - beta_two) * grad * grad
    fix_one = 1.0 - beta_one**STEP
    fix_two = 1.0 - beta_two**STEP
    direction = first_new / fix_one / (jnp.sqrt(second_new / fix_two) + eps_adam)
    return (weight - rate_value * (direction + decay_value * weight), first_new, second_new)


def normalize(values):
    centred = values - jnp.mean(values, axis=-1, keepdims=True)
    spread = jnp.mean(centred * centred, axis=-1, keepdims=True)
    scale = lax.rsqrt(spread + eps_norm)
    return centred * scale, scale


def rotary_rows(position):
    lane = jnp.arange(LANES)
    frequency = 10000.0 ** (-(2.0 * (lane % (ROT // 2)).astype(f32)) / ROT)
    angles = position[:, None] * frequency[None, :]
    sine = jnp.sin(angles)
    cosine = jnp.where(lane < ROT, jnp.cos(angles), 1.0)
    return (
        cosine,
        jnp.where(lane < ROT // 2, -sine, 0.0),
        jnp.where((lane >= ROT // 2) & (lane < ROT), sine, 0.0),
    )


def gelu_pair(hidden):
    cumulative = 0.5 * (1.0 + lax.erf(hidden * (0.5**0.5)))
    density = jnp.exp(-0.5 * hidden * hidden) * 0.3989422804014327
    return hidden * cumulative, cumulative + hidden * density


def stacked_copies(refs, buffer, sems, rows_dev, columns=None):
    copies, begin = [], 0
    for ref in refs:
        parts = [ref] if len(ref.shape) == 2 else [ref.at[k, 0:rows_dev] for k in range(ref.shape[0])]
        for part in parts:
            rows = part.shape[0]
            source = part if columns is None else part.at[:, columns]
            copies.append(pltpu.make_async_copy(source, buffer.at[begin : begin + rows], sems.at[len(copies)]))
            begin += rows
    return copies


def copy_count(pieces):
    return sum(1 if piece.ndim == 2 else piece.shape[0] for piece in pieces)


def member_copies(members_ref, team_ref, kind, buffer, sems):
    count, both, _ = team_ref.shape
    rows = both // 2
    return [
        pltpu.make_async_copy(
            team_ref.at[members_ref[k], kind * rows : (kind + 1) * rows],
            buffer.at[k * rows : (k + 1) * rows],
            sems.at[k],
        )
        for k in range(count)
    ]


def prepare_tokens(order, live, tokens, cotangent):
    slots = tokens.shape[0]

    def kernel(order_ref, live_ref, x_ref, y_ref, both_ref):
        row = lax.broadcasted_iota(jnp.int32, (slots, LANES), 0)
        end = jnp.where(row < BLOCK, live_ref[0], live_ref[1] + BLOCK)
        alive = row < end
        for k in range(D // LANES):
            source = pl.ds(pl.multiple_of(order_ref[k] * LANES, LANES), LANES)
            here = slice(k * LANES, (k + 1) * LANES)
            both_ref[:slots, here] = x_ref[:, source]
            both_ref[slots:, here] = jnp.where(alive, y_ref[:, source].astype(f32), 0.0).astype(bf16)

    whole = blocks((slots, D), lambda i, *_: (0, 0))
    return pl.pallas_call(
        kernel,
        grid_spec=pltpu.PrefetchScalarGridSpec(
            num_scalar_prefetch=2,
            grid=(1,),
            in_specs=[whole, whole],
            out_specs=blocks((2 * slots, D), lambda i, *_: (0, 0)),
        ),
        out_shape=shaped((2 * slots, D), bf16),
        **params(4),
    )(order, live, tokens, cotangent)


def norm_inputs(members, team, gain_one, shift_one, gain_two, shift_two):
    count, both, _ = team.shape
    rows = both // 2

    def kernel(members_ref, team_ref, g1, s1, g2, s2, one_ref, two_ref, hat_ref, buffer, sems):
        step = pl.program_id(0)
        copies = member_copies(members_ref, team_ref, 0, buffer, sems)

        @pl.when(step == 0)
        def _():
            for copy in copies:
                copy.start()

        for k in range(count):

            @pl.when(step == k)
            def _(k=k):
                copies[k].wait()

        hat, _ = normalize(buffer[pl.ds(pl.multiple_of(step * rows, rows), rows), :].astype(f32))
        hat_ref[...] = hat.astype(bf16)
        one_ref[...] = (hat * g1[...] + s1[...]).astype(bf16)
        two_ref[...] = (hat * g2[...] + s2[...]).astype(bf16)

    line = blocks((1, D), lambda i, *_: (0, 0))
    return pl.pallas_call(
        kernel,
        grid_spec=pltpu.PrefetchScalarGridSpec(
            num_scalar_prefetch=1,
            grid=(count,),
            in_specs=[ANYWHERE] + [line] * 4,
            out_specs=[blocks((rows, D), lambda i, *_: (i, 0))] * 3,
            scratch_shapes=[pltpu.VMEM((count * rows, D), bf16), pltpu.SemaphoreType.DMA((count,))],
        ),
        out_shape=[shaped((count * rows, D), bf16)] * 3,
        **params(FENCE),
    )(members, team, gain_one, shift_one, gain_two, shift_two)


def open_chunk(step, rows, rows_dev, members_ref, team_ref, w_refs, y_all, w_all, y_sems, w_sems):
    y_copies = member_copies(members_ref, team_ref, 1, y_all, y_sems)
    w_copies = stacked_copies(w_refs, w_all, w_sems, rows_dev)
    slots = team_ref.shape[1] // 2

    @pl.when(step == 0)
    def _():
        for copy in w_copies + y_copies:
            copy.start()
        for copy in w_copies:
            copy.wait()

    for k, copy in enumerate(y_copies):

        @pl.when(step == k * slots // rows)
        def _(copy=copy):
            copy.wait()

    return y_all[pl.ds(pl.multiple_of(step * rows, rows), rows), :]


def close_chunk(step, last, acc_ref, keep_ref, send_ref, sum_ref, cols, first_term, second_term, column_sum):
    @pl.when(step == 0)
    def _():
        acc_ref[:, :cols] = first_term
        acc_ref[:, cols:] = second_term
        sum_ref[...] = column_sum

    @pl.when((step > 0) & (step < last))
    def _():
        acc_ref[:, :cols] += first_term
        acc_ref[:, cols:] += second_term
        sum_ref[...] += column_sum

    @pl.when(step == last)
    def _():
        half = D // 2
        keep_ref[:, :cols] = (acc_ref[:half, :cols] + first_term[:half]).astype(bf16)
        keep_ref[:, cols:] = (acc_ref[:half, cols:] + second_term[:half]).astype(bf16)
        send_ref[:, :cols] = (acc_ref[half:, :cols] + first_term[half:]).astype(bf16)
        send_ref[:, cols:] = (acc_ref[half:, cols:] + second_term[half:]).astype(bf16)
        sum_ref[...] += column_sum


def chunk_scratch(total, width, y_count, w_count):
    return [
        pltpu.VMEM((D, width), f32),
        pltpu.VMEM((total, D), bf16),
        pltpu.VMEM((D, width), bf16),
        pltpu.SemaphoreType.DMA((y_count,)),
        pltpu.SemaphoreType.DMA((w_count,)),
    ]


def mlp_chunk(members, team, a, w_pieces, b, rows_dev, rows=512):
    total, width = a.shape[0], w_pieces[0].shape[-1]
    cols = width // 2
    nw = len(w_pieces)

    def kernel(members_ref, team_ref, *refs):
        w_refs = refs[:nw]
        a_ref, b_ref, act_ref, dh_ref, keep_ref, send_ref, sum_ref, acc_ref, y_all, w_all, y_sems, w_sems = refs[nw:]
        step, last = pl.program_id(0), pl.num_programs(0) - 1
        y = open_chunk(step, rows, rows_dev, members_ref, team_ref, w_refs, y_all, w_all, y_sems, w_sems)
        a = a_ref[...]
        act, slope = gelu_pair(dot(a, w_all[:, :cols]) + b_ref[...])
        act = act.astype(bf16)
        dh = (dot(y, w_all[:, cols:]) * slope).astype(bf16)
        act_ref[...] = act
        dh_ref[...] = dh
        column_sum = jnp.sum(dh.astype(f32), axis=0, keepdims=True)
        first_term, second_term = dot(a, dh, contract_rows), dot(y, act, contract_rows)
        close_chunk(step, last, acc_ref, keep_ref, send_ref, sum_ref, cols, first_term, second_term, column_sum)

    fixed = lambda r, c: blocks((r, c), lambda i, *_: (0, 0))
    moving = lambda c: blocks((rows, c), lambda i, *_: (i, 0))
    return pl.pallas_call(
        kernel,
        grid_spec=pltpu.PrefetchScalarGridSpec(
            num_scalar_prefetch=1,
            grid=(total // rows,),
            in_specs=[ANYWHERE] * (1 + nw) + [moving(D), fixed(1, cols)],
            out_specs=[moving(cols), moving(cols), fixed(D // 2, width), fixed(D // 2, width), fixed(1, cols)],
            scratch_shapes=chunk_scratch(total, width, team.shape[0], copy_count(w_pieces)),
        ),
        out_shape=[shaped((total, cols), bf16)] * 2 + [shaped((D // 2, width), bf16)] * 2 + [shaped((1, cols), f32)],
        **params(FENCE if width > D // 4 else 15),
    )(members, team, *w_pieces, a, b)


def turn_lanes(values, cosine, low_sine, high_sine):
    part = values[:, :LANES]
    part = part * cosine + pltpu.roll(part, LANES - ROT // 2, 1) * low_sine + pltpu.roll(part, ROT // 2, 1) * high_sine
    return jnp.concatenate([part, values[:, LANES:]], axis=1)


def attn_chunk(members, first, live, team, a, w_pieces, b, rotary, rows_dev, rows=512):
    total, width = a.shape[0], w_pieces[0].shape[-1]
    nw = len(w_pieces)
    slots = BLK_DEV * BLOCK
    buffers = rows // slots

    def kernel(members_ref, first_ref, live_ref, team_ref, *refs):
        w_refs = refs[:nw]
        a_ref, b_ref, cos_ref, low_ref, high_ref, att_ref, dm_ref, keep_ref, send_ref, sum_ref = refs[nw : nw + 10]
        acc_ref, y_all, w_all, y_sems, w_sems = refs[nw + 10 :]
        step, last = pl.program_id(0), pl.num_programs(0) - 1
        y = open_chunk(step, rows, rows_dev, members_ref, team_ref, w_refs, y_all, w_all, y_sems, w_sems)
        a = a_ref[...]
        mixed = dot(a, w_all[:, : 3 * HEAD]) + b_ref[...]
        datt_all = dot(y, w_all[:, 3 * HEAD :]).astype(bf16)
        row = lax.broadcasted_iota(jnp.int32, (slots, slots), 0)
        col = lax.broadcasted_iota(jnp.int32, (slots, slots), 1)
        for k in range(buffers):
            buf = step * buffers + k
            part = slice(k * slots, (k + 1) * slots)
            cosine, low_sine, high_sine = cos_ref[part], low_ref[part], high_ref[part]
            queries = turn_lanes(mixed[part, :HEAD], cosine, low_sine, high_sine).astype(bf16)
            keys = turn_lanes(mixed[part, HEAD : 2 * HEAD], cosine, low_sine, high_sine).astype(bf16)
            values = mixed[part, 2 * HEAD :].astype(bf16)
            datt = datt_all[part]
            parted = jnp.where(first_ref[buf, 0] == first_ref[buf, 1], 0, 1)
            live_end = jnp.where(col < BLOCK, live_ref[buf, 0], live_ref[buf, 1] + BLOCK)
            other = jnp.where((row >= BLOCK) & (col < BLOCK), parted, 0)
            allowed = (col <= row) & (other == 0) & ((col < live_end) | (col == row))
            scores = jnp.where(allowed, dot(queries, keys, contract_cols) * HEAD ** (-0.5), masked_score)
            raised = jnp.exp(scores - jnp.max(scores, axis=1, keepdims=True))
            probs = raised / jnp.sum(raised, axis=1, keepdims=True)
            probs_low = probs.astype(bf16)
            att_ref[part] = dot(probs_low, values).astype(bf16)
            d_probs = dot(datt, values, contract_cols)
            d_scores = (probs * (d_probs - jnp.sum(probs * d_probs, axis=1, keepdims=True))).astype(bf16)
            d_queries = dot(d_scores, keys) * HEAD ** (-0.5)
            d_keys = dot(d_scores, queries, contract_rows) * HEAD ** (-0.5)
            dm_ref[part, :HEAD] = turn_lanes(d_queries, cosine, -low_sine, -high_sine).astype(bf16)
            dm_ref[part, HEAD : 2 * HEAD] = turn_lanes(d_keys, cosine, -low_sine, -high_sine).astype(bf16)
            dm_ref[part, 2 * HEAD :] = dot(probs_low, datt, contract_rows).astype(bf16)
        d_mixed = dm_ref[...]
        column_sum = jnp.sum(d_mixed.astype(f32), axis=0, keepdims=True)
        first_term, second_term = dot(a, d_mixed, contract_rows), dot(y, att_ref[...], contract_rows)
        close_chunk(step, last, acc_ref, keep_ref, send_ref, sum_ref, 3 * HEAD, first_term, second_term, column_sum)

    fixed = lambda r, c: blocks((r, c), lambda i, *_: (0, 0))
    moving = lambda c: blocks((rows, c), lambda i, *_: (i, 0))
    return pl.pallas_call(
        kernel,
        grid_spec=pltpu.PrefetchScalarGridSpec(
            num_scalar_prefetch=3,
            grid=(total // rows,),
            in_specs=[ANYWHERE] * (1 + nw) + [moving(D), fixed(1, 3 * HEAD)] + [moving(LANES)] * 3,
            out_specs=[moving(HEAD), moving(3 * HEAD), fixed(D // 2, width), fixed(D // 2, width), fixed(1, 3 * HEAD)],
            scratch_shapes=chunk_scratch(total, width, team.shape[0], copy_count(w_pieces)),
        ),
        out_shape=[shaped((total, HEAD), bf16), shaped((total, 3 * HEAD), bf16)]
        + [shaped((D // 2, width), bf16)] * 2
        + [shaped((1, 3 * HEAD), f32)],
        **params(FENCE),
    )(members, first, live, team, *w_pieces, a, b, *rotary)


def token_block(i, low_first):
    half = TEAM // 2
    within = i % half
    if low_first:
        within = within % 2 * 2 + within // 2
    return (i // half + 1) % 2 * half + within


def write_half(value, send_ref, keep_ref):
    first_half = pl.program_id(0) < TEAM // 2

    @pl.when(first_half)
    def _():
        send_ref[...] = value

    @pl.when(jnp.logical_not(first_half))
    def _():
        keep_ref[...] = value


def half_outputs(rows, total):
    half = TEAM // 2
    specs = [
        blocks((rows, D), lambda i: (jnp.minimum(i, half - 1), 0)),
        blocks((rows, D), lambda i: (jnp.maximum(i - half, 0), 0)),
    ]
    return specs, [shaped((total // 2, D), bf16)] * 2


def fetch_columns(groups, buffers, sems, places, rows_dev):
    copies = []
    for k, refs in enumerate(groups):
        begin, end = places[k]
        copies += stacked_copies(refs, buffers[k], sems[k], rows_dev, slice(begin, end))

    @pl.when(pl.program_id(0) == 0)
    def _():
        for copy in copies:
            copy.start()
        for copy in copies:
            copy.wait()


def out_part(lefts, weights, places, rows_dev):
    count, per, total = len(lefts), len(weights[0]), lefts[0].shape[0]
    rows = total // TEAM

    def kernel(*refs):
        groups = [refs[k * per : (k + 1) * per] for k in range(count)]
        left_refs = refs[count * per : count * per + count]
        send_ref, keep_ref, *scratch = refs[count * per + count :]
        fetch_columns(groups, scratch[:count], scratch[count:], places, rows_dev)
        buffers = scratch[:count]
        value = None
        for k in range(count):
            term = dot(left_refs[k][...], buffers[k][...], contract_cols)
            value = term if value is None else value + term
        write_half(value.astype(bf16), send_ref, keep_ref)

    specs, shapes = half_outputs(rows, total)
    return pl.pallas_call(
        kernel,
        grid=(TEAM,),
        in_specs=[ANYWHERE] * (count * per) + [blocks((rows, v.shape[1]), lambda i: (token_block(i, True), 0)) for v in lefts],
        out_specs=specs,
        out_shape=shapes,
        scratch_shapes=[pltpu.VMEM((D, e - b), bf16) for b, e in places]
        + [pltpu.SemaphoreType.DMA((copy_count(group),)) for group in weights],
        **params(19),
    )(*[piece for group in weights for piece in group], *lefts)


def back_part(hat, lefts, weights, places, attn_index, gain_one, gain_two, rows_dev):
    count, per, total = len(lefts), len(weights[0]), hat.shape[0]
    rows = total // TEAM

    def kernel(*refs):
        groups = [refs[k * per : (k + 1) * per] for k in range(count)]
        left_refs = refs[count * per : count * per + count]
        hat_ref, one_ref, two_ref, send_ref, keep_ref, sums_ref, *scratch = refs[count * per + count :]
        fetch_columns(groups, scratch[:count], scratch[count:], places, rows_dev)
        buffers = scratch[:count]
        d_one, d_two = None, None
        for k in range(count):
            term = dot(left_refs[k][...], buffers[k][...], contract_cols)
            if k == attn_index:
                d_one = term
            else:
                d_two = term if d_two is None else d_two + term
        write_half((d_one * one_ref[...] + d_two * two_ref[...]).astype(bf16), send_ref, keep_ref)
        hat_now = hat_ref[...].astype(f32)
        sums = [jnp.sum(v, axis=0, keepdims=True) for v in (d_one * hat_now, d_one, d_two * hat_now, d_two)]

        @pl.when(pl.program_id(0) == 0)
        def _():
            for k in range(4):
                sums_ref[k : k + 1] = sums[k]

        @pl.when(pl.program_id(0) > 0)
        def _():
            for k in range(4):
                sums_ref[k : k + 1] += sums[k]

    moving = lambda c: blocks((rows, c), lambda i: (token_block(i, False), 0))
    fixed = lambda r, c: blocks((r, c), lambda i: (0, 0))
    specs, shapes = half_outputs(rows, total)
    return pl.pallas_call(
        kernel,
        grid=(TEAM,),
        in_specs=[ANYWHERE] * (count * per)
        + [moving(v.shape[1]) for v in lefts]
        + [moving(D), fixed(1, D), fixed(1, D)],
        out_specs=specs + [fixed(8, D)],
        out_shape=shapes + [shaped((8, D), f32)],
        scratch_shapes=[pltpu.VMEM((D, e - b), bf16) for b, e in places]
        + [pltpu.SemaphoreType.DMA((copy_count(group),)) for group in weights],
        **params(FENCE),
    )(*[piece for group in weights for piece in group], *lefts, hat, gain_one, gain_two)


def split_sum(left, right, steps):
    rows, width = left.shape
    block = rows // 2 // steps

    def kernel(l_low, l_high, r_low, r_high, keep_ref, send_ref):
        keep_ref[...] = l_low[...].astype(f32) + r_low[...].astype(f32)
        send_ref[...] = (l_high[...].astype(f32) + r_high[...].astype(f32)).astype(bf16)

    low = blocks((block, width), lambda i: (i, 0))
    high = blocks((block, width), lambda i: (i + steps, 0))
    return pl.pallas_call(
        kernel,
        grid=(steps,),
        in_specs=[low, high, low, high],
        out_specs=[low, low],
        out_shape=[shaped((rows // 2, width), f32), shaped((rows // 2, width), bf16)],
        **params(4),
    )(left, left, right, right)


def last_sum(kept, got, steps, cost):
    rows, width = kept.shape

    def kernel(l_ref, r_ref, out_ref):
        out_ref[...] = (l_ref[...] + r_ref[...].astype(f32)).astype(bf16)

    spec = blocks((rows // steps, width), lambda i: (i, 0))
    return pl.pallas_call(
        kernel,
        grid=(steps,),
        in_specs=[spec, spec],
        out_specs=spec,
        out_shape=shaped((rows, width), bf16),
        **params(cost),
    )(kept, got)


def finish_tokens(order, tokens, other, kept, got, back):
    slots = tokens.shape[0]
    steps = 2
    rows = slots // steps

    def kernel(order_ref, x_ref, other_ref, kept_ref, got_ref, out_ref, sum_ref):
        for k in range(D // LANES):
            source = pl.ds(pl.multiple_of(order_ref[k] * LANES, LANES), LANES)
            sum_ref[:, k * LANES : (k + 1) * LANES] = kept_ref[:, source] + got_ref[:, source].astype(f32)
        total = sum_ref[...]
        x = x_ref[...].astype(f32)
        if back:
            hat, scale = normalize(x)
            inner = jnp.mean(total * hat, axis=-1, keepdims=True)
            total = scale * (total - jnp.mean(total, axis=-1, keepdims=True) - hat * inner)
            x = other_ref[...].astype(f32)
        else:
            total = total + other_ref[...]
        out_ref[...] = (x + total).astype(bf16)

    moving = blocks((rows, D), lambda i, *_: (i, 0))
    return pl.pallas_call(
        kernel,
        grid_spec=pltpu.PrefetchScalarGridSpec(
            num_scalar_prefetch=1,
            grid=(steps,),
            in_specs=[moving, moving if back else blocks((1, D), lambda i, *_: (0, 0)), moving, moving],
            out_specs=moving,
            scratch_shapes=[pltpu.VMEM((rows, D), f32)],
        ),
        out_shape=shaped((slots, D), bf16),
        **params(4),
    )(order, tokens, other, kept, got)


def adamw_columns(got, weight, first_m, second_m, section, unit, offset, sections, cost, held=None):
    rows, width = weight.shape
    span = TEAM * unit
    part = max(rows // 4, 16) if rows % 16 == 0 else rows
    got_spec = blocks((TEAM, part, unit), lambda k, i: (0, i, section + k))
    full = blocks((part, span), lambda k, i: (i, offset + k))

    def kernel(g_ref, w_ref, m_ref, u_ref, *refs):
        grad_ref, new_ref, mo_ref, uo_ref = refs[-4:]
        for k in range(TEAM):
            here = slice(k * unit, (k + 1) * unit)
            grad = g_ref[k].astype(f32)
            new, m_new, u_new = adamw_update(
                w_ref[:, here], grad, m_ref[:, here], u_ref[:, here], learn_rate, decay_matrix
            )
            grad_ref[:, here] = grad
            new_ref[:, here] = new
            mo_ref[:, here] = m_new
            uo_ref[:, here] = u_new

    extra = list(held) if held is not None else []
    return pl.pallas_call(
        kernel,
        grid=(sections, rows // part),
        in_specs=[got_spec, full, full, full] + [ANYWHERE] * len(extra),
        out_specs=[full] * 4,
        out_shape=[shaped((rows, width), f32)] * 4,
        input_output_aliases={4 + k: k for k in range(len(extra))},
        **params(cost),
    )(got, weight, first_m, second_m, *extra)


def body(
    tokens,
    cotangent,
    block_first,
    block_live,
    w_qkv,
    w_attn_out,
    w_mlp_in,
    w_mlp_out,
    vectors,
    first_qkv,
    second_qkv,
    first_attn_out,
    second_attn_out,
    first_mlp_in,
    second_mlp_in,
    first_mlp_out,
    second_mlp_out,
    first_vectors,
    second_vectors,
):
    far_size = lax.axis_size("far")
    paired = far_size == 2
    groups = 2 * far_size
    slot_total = tokens.shape[0]
    rows_dev = w_qkv.shape[0]
    rows_team = rows_dev * TEAM
    team_slots = slot_total * TEAM
    piece = vectors.shape[0]
    half = TEAM // 2
    count = len(CHUNKS)
    me = lax.axis_index(NEAR)
    far, column = lax.axis_index("far"), lax.axis_index("col")

    def flips(values, col_axis, far_axis):
        if not paired:
            return values
        values = jnp.where(column == 1, jnp.flip(values, col_axis), values)
        return jnp.where(far == 1, jnp.flip(values, far_axis), values)

    def local_order(values):
        lead = values.shape[:-1]
        k = len(lead)
        parts = values.reshape(*lead, far_size, half, 2, 2 * rows_dev)
        parts = jnp.transpose(parts, (*range(k), k + 2, k, k + 1, k + 3))
        return flips(parts, k, k + 1).reshape(*lead, D)

    def own_order(values):
        lead = values.shape[:-1]
        k = len(lead)
        parts = flips(values.reshape(*lead, 2, far_size, half, 2 * rows_dev), k, k + 1)
        return jnp.transpose(parts, (*range(k), k + 1, k + 2, k, k + 3)).reshape(*lead, D)

    place_in_row = jnp.arange(D // LANES, dtype=jnp.int32)
    if paired:
        c, f, r = place_in_row // (2 * half), place_in_row // half % 2, place_in_row % half
        to_local = ((f ^ far) * half + r) * 2 + (c ^ column)
        f, r, c = place_in_row // (2 * half), place_in_row // 2 % half, place_in_row % 2
        to_own = ((c ^ column) * 2 + (f ^ far)) * half + r
    else:
        to_local, to_own = place_in_row, place_in_row

    payload = jnp.concatenate([vectors.astype(bf16), block_first.astype(bf16), block_live.astype(bf16)])

    def columns(chunk):
        cut = lambda w, parts: w.astype(bf16).reshape(rows_dev, parts, TEAM, -1)
        if chunk is None:
            query = cut(w_qkv, 3).transpose(2, 0, 1, 3).reshape(TEAM, rows_dev, 3 * HEAD)
            return jnp.concatenate([query, cut(w_attn_out, 1)[:, 0].transpose(1, 0, 2)], axis=2)
        begin, end = chunk
        span = slice(TEAM * begin, TEAM * end)
        return jnp.concatenate([cut(w[:, span], 1)[:, 0].transpose(1, 0, 2) for w in (w_mlp_in, w_mlp_out)], axis=2)

    owns, far_got = [], [None] * count
    for index, chunk in enumerate(CHUNKS):
        block = columns(chunk)
        if index == 0 and paired:
            width = block.shape[2]
            extra = jnp.pad(payload, (0, PACK_ROWS * width - payload.shape[0])).reshape(1, PACK_ROWS, width)
            block = jnp.concatenate([block, jnp.broadcast_to(extra, (TEAM, PACK_ROWS, width))], axis=1)
        waits = owns[-1:]
        if paired and index == 2:
            far_got[0] = lax.ppermute(owns[0], "far", SWAP)
            waits = waits + far_got[:1]
        got = lax.all_to_all(after(block, *waits) if waits else block, NEAR, 0, 0, tiled=True)
        owns.append(got if got.shape[1] != rows_dev else got.reshape(rows_team, got.shape[2]))

    if paired:
        both_send = prepare_tokens(to_local, block_live, tokens, cotangent)
    else:
        both_send = prepare_tokens(to_local, block_live, local_order(tokens), local_order(cotangent))
    team = lax.all_gather(both_send, NEAR, axis=0, tiled=False)
    members = jnp.array([4 * l + 2 * r + c for c in range(2) for r in range(2) for l in range(2)], jnp.int32) ^ me

    w_chunks = []

    def send_far(index, *waits):
        far_got[index] = lax.ppermute(after(owns[index], far_got[index - 1], *waits), "far", SWAP)

    def cross(index, *waits):
        if paired:
            w_chunks[index][1] = far_got[index]
            over = after(far_got[index], *waits) if waits else far_got[index]
            w_chunks[index][3] = lax.ppermute(over, "col", SWAP)

    if paired:
        for own in owns:
            w_chunks.append([own, None, lax.ppermute(own, "col", SWAP), None])
        send_far(1, owns[2])
        send_far(2, owns[3])
    else:
        for own in owns:
            w_chunks.append([lax.all_gather(own, CROSS, axis=0, tiled=True)])
    cross(0)
    cross(1)

    length = piece + 2 * BLK_DEV
    if paired:
        got = jnp.stack([part[:, rows_dev:].reshape(TEAM, -1)[:, :length] for part in (*w_chunks[0][:3], after(w_chunks[0][3], far_got[1]))])
        mine = got[0]
        got = flips(got.reshape(2, 2, half, 2, length), 0, 1)
        everyone = got.transpose(1, 2, 0, 3, 4).reshape(4 * TEAM, length)
    else:
        everyone = lax.all_gather(payload, EVERY, axis=0, tiled=False).reshape(-1, length)
        mine = lax.all_gather(payload, NEAR, axis=0, tiled=False).reshape(TEAM, length)
    tables = mine[members, piece:].astype(f32).astype(jnp.int32)
    first_table, live_table = tables[:, :BLK_DEV], tables[:, BLK_DEV:]
    vec_full = everyone[:, :piece].astype(f32).reshape(VEC)
    b_query, b_value, b_att, b_in, b_mlp, *norm_vectors = split_vectors(vec_full)
    gain_one, shift_one, gain_two, shift_two = (local_order(v)[None] for v in norm_vectors)
    slot = jnp.arange(slot_total, dtype=jnp.int32)
    position = slot[None, :] - BLOCK * jnp.repeat(first_table, BLOCK, axis=1)
    rotary = rotary_rows(position.reshape(team_slots).astype(f32))
    bias_q = lax.dynamic_slice(b_query, (me * HEAD,), (HEAD,))
    bias_v = lax.dynamic_slice(b_value, (me * HEAD,), (HEAD,))
    bias_qkv = jnp.concatenate([bias_q, jnp.zeros_like(bias_q), bias_v])[None]

    def bias_in(begin, end):
        return lax.dynamic_slice(b_in, (TEAM * begin + me * (end - begin),), (end - begin,))[None]

    attn_in, mlp_in, hat = norm_inputs(members, team, gain_one, shift_one, gain_two, shift_two)

    lefts_out, lefts_back, places_out, places_back, sums, terms = [], [], [], [], [], []

    def run_chunk(index, *waits):
        chunk = CHUNKS[index]
        ready = after(attn_in if chunk is None else mlp_in, *waits) if waits else (attn_in if chunk is None else mlp_in)
        if chunk is None:
            left_out, left_back, keep, send, total = attn_chunk(
                members, first_table, live_table, team, ready, w_chunks[index], bias_qkv, rotary, rows_dev
            )
            places_out.append((3 * HEAD, 4 * HEAD))
            places_back.append((0, 3 * HEAD))
        else:
            begin, end = chunk
            left_out, left_back, keep, send, total = mlp_chunk(
                members, team, ready, w_chunks[index], bias_in(begin, end), rows_dev
            )
            places_out.append((end - begin, 2 * (end - begin)))
            places_back.append((0, end - begin))
        lefts_out.append(left_out)
        lefts_back.append(left_back)
        sums.append(total[0])
        terms.append((keep, lax.ppermute(send, "col", SWAP) if paired else send))
        return total

    grouped, owned = [None] * count, [None] * count

    def sum_columns(index, *tokens):
        keep, got = terms[index]
        if not paired:
            term = jnp.concatenate([keep, got], axis=0)
            owned[index] = lax.psum_scatter(term, CROSS, scatter_dimension=0, tiled=True)
            return tokens[0]
        kept, sent = split_sum(after(keep, *tokens), got, 2)
        grouped[index] = (kept, lax.ppermute(sent, "far", SWAP))
        return kept

    def sum_far(index, *tokens, cost=2.5):
        if not paired:
            return tokens[0]
        kept, got = grouped[index]
        owned[index] = last_sum(after(kept, *tokens), got, 2, cost)
        return owned[index]

    def to_rows(index):
        term = owned[index]
        return lax.all_to_all(term.reshape(TEAM, rows_dev, term.shape[1]), NEAR, 0, 0, tiled=True)

    held = {}

    def update(index, got, *tokens):
        chunk = CHUNKS[index]
        got = after(got, *tokens)
        if chunk is None:
            held["qkv"] = adamw_columns(got, w_qkv, first_qkv, second_qkv, 0, HEAD, 0, 3, FENCE)
            held["att"] = adamw_columns(got, w_attn_out, first_attn_out, second_attn_out, 3, HEAD, 0, 1, 3)
            return held["att"][0]
        begin, end = chunk
        unit = end - begin
        for kind, name, arrays in ((0, "in", (w_mlp_in, first_mlp_in, second_mlp_in)), (1, "out", (w_mlp_out, first_mlp_out, second_mlp_out))):
            held[name] = adamw_columns(got, *arrays, kind, unit, begin // unit, 1, 4, held.get(name))
        return held["out"][0]

    token = run_chunk(0)
    cross(2, token)
    if paired:
        send_far(3, token)
    token = run_chunk(1, token, *far_got[2:3] if paired else ())
    cross(3, token)
    token = sum_columns(0, token)
    token = run_chunk(2, token, *far_got[3:4] if paired else ())
    token = sum_far(0, token)
    rows_zero = to_rows(0)
    token = run_chunk(3, token)
    token = sum_columns(1, token)
    attn_index = CHUNKS.index(None)
    lefts_back[0] = after(lefts_back[0], token, rows_zero)
    back_send, back_keep, norm_sums = back_part(
        hat, lefts_back, w_chunks, places_back, attn_index, gain_one, gain_two, rows_dev
    )
    lefts_out[0] = after(lefts_out[0], back_keep)
    out_send, out_keep = out_part(lefts_out, w_chunks, places_out, rows_dev)

    def own_step(pair, axis, steps, *tokens):
        kept, sent = pair
        return split_sum(after(kept, *tokens), lax.ppermute(sent, axis, SWAP), steps)

    alive = (jnp.arange(BLOCK, dtype=jnp.int32)[None, :] < block_live[:, None]).reshape(slot_total)
    seed_own = jnp.where(alive[:, None], cotangent, jnp.zeros_like(cotangent))
    seed_sum = jnp.sum(seed_own.astype(f32), axis=0)

    def place(values, width):
        return lax.dynamic_update_slice(jnp.zeros((width,), f32), values, (me * values.shape[0],))

    mlp_order = sorted((k for k in range(count) if CHUNKS[k] is not None), key=lambda k: CHUNKS[k][0])
    local_vec = jnp.concatenate(
        [
            place(sums[attn_index][:HEAD], D),
            place(sums[attn_index][2 * HEAD :], D),
            seed_sum,
            *[place(sums[k], TEAM * sums[k].shape[0]) for k in mlp_order],
            seed_sum,
            own_order(norm_sums[:4]).reshape(4 * D),
        ]
    )
    vec_terms = local_vec.reshape(far_size, half, 2, 2, piece).transpose(1, 3, 0, 2, 4).reshape(TEAM, groups, piece)
    vec_team = jnp.sum(lax.all_to_all(vec_terms, NEAR, 0, 0, tiled=True), axis=0)
    if paired:
        pick = lambda f, c: lax.dynamic_index_in_dim(vec_team, 2 * (far ^ f) + (column ^ c), 0, keepdims=False)
        grad_vectors = pick(0, 0) + lax.ppermute(pick(0, 1), "col", SWAP) + lax.ppermute(pick(1, 0), "far", SWAP)
        grad_vectors = grad_vectors + lax.ppermute(pick(1, 1), ("far", "col"), [(i, 3 - i) for i in range(4)])
    else:
        grad_vectors = jnp.sum(lax.all_to_all(vec_team, ("far", "col"), 0, 0, tiled=True), axis=0)
    new_vec, m_vec, u_vec = adamw_update(vectors, grad_vectors, first_vectors, second_vectors, vector_rate, 0.0)

    token = sum_columns(2, out_keep)
    token = sum_far(1, token, vec_team, cost=FENCE)
    rows_one = to_rows(1)
    back_pair = own_step((back_keep, back_send), "core", 4, token)
    out_pair = own_step((out_keep, out_send), "core", 4, back_pair[0])
    token = sum_columns(3, out_pair[0])
    token = update(0, rows_zero, token)
    token = update(1, rows_one, token)
    token = sum_far(2, token)
    rows_two = to_rows(2)
    back_pair = own_step(back_pair, "row", 2, token)
    out_pair = own_step(out_pair, "low", 2, back_pair[0])
    token = sum_far(3, out_pair[0])
    rows_three = to_rows(3)
    token = update(2, rows_two, token)
    ordered = (lambda v: v) if paired else own_order
    back_got = lax.ppermute(back_pair[1], "low", SWAP)
    out_got = lax.ppermute(out_pair[1], "row", SWAP)
    grad_tokens = finish_tokens(to_own, after(tokens, token), seed_own, ordered(back_pair[0]), ordered(back_got), True)
    bias_out = (b_att + b_mlp)[None]
    out = finish_tokens(
        to_own, after(tokens, grad_tokens), bias_out, ordered(out_pair[0]), ordered(out_got), False
    )
    update(3, rows_three, out)
    grad_qkv, new_qkv, m_qkv, u_qkv = held["qkv"]
    grad_attn_out, new_att, m_att, u_att = held["att"]
    grad_mlp_in, new_in, m_in, u_in = held["in"]
    grad_mlp_out, new_out, m_out, u_out = held["out"]
    return (
        out,
        grad_tokens,
        grad_qkv,
        grad_attn_out,
        grad_mlp_in,
        grad_mlp_out,
        grad_vectors,
        new_qkv,
        new_att,
        new_in,
        new_out,
        new_vec,
        m_qkv,
        u_qkv,
        m_att,
        u_att,
        m_in,
        u_in,
        m_out,
        u_out,
        m_vec,
        u_vec,
    )


def solution(mesh):
    devices = mesh.devices.reshape(-1)
    layout = Mesh(devices.reshape(devices.size // 16, 2, 2, 2, 2), EVERY)
    matrix, line = P(EVERY, None), P(EVERY)
    in_specs = (matrix, matrix, line, line) + (matrix,) * 4 + (line,) + (matrix,) * 8 + (line,) * 2
    out_specs = (matrix,) * 6 + (line,) + (matrix,) * 4 + (line,) + (matrix,) * 8 + (line,) * 2
    return jax.shard_map(body, mesh=layout, in_specs=in_specs, out_specs=out_specs, check_vma=False)
```

time: 806 us -> 609 us (0.76)
  Pallas kernels: 0 us -> 267 us
  matrix products: 188 us -> 0 us
  waiting for transfers between devices: 325 us -> 193 us
  blocking collectives: 125 us -> 0 us
  starting transfers between devices: 16 us -> 80.9 us
  other arithmetic: 65.4 us -> 20.5 us
  local copies, waits for them, and re-layouts: 64.3 us -> 26.6 us
    pallas_call x0 -> x30, Pallas kernels: none -> 267 us  [the longest x3 70.5 us: mlp_chunk(): pl.pallas_call(kernel, grid_spec=pltpu.PrefetchScalarGridSpec(num_scalar_...]
    dot_general x18 -> x0, matrix products: 188 us -> none  [the longest x12 174 us: dot(): return lax.dot_general(left, right, dims, preferred_element_type=f32)]
    reduce_scatter x4 -> x0, waiting for transfers between devices: 165 us -> none  [the longest x1 72.9 us: body(): lax.psum_scatter(part_out.astype(bf16), PLANE, scatter_dimension=0, tiled...]
    ppermute x0 -> x29, waiting for transfers between devices: none -> 148 us  [the longest x1 44.9 us: body(): far_got[0] = lax.ppermute(owns[0], 'far', SWAP)]
    all_gather x4 -> x1, waiting for transfers between devices: 141 us -> 0.01 us  [body(): team = lax.all_gather(both_send, NEAR, axis=0, tiled=False)]
    all_gather x2 -> x0, blocking collectives: 87.2 us -> none  [the longest x1 45.4 us: body(): lax.all_gather(jnp.stack([block_first, block_live]), PLANE, axis=0, tiled...]
    ppermute x0 -> x29, starting transfers between devices: none -> 38.9 us  [the longest x4 6.21 us: sum_columns(): grouped[index] = (kept, lax.ppermute(sent, 'far', SWAP))]
    all_to_all x2 -> x0, blocking collectives: 37.9 us -> none  [the longest x1 29.3 us: fetch(): got = lax.all_to_all(block, PLANE, 0, 0, tiled=True)]
  transfers between devices with their start and end apart: 12 -> 39, of which waited for: 8 -> 12; matrix products, arithmetic and copies ran while one was open for 36% -> 7% of each run, Pallas kernels for 0% -> 42%
where the time goes in v2:
time: 609 us; the launch traced here: 603 us
  Pallas kernels  267 us (44%)
  waiting for transfers between devices  193 us (32%)
  starting transfers between devices  80.9 us (13%)
  local copies, waits for them, and re-layouts  26.6 us (4%)
  other arithmetic  20.5 us (3%)
  between operations  15.1 us (2%)
    pallas_call x3, Pallas kernels, mlp_chunk(): pl.pallas_call(kernel, grid_spec=pltpu.PrefetchScalarGridSpec(num_scalar_...  70.5 us
    all_to_all x4, waiting for transfers between devices, body(): lax.all_to_all(after(block, *waits) if waits else block, NEAR, 0, 0, tile...  45.2 us
    ppermute x1, waiting for transfers between devices, body(): far_got[0] = lax.ppermute(owns[0], 'far', SWAP)  44.9 us
    pallas_call x8, Pallas kernels, adamw_columns(): pl.pallas_call(kernel, grid=(sections, rows // part), in_specs=[got_spec,...  39 us
    ppermute x1, waiting for transfers between devices, body(): lax.ppermute(pick(1, 0), 'far', SWAP)  38.1 us
    pallas_call x1, Pallas kernels, attn_chunk(): pl.pallas_call(kernel, grid_spec=pltpu.PrefetchScalarGridSpec(num_scalar_...  36.3 us
    pallas_call x8, Pallas kernels, split_sum(): pl.pallas_call(kernel, grid=(steps,), in_specs=[low, high, low, high], ou...  32.6 us
    pallas_call x1, Pallas kernels, back_part(): pl.pallas_call(kernel, grid=(TEAM,), in_specs=[ANYWHERE] * (count * per)...  32.4 us
  transfers between devices with their start and end apart: 39, of which 12 were waited for; matrix products, arithmetic and copies ran while one was open for 7% of the time, Pallas kernels for 42%

profile of v2, /device:TPU:0, one launch (start us, length us, event | category | flops | bytes accessed | tf_op | source)
XLA Modules:
  0.0 602.8 jit_solution(4280334053899758868)
XLA Ops:
  7.8 4.1 shard_map.363
  17.0 5.3 all-to-all-start
  25.5 3.5 reshape.164
  32.4 6.2 %all-to-all-done.refs_0_ = bf16[8,80,512]{2,1,0:T(8,128)(2,1)S(1)} async-done(((bf16[8,80,512]{2,1,0:T(8,128)(2,1)}), bf16[8,80,512]{2,1,0:T(8,128)(2,1)S(1)}, u32[]{:S(2)}, u32[]{:S(2)}) %all-to-all-start) | async-done | bytes 655392 | tf_op jit(solution)/shard_map/all_to_all | solution.py:672
  38.6 4.3 all-to-all-start.1
  49.6 44.9 %collective-permute-done.refs_1_ = bf16[8,80,512]{2,1,0:T(8,128)(2,1)S(1)} collective-permute-done((bf16[8,80,512]{2,1,0:T(8,128)(2,1)S(1)}, bf16[8,80,512]{2,1,0:T(8,128)(2,1)S(1)}, u32[]{:S(2)}, u32[]{:S(2)}) %collective-permute-start) | collective-permute-done | bytes 655392 | tf_op jit(solution)/shard_map/ppermute | solution.py:670
  94.5 7.2 %all-to-all-start.2 = ((bf16[8,64,1024]{2,1,0:T(8,128)(2,1)}), bf16[8,64,1024]{2,1,0:T(8,128)(2,1)}, u32[]{:S(2)}, u32[]{:S(2)}) async-start(bf16[8,64,1024]{2,1,0:T(8,128)(2,1)} %pad_maximum_fusion), calls=%async_computation.2 | async-start | bytes 2097152 | tf_op jit(solution)/shard_map/all_to_all | solution.py:672
  109.3 18.5 %all-to-all-done.2 = bf16[8,64,1024]{2,1,0:T(8,128)(2,1)} async-done(((bf16[8,64,1024]{2,1,0:T(8,128)(2,1)}), bf16[8,64,1024]{2,1,0:T(8,128)(2,1)}, u32[]{:S(2)}, u32[]{:S(2)}) %all-to-all-start.2) | async-done | bytes 1048608 | tf_op jit(solution)/shard_map/all_to_all | solution.py:672
  128.2 4.4 all-to-all-start.3
  132.5 5.8 fusion
  142.1 20.4 %all-to-all-done.3 = bf16[8,64,512]{2,1,0:T(8,128)(2,1)} async-done(((bf16[8,64,512]{2,1,0:T(8,128)(2,1)}), bf16[8,64,512]{2,1,0:T(8,128)(2,1)}, u32[]{:S(2)}, u32[]{:S(2)}) %all-to-all-start.3) | async-done | bytes 524320 | tf_op jit(solution)/shard_map/all_to_all | solution.py:672
  164.0 12.2 %collective-permute-done.1.refs_1_.refs_5_ = bf16[512,1024]{1,0:T(8,128)(2,1)} collective-permute-done((bf16[512,1024]{1,0:T(8,128)(2,1)}, bf16[512,1024]{1,0:T(8,128)(2,1)}, u32[]{:S(2)}, u32[]{:S(2)}) %collective-permute-start.1) | collective-permute-done | bytes 1048608 | tf_op jit(solution)/shard_map/ppermute | solution.py:685
  183.5 14.2 %shard_map.364 = (bf16[2048,2048]{1,0:T(8,128)(2,1)}, bf16[2048,2048]{1,0:T(8,128)(2,1)}, bf16[2048,2048]{1,0:T(8,128)(2,1)}) custom-call(s32[8]{0:T(128)} %get-tuple-element.280.members_ref, bf16[8,512,2048]{2,1,0:T(8,128)(2,1)} %bitcast.126, f32[1,2048]{1,0:T(1,128)} %bitcast.157, f32[1,2048]{1,0:T(1,128)} %bitcast.159, f32[1,2048]{1,0:T(1,128)} %bitcast.155, ...), custom_call_target="tpu_custom_call" | custom-call | flops 2300000075776 | bytes 1024 | tf_op jit(solution)/shard_map/pallas_call | solution.py:190
  197.8 19.9 %shard_map.365 = (bf16[2048,256]{1,0:T(8,128)(2,1)}, bf16[2048,256]{1,0:T(8,128)(2,1)}, bf16[1024,512]{1,0:T(8,128)(2,1)}, bf16[1024,512]{1,0:T(8,128)(2,1)}, f32[1,256]{1,0:T(1,128)}) custom-call(s32[8]{0:T(128)} %get-tuple-element.280.members_ref, bf16[8,512,2048]{2,1,0:T(8,128)(2,1)} %bitcast.127, bf16[8,80,512]{2,1,0:T(8,128)(2,1)} %copy-done.4, ...), custom_call_target="tpu_custom_call" | custom-call | flops 1724999936 | bytes 1024 | tf_op jit(solution)/shard_map/pallas_call | solution.py:280
  217.7 7.1 %collective-permute-done.2.refs_1_.refs_9_ = bf16[512,1024]{1,0:T(8,128)(2,1)} collective-permute-done((bf16[512,1024]{1,0:T(8,128)(2,1)}, bf16[512,1024]{1,0:T(8,128)(2,1)}, u32[]{:S(2)}, u32[]{:S(2)}) %collective-permute-start.2) | collective-permute-done | bytes 1048608 | tf_op jit(solution)/shard_map/ppermute | solution.py:685
  226.6 8.2 %collective-permute-done.8.refs_3_.refs_7_ = bf16[512,1024]{1,0:T(8,128)(2,1)} collective-permute-done((bf16[512,1024]{1,0:T(8,128)(2,1)}, bf16[512,1024]{1,0:T(8,128)(2,1)}, u32[]{:S(2)}, u32[]{:S(2)}) %collective-permute-start.8) | collective-permute-done | bytes 1048608 | tf_op jit(solution)/shard_map/ppermute | solution.py:691
  236.2 36.3 %shard_map.366 = (bf16[2048,256]{1,0:T(8,128)(2,1)}, bf16[2048,768]{1,0:T(8,128)(2,1)}, bf16[1024,1024]{1,0:T(8,128)(2,1)}, bf16[1024,1024]{1,0:T(8,128)(2,1)}, f32[1,768]{1,0:T(1,128)}) custom-call(s32[8]{0:T(128)} %get-tuple-element.280.members_ref, s32[8,2]{1,0:T(8,128)} %get-tuple-element.274.first_ref, s32[8,2]{1,0:T(8,128)} %get-tuple-element.273.live_ref, ...), custom_call_target="tpu_custom_call" | custom-call | flops 2300000075776 | bytes 1024 | tf_op jit(solution)/shard_map/pallas_call | solution.py:348
  278.5 2.9 collective-permute-start.13
  281.4 31.1 %shard_map.368 = (bf16[2048,512]{1,0:T(8,128)(2,1)}, bf16[2048,512]{1,0:T(8,128)(2,1)}, bf16[1024,1024]{1,0:T(8,128)(2,1)}, bf16[1024,1024]{1,0:T(8,128)(2,1)}, f32[1,512]{1,0:T(1,128)}) custom-call(s32[8]{0:T(128)} %get-tuple-element.280.members_ref, bf16[8,512,2048]{2,1,0:T(8,128)(2,1)} %bitcast.129, bf16[512,1024]{1,0:T(8,128)(2,1)} %bitcast.8.refs_0_.refs_8_, ...), custom_call_target="tpu_custom_call" | custom-call | flops 2300000075776 | bytes 1024 | tf_op jit(solution)/shard_map/pallas_call | solution.py:280
  314.7 4.4 all-to-all-start.4
  320.3 15.5 %collective-permute-done.12.refs_3_.refs_15_ = bf16[512,512]{1,0:T(8,128)(2,1)} collective-permute-done((bf16[512,512]{1,0:T(8,128)(2,1)}, bf16[512,512]{1,0:T(8,128)(2,1)}, u32[]{:S(2)}, u32[]{:S(2)}) %collective-permute-start.12) | collective-permute-done | bytes 524320 | tf_op jit(solution)/shard_map/ppermute | solution.py:691
  335.9 19.5 %shard_map.370 = (bf16[2048,256]{1,0:T(8,128)(2,1)}, bf16[2048,256]{1,0:T(8,128)(2,1)}, bf16[1024,512]{1,0:T(8,128)(2,1)}, bf16[1024,512]{1,0:T(8,128)(2,1)}, f32[1,256]{1,0:T(1,128)}) custom-call(s32[8]{0:T(128)} %get-tuple-element.280.members_ref, bf16[8,512,2048]{2,1,0:T(8,128)(2,1)} %bitcast.130, bf16[512,512]{1,0:T(8,128)(2,1)} %bitcast.11.refs_0_.refs_12_, ...), custom_call_target="tpu_custom_call" | custom-call | flops 1724999936 | bytes 1024 | tf_op jit(solution)/shard_map/pallas_call | solution.py:280
  356.4 3.5 shard_map.371
  362.5 32.4 %shard_map.372 = (bf16[1024,2048]{1,0:T(8,128)(2,1)}, bf16[1024,2048]{1,0:T(8,128)(2,1)}, f32[8,2048]{1,0:T(8,128)}) custom-call(bf16[8,80,512]{2,1,0:T(8,128)(2,1)} %copy-done.4, bf16[8,80,512]{2,1,0:T(8,128)(2,1)} %copy-done.11, bf16[8,80,512]{2,1,0:T(8,128)(2,1)} %copy-done.12, bf16[8,80,512]{2,1,0:T(8,128)(2,1)} %copy-done.13, ...), custom_call_target="tpu_custom_call" | custom-call | flops 2300000075776 | bytes 1024 | tf_op jit(solution)/shard_map/pallas_call | solution.py:470
  396.9 4.2 all-to-all-start.5
  401.1 19.2 %shard_map.373 = (bf16[1024,2048]{1,0:T(8,128)(2,1)}, bf16[1024,2048]{1,0:T(8,128)(2,1)}) custom-call(bf16[8,80,512]{2,1,0:T(8,128)(2,1)} %copy-done.4, bf16[8,80,512]{2,1,0:T(8,128)(2,1)} %copy-done.11, bf16[8,80,512]{2,1,0:T(8,128)(2,1)} %copy-done.12, bf16[8,80,512]{2,1,0:T(8,128)(2,1)} %copy-done.13, bf16[512,1024]{1,0:T(8,128)(2,1)} %bitcast.7.refs_0_.refs_4_, ...), custom_call_target="tpu_custom_call" | custom-call | flops 2184999936 | bytes 1024 | tf_op jit(solution)/shard_map/pallas_call | solution.py:424
  421.6 3.5 shard_map.374
  427.8 4.4 all-to-all-start.6
  433.9 6.3 %shard_map.376 = (f32[512,2048]{1,0:T(8,128)}, bf16[512,2048]{1,0:T(8,128)(2,1)}) custom-call(bf16[1024,2048]{1,0:T(8,128)(2,1)} %get-tuple-element.179.l_low.l_high, bf16[1024,2048]{1,0:T(8,128)(2,1)} %get-tuple-element.179.l_low.l_high, bf16[1024,2048]{1,0:T(8,128)(2,1)} %collective-permute-done.17.r_low.r_high, ...), custom_call_target="tpu_custom_call" | custom-call | flops 460000000 | bytes 1024 | tf_op jit(solution)/shard_map/pallas_call | solution.py:494
  442.3 6.3 %shard_map.377 = (f32[512,2048]{1,0:T(8,128)}, bf16[512,2048]{1,0:T(8,128)(2,1)}) custom-call(bf16[1024,2048]{1,0:T(8,128)(2,1)} %get-tuple-element.182.l_low.l_high, bf16[1024,2048]{1,0:T(8,128)(2,1)} %get-tuple-element.182.l_low.l_high, bf16[1024,2048]{1,0:T(8,128)(2,1)} %collective-permute-done.18.r_low.r_high, ...), custom_call_target="tpu_custom_call" | custom-call | flops 460000000 | bytes 1024 | tf_op jit(solution)/shard_map/pallas_call | solution.py:494
  450.1 8.0 %collective-permute-done.19.r_low.r_high = bf16[1024,512]{1,0:T(8,128)(2,1)S(1)} collective-permute-done((bf16[1024,512]{1,0:T(8,128)(2,1)}, bf16[1024,512]{1,0:T(8,128)(2,1)S(1)}, u32[]{:S(2)}, u32[]{:S(2)}) %collective-permute-start.19) | collective-permute-done | bytes 1048608 | tf_op jit(solution)/shard_map/ppermute | solution.py:751
  461.4 3.9 shard_map.379
  466.3 3.9 shard_map.380
  470.2 12.7 %collective-permute-done.20.r_ref = bf16[512,1024]{1,0:T(8,128)(2,1)} collective-permute-done((bf16[512,1024]{1,0:T(8,128)(2,1)}, bf16[512,1024]{1,0:T(8,128)(2,1)}, u32[]{:S(2)}, u32[]{:S(2)}) %collective-permute-start.20) | collective-permute-done | bytes 1048608 | tf_op jit(solution)/shard_map/ppermute | solution.py:763
  485.7 3.7 all-to-all-start.7
  496.6 38.1 %collective-permute-done.27 = f32[768]{0:T(1024)S(1)} collective-permute-done((f32[768]{0:T(1024)S(1)}, f32[768]{0:T(1024)S(1)}, u32[]{:S(2)}, u32[]{:S(2)}) %collective-permute-start.27) | collective-permute-done | bytes 3104 | tf_op jit(solution)/shard_map/ppermute | solution.py:838
  536.6 4.1 shard_map.382
  540.7 4.1 shard_map.383
  544.7 3.2 collective-permute-start.24
  551.5 4.1 all-to-all-start.8
  555.7 9.6 %shard_map.388 = (f32[64,6144]{1,0:T(8,128)}, f32[64,6144]{1,0:T(8,128)}, f32[64,6144]{1,0:T(8,128)}, f32[64,6144]{1,0:T(8,128)}) custom-call(bf16[8,64,1024]{2,1,0:T(8,128)(2,1)} %copy-done.9, f32[64,6144]{1,0:T(8,128)} %w_ref.11, f32[64,6144]{1,0:T(8,128)} %m_ref.11, f32[64,6144]{1,0:T(8,128)} %u_ref.11), custom_call_target="tpu_custom_call" | custom-call | flops 2300000075776 | bytes 1024 | tf_op jit(solution)/shard_map/pallas_call | solution.py:577
  565.2 3.9 shard_map.389
  569.2 4.9 shard_map.385
  574.1 4.9 shard_map.390
  579.0 4.9 shard_map.386
  584.0 3.9 shard_map.387
  587.9 3.9 shard_map.392
  591.8 3.9 shard_map.391
  (252 shorter events, 86.1 us)
Async XLA Ops:
  7.2 176.3 %all-gather.3.cloned.1.call-start = ((), (), s32[]{:S(2)}) async-start(), calls=%async_computation.9 | async-start | bytes 18874368 | tf_op jit(solution)/shard_map/all_gather | solution.py:679
  17.0 21.6 %all-to-all-start = ((bf16[8,80,512]{2,1,0:T(8,128)(2,1)}), bf16[8,80,512]{2,1,0:T(8,128)(2,1)S(1)}, u32[]{:S(2)}, u32[]{:S(2)}) async-start(bf16[8,80,512]{2,1,0:T(8,128)(2,1)} %pad_maximum_fusion.2), calls=%async_computation | async-start | bytes 1310720 | tf_op jit(solution)/shard_map/all_to_all | solution.py:672
  38.6 68.3 %copy-start.4 = (bf16[8,80,512]{2,1,0:T(8,128)(2,1)}, bf16[8,80,512]{2,1,0:T(8,128)(2,1)S(1)}, u32[]{:S(2)}) copy-start(bf16[8,80,512]{2,1,0:T(8,128)(2,1)S(1)} %all-to-all-done.refs_0_) | copy-start | bytes 1966084
  38.6 55.9 %all-to-all-start.1 = ((bf16[8,64,1024]{2,1,0:T(8,128)(2,1)}), bf16[8,64,1024]{2,1,0:T(8,128)(2,1)}, u32[]{:S(2)}, u32[]{:S(2)}) async-start(bf16[8,64,1024]{2,1,0:T(8,128)(2,1)} %pad_maximum_fusion.1), calls=%async_computation.1 | async-start | bytes 2097152 | tf_op jit(solution)/shard_map/all_to_all | solution.py:672
  45.0 56.8 %copy-start.6 = (bf16[256,2048]{1,0:T(8,128)(2,1)S(1)}, bf16[256,2048]{1,0:T(8,128)(2,1)}, u32[]{:S(2)}) copy-start(bf16[256,2048]{1,0:T(8,128)(2,1)} %y_ref.1) | copy-start | bytes 3145732
  46.2 48.3 %collective-permute-start = (bf16[8,80,512]{2,1,0:T(8,128)(2,1)S(1)}, bf16[8,80,512]{2,1,0:T(8,128)(2,1)S(1)}, u32[]{:S(2)}, u32[]{:S(2)}) collective-permute-start(bf16[8,80,512]{2,1,0:T(8,128)(2,1)S(1)} %all-to-all-done.refs_0_), channel_id=1, source_target_pairs={{0,16},{16,0},{1,17},{17,1},{2,18},{18,2},{3,19},{19,3},{4,20},{20... | collective-permute-start | bytes 1966088 | tf_op jit(solution)/shard_map/ppermute | solution.py:670
  94.5 43.9 %copy-start.11 = (bf16[8,80,512]{2,1,0:T(8,128)(2,1)}, bf16[8,80,512]{2,1,0:T(8,128)(2,1)S(1)}, u32[]{:S(2)}) copy-start(bf16[8,80,512]{2,1,0:T(8,128)(2,1)S(1)} %collective-permute-done.refs_1_) | copy-start | bytes 1966084
  94.5 33.4 %all-to-all-start.2 = ((bf16[8,64,1024]{2,1,0:T(8,128)(2,1)}), bf16[8,64,1024]{2,1,0:T(8,128)(2,1)}, u32[]{:S(2)}, u32[]{:S(2)}) async-start(bf16[8,64,1024]{2,1,0:T(8,128)(2,1)} %pad_maximum_fusion), calls=%async_computation.2 | async-start | bytes 2097152 | tf_op jit(solution)/shard_map/all_to_all | solution.py:672
  106.9 33.0 %collective-permute-start.4 = (bf16[8,80,512]{2,1,0:T(8,128)(2,1)S(1)}, bf16[8,80,512]{2,1,0:T(8,128)(2,1)S(1)}, u32[]{:S(2)}, u32[]{:S(2)}) collective-permute-start(bf16[8,80,512]{2,1,0:T(8,128)(2,1)S(1)} %all-to-all-done.refs_0_), channel_id=1, source_target_pairs={{0,2},{2,0},{1,3},{3,1},{4,6},{6,4},{5,7},{7,5},{8,10},{10,8},{9,1... | collective-permute-start | bytes 1966088 | tf_op jit(solution)/shard_map/ppermute | solution.py:695
  127.9 48.3 %collective-permute-start.1 = (bf16[512,1024]{1,0:T(8,128)(2,1)}, bf16[512,1024]{1,0:T(8,128)(2,1)}, u32[]{:S(2)}, u32[]{:S(2)}) collective-permute-start(bf16[512,1024]{1,0:T(8,128)(2,1)} %bitcast.7.refs_0_.refs_4_), channel_id=1, source_target_pairs={{0,16},{16,0},{1,17},{17,1},{2,18},{18,2},{3,19},{19,3},{4,20},{20... | collective-permute-start | bytes 3145736 | tf_op jit(solution)/shard_map/ppermute | solution.py:685
  128.2 34.4 %all-to-all-start.3 = ((bf16[8,64,512]{2,1,0:T(8,128)(2,1)}), bf16[8,64,512]{2,1,0:T(8,128)(2,1)}, u32[]{:S(2)}, u32[]{:S(2)}) async-start(bf16[8,64,512]{2,1,0:T(8,128)(2,1)} %pad_maximum_fusion.3), calls=%async_computation.3 | async-start | bytes 1048576 | tf_op jit(solution)/shard_map/all_to_all | solution.py:672
  138.4 25.6 %collective-permute-start.5 = (bf16[8,80,512]{2,1,0:T(8,128)(2,1)S(1)}, bf16[8,80,512]{2,1,0:T(8,128)(2,1)S(1)}, u32[]{:S(2)}, u32[]{:S(2)}) collective-permute-start(bf16[8,80,512]{2,1,0:T(8,128)(2,1)S(1)} %collective-permute-done.refs_1_), channel_id=1, source_target_pairs={{0,2},{2,0},{1,3},{3,1},{4,6},{6,4},{5,7},{7,5},{8,10},{10,8},{9,1... | collective-permute-start | bytes 1966088 | tf_op jit(solution)/shard_map/ppermute | solution.py:691
  139.9 57.8 %copy-start.12 = (bf16[8,80,512]{2,1,0:T(8,128)(2,1)}, bf16[8,80,512]{2,1,0:T(8,128)(2,1)S(1)}, u32[]{:S(2)}) copy-start(bf16[8,80,512]{2,1,0:T(8,128)(2,1)S(1)} %collective-permute-done.4.refs_2_) | copy-start | bytes 1966084
  140.0 84.7 %collective-permute-start.7 = (bf16[512,1024]{1,0:T(8,128)(2,1)}, bf16[512,1024]{1,0:T(8,128)(2,1)}, u32[]{:S(2)}, u32[]{:S(2)}) collective-permute-start(bf16[512,1024]{1,0:T(8,128)(2,1)} %bitcast.7.refs_0_.refs_4_), channel_id=1, source_target_pairs={{0,2},{2,0},{1,3},{3,1},{4,6},{6,4},{5,7},{7,5},{8,10},{10,8},{9,1... | collective-permute-start | bytes 3145736 | tf_op jit(solution)/shard_map/ppermute | solution.py:695
  140.7 137.8 %collective-permute-start.3 = (bf16[512,1024]{1,0:T(8,128)(2,1)}, bf16[512,1024]{1,0:T(8,128)(2,1)}, u32[]{:S(2)}, u32[]{:S(2)}) collective-permute-start(bf16[512,1024]{1,0:T(8,128)(2,1)} %bitcast.8.refs_0_.refs_8_), channel_id=1, source_target_pairs={{0,2},{2,0},{1,3},{3,1},{4,6},{6,4},{5,7},{7,5},{8,10},{10,8},{9,1... | collective-permute-start | bytes 3145736 | tf_op jit(solution)/shard_map/ppermute | solution.py:695
  162.5 157.8 %collective-permute-start.11 = (bf16[512,512]{1,0:T(8,128)(2,1)}, bf16[512,512]{1,0:T(8,128)(2,1)}, u32[]{:S(2)}, u32[]{:S(2)}) collective-permute-start(bf16[512,512]{1,0:T(8,128)(2,1)} %bitcast.11.refs_0_.refs_12_), channel_id=1, source_target_pairs={{0,2},{2,0},{1,3},{3,1},{4,6},{6,4},{5,7},{7,5},{8,10},{10,8},{9,1... | collective-permute-start | bytes 1572872 | tf_op jit(solution)/shard_map/ppermute | solution.py:695
  164.0 33.8 %copy-start.13 = (bf16[8,80,512]{2,1,0:T(8,128)(2,1)}, bf16[8,80,512]{2,1,0:T(8,128)(2,1)S(1)}, u32[]{:S(2)}) copy-start(bf16[8,80,512]{2,1,0:T(8,128)(2,1)S(1)} %collective-permute-done.5.refs_3_) | copy-start | bytes 1966084
  179.3 45.5 %collective-permute-start.2 = (bf16[512,1024]{1,0:T(8,128)(2,1)}, bf16[512,1024]{1,0:T(8,128)(2,1)}, u32[]{:S(2)}, u32[]{:S(2)}) collective-permute-start(bf16[512,1024]{1,0:T(8,128)(2,1)} %bitcast.8.refs_0_.refs_8_), channel_id=1, source_target_pairs={{0,16},{16,0},{1,17},{17,1},{2,18},{18,2},{3,19},{19,3},{4,20},{20... | collective-permute-start | bytes 3145736 | tf_op jit(solution)/shard_map/ppermute | solution.py:685
  181.3 53.5 %collective-permute-start.8 = (bf16[512,1024]{1,0:T(8,128)(2,1)}, bf16[512,1024]{1,0:T(8,128)(2,1)}, u32[]{:S(2)}, u32[]{:S(2)}) collective-permute-start(bf16[512,1024]{1,0:T(8,128)(2,1)} %collective-permute-done.1.refs_1_.refs_5_), channel_id=1, source_target_pairs={{0,2},{2,0},{1,3},{3,1},{4,6},{6,4},{5,7},{7,5},{8,10},{10,8},{9,1... | collective-permute-start | bytes 3145736 | tf_op jit(solution)/shard_map/ppermute | solution.py:691
  224.7 49.2 %collective-permute-start.10 = (bf16[512,512]{1,0:T(8,128)(2,1)}, bf16[512,512]{1,0:T(8,128)(2,1)}, u32[]{:S(2)}, u32[]{:S(2)}) collective-permute-start(bf16[512,512]{1,0:T(8,128)(2,1)} %bitcast.11.refs_0_.refs_12_), channel_id=1, source_target_pairs={{0,16},{16,0},{1,17},{17,1},{2,18},{18,2},{3,19},{19,3},{4,20},{20... | collective-permute-start | bytes 1572872 | tf_op jit(solution)/shard_map/ppermute | solution.py:685
  224.8 49.9 %collective-permute-start.9 = (bf16[1024,512]{1,0:T(8,128)(2,1)}, bf16[1024,512]{1,0:T(8,128)(2,1)}, u32[]{:S(2)}, u32[]{:S(2)}) collective-permute-start(bf16[1024,512]{1,0:T(8,128)(2,1)} %get-tuple-element.144), channel_id=1, source_target_pairs={{0,2},{2,0},{1,3},{3,1},{4,6},{6,4},{5,7},{7,5},{8,10},{10,8},{9,1... | collective-permute-start | bytes 3145736 | tf_op jit(solution)/shard_map/ppermute | solution.py:751
  234.8 46.6 %collective-permute-start.6 = (bf16[512,1024]{1,0:T(8,128)(2,1)}, bf16[512,1024]{1,0:T(8,128)(2,1)}, u32[]{:S(2)}, u32[]{:S(2)}) collective-permute-start(bf16[512,1024]{1,0:T(8,128)(2,1)} %collective-permute-done.2.refs_1_.refs_9_), channel_id=1, source_target_pairs={{0,2},{2,0},{1,3},{3,1},{4,6},{6,4},{5,7},{7,5},{8,10},{10,8},{9,1... | collective-permute-start | bytes 3145736 | tf_op jit(solution)/shard_map/ppermute | solution.py:691
  274.0 82.4 %collective-permute-start.14 = (bf16[1024,1024]{1,0:T(8,128)(2,1)}, bf16[1024,1024]{1,0:T(8,128)(2,1)}, u32[]{:S(2)}, u32[]{:S(2)}) collective-permute-start(bf16[1024,1024]{1,0:T(8,128)(2,1)} %get-tuple-element.159), channel_id=1, source_target_pairs={{0,2},{2,0},{1,3},{3,1},{4,6},{6,4},{5,7},{7,5},{8,10},{10,8},{9,1... | collective-permute-start | bytes 6291464 | tf_op jit(solution)/shard_map/ppermute | solution.py:751
  274.6 61.3 %collective-permute-start.12 = (bf16[512,512]{1,0:T(8,128)(2,1)}, bf16[512,512]{1,0:T(8,128)(2,1)}, u32[]{:S(2)}, u32[]{:S(2)}) collective-permute-start(bf16[512,512]{1,0:T(8,128)(2,1)} %collective-permute-done.10.refs_1_.refs_13_), channel_id=1, source_target_pairs={{0,2},{2,0},{1,3},{3,1},{4,6},{6,4},{5,7},{7,5},{8,10},{10,8},{9,1... | collective-permute-start | bytes 1572872 | tf_op jit(solution)/shard_map/ppermute | solution.py:691
  278.5 34.0 %collective-permute-start.13 = (bf16[512,512]{1,0:T(8,128)(2,1)}, bf16[512,512]{1,0:T(8,128)(2,1)}, u32[]{:S(2)}, u32[]{:S(2)}) collective-permute-start(bf16[512,512]{1,0:T(8,128)(2,1)} %get-tuple-element.155), channel_id=1, source_target_pairs={{0,16},{16,0},{1,17},{17,1},{2,18},{18,2},{3,19},{19,3},{4,20},{20... | collective-permute-start | bytes 1572872 | tf_op jit(solution)/shard_map/ppermute | solution.py:763
  314.7 47.9 %all-to-all-start.4 = ((bf16[8,64,512]{2,1,0:T(8,128)(2,1)}), bf16[8,64,512]{2,1,0:T(8,128)(2,1)S(1)}, u32[]{:S(2)}, u32[]{:S(2)}) async-start(bf16[8,64,512]{2,1,0:T(8,128)(2,1)} %bitcast.137), calls=%async_computation.4 | async-start | bytes 1048576 | tf_op jit(solution)/shard_map/all_to_all | solution.py:775
  319.7 101.9 %collective-permute-start.15 = (bf16[1024,1024]{1,0:T(8,128)(2,1)}, bf16[1024,1024]{1,0:T(8,128)(2,1)}, u32[]{:S(2)}, u32[]{:S(2)}) collective-permute-start(bf16[1024,1024]{1,0:T(8,128)(2,1)} %get-tuple-element.173), channel_id=1, source_target_pairs={{0,2},{2,0},{1,3},{3,1},{4,6},{6,4},{5,7},{7,5},{8,10},{10,8},{9,1... | collective-permute-start | bytes 6291464 | tf_op jit(solution)/shard_map/ppermute | solution.py:751
  359.8 65.2 %collective-permute-start.16 = (bf16[512,1024]{1,0:T(8,128)(2,1)}, bf16[512,1024]{1,0:T(8,128)(2,1)}, u32[]{:S(2)}, u32[]{:S(2)}) collective-permute-start(bf16[512,1024]{1,0:T(8,128)(2,1)} %get-tuple-element.177), channel_id=1, source_target_pairs={{0,16},{16,0},{1,17},{17,1},{2,18},{18,2},{3,19},{19,3},{4,20},{20... | collective-permute-start | bytes 3145736 | tf_op jit(solution)/shard_map/ppermute | solution.py:763
  362.5 33.5 %copy-start.15 = (f32[24576]{0:T(1024)S(1)}, f32[24576]{0:T(1024)}, u32[]{:S(2)}) copy-start(f32[24576]{0:T(1024)} %copy-done.14) | copy-start | bytes 294916
  396.9 24.1 %all-to-all-start.5 = ((f32[8,4,768]{2,1,0:T(4,128)}), f32[8,4,768]{2,1,0:T(4,128)S(1)}, u32[]{:S(2)}, u32[]{:S(2)}) async-start(f32[8,4,768]{2,1,0:T(4,128)} %reshape.211), calls=%async_computation.5 | async-start | bytes 196608 | tf_op jit(solution)/shard_map/all_to_all | solution.py:835
  420.3 13.6 %collective-permute-start.17 = (bf16[1024,2048]{1,0:T(8,128)(2,1)}, bf16[1024,2048]{1,0:T(8,128)(2,1)}, u32[]{:S(2)}, u32[]{:S(2)}) collective-permute-start(bf16[1024,2048]{1,0:T(8,128)(2,1)} %get-tuple-element.180), channel_id=1, source_target_pairs={{0,1},{1,0},{2,3},{3,2},{4,5},{5,4},{6,7},{7,6},{8,9},{9,8},{10,11... | collective-permute-start | bytes 12582920 | tf_op jit(solution)/shard_map/ppermute | solution.py:814
  420.9 21.4 %collective-permute-start.18 = (bf16[1024,2048]{1,0:T(8,128)(2,1)}, bf16[1024,2048]{1,0:T(8,128)(2,1)}, u32[]{:S(2)}, u32[]{:S(2)}) collective-permute-start(bf16[1024,2048]{1,0:T(8,128)(2,1)} %get-tuple-element.183), channel_id=1, source_target_pairs={{0,1},{1,0},{2,3},{3,2},{4,5},{5,4},{6,7},{7,6},{8,9},{9,8},{10,11... | collective-permute-start | bytes 12582920 | tf_op jit(solution)/shard_map/ppermute | solution.py:814
  427.8 37.6 %all-to-all-start.6 = ((bf16[8,64,1024]{2,1,0:T(8,128)(2,1)}), bf16[8,64,1024]{2,1,0:T(8,128)(2,1)S(1)}, u32[]{:S(2)}, u32[]{:S(2)}) async-start(bf16[8,64,1024]{2,1,0:T(8,128)(2,1)} %bitcast.140), calls=%async_computation.6 | async-start | bytes 2097152 | tf_op jit(solution)/shard_map/all_to_all | solution.py:775
  432.2 25.8 %collective-permute-start.19 = (bf16[1024,512]{1,0:T(8,128)(2,1)}, bf16[1024,512]{1,0:T(8,128)(2,1)S(1)}, u32[]{:S(2)}, u32[]{:S(2)}) collective-permute-start(bf16[1024,512]{1,0:T(8,128)(2,1)} %get-tuple-element.186), channel_id=1, source_target_pairs={{0,2},{2,0},{1,3},{3,1},{4,6},{6,4},{5,7},{7,5},{8,10},{10,8},{9,1... | collective-permute-start | bytes 3145736 | tf_op jit(solution)/shard_map/ppermute | solution.py:751
  433.8 49.1 %collective-permute-start.20 = (bf16[512,1024]{1,0:T(8,128)(2,1)}, bf16[512,1024]{1,0:T(8,128)(2,1)}, u32[]{:S(2)}, u32[]{:S(2)}) collective-permute-start(bf16[512,1024]{1,0:T(8,128)(2,1)} %get-tuple-element.193), channel_id=1, source_target_pairs={{0,16},{16,0},{1,17},{17,1},{2,18},{18,2},{3,19},{19,3},{4,20},{20... | collective-permute-start | bytes 3145736 | tf_op jit(solution)/shard_map/ppermute | solution.py:763
  440.3 95.0 %collective-permute-start.21 = (bf16[512,2048]{1,0:T(8,128)(2,1)}, bf16[512,2048]{1,0:T(8,128)(2,1)S(1)}, u32[]{:S(2)}, u32[]{:S(2)}) collective-permute-start(bf16[512,2048]{1,0:T(8,128)(2,1)} %get-tuple-element.195), channel_id=1, source_target_pairs={{0,4},{4,0},{1,5},{5,1},{2,6},{6,2},{3,7},{7,3},{8,12},{12,8},{9,1... | collective-permute-start | bytes 6291464 | tf_op jit(solution)/shard_map/ppermute | solution.py:814
  448.6 92.1 %collective-permute-start.22 = (bf16[512,2048]{1,0:T(8,128)(2,1)}, bf16[512,2048]{1,0:T(8,128)(2,1)}, u32[]{:S(2)}, u32[]{:S(2)}) collective-permute-start(bf16[512,2048]{1,0:T(8,128)(2,1)} %get-tuple-element.198), channel_id=1, source_target_pairs={{0,8},{8,0},{1,9},{9,1},{2,10},{10,2},{3,11},{11,3},{4,12},{12,4},... | collective-permute-start | bytes 6291464 | tf_op jit(solution)/shard_map/ppermute | solution.py:814
  485.7 48.9 %copy-start.21 = (f32[768]{0:T(1024)S(1)}, f32[768]{0:T(1024)}, u32[]{:S(2)}) copy-start(f32[768]{0:T(1024)} %param.28) | copy-start | bytes 9220
  485.7 48.9 %copy-start.23 = (f32[768]{0:T(1024)S(1)}, f32[768]{0:T(1024)}, u32[]{:S(2)}) copy-start(f32[768]{0:T(1024)} %param.37) | copy-start | bytes 9220
  485.7 48.9 %copy-start.24 = (f32[768]{0:T(1024)S(1)}, f32[768]{0:T(1024)}, u32[]{:S(2)}) copy-start(f32[768]{0:T(1024)} %param.38) | copy-start | bytes 9220
  485.7 65.8 %all-to-all-start.7 = ((bf16[8,64,1024]{2,1,0:T(8,128)(2,1)}), bf16[8,64,1024]{2,1,0:T(8,128)(2,1)S(1)}, u32[]{:S(2)}, u32[]{:S(2)}) async-start(bf16[8,64,1024]{2,1,0:T(8,128)(2,1)} %bitcast.134), calls=%async_computation.7 | async-start | bytes 2097152 | tf_op jit(solution)/shard_map/all_to_all | solution.py:775
  489.4 60.0 %collective-permute-start.23 = (bf16[512,512]{1,0:T(8,128)(2,1)}, bf16[512,512]{1,0:T(8,128)(2,1)}, u32[]{:S(2)}, u32[]{:S(2)}) collective-permute-start(bf16[512,512]{1,0:T(8,128)(2,1)} %get-tuple-element.201), channel_id=1, source_target_pairs={{0,16},{16,0},{1,17},{17,1},{2,18},{18,2},{3,19},{19,3},{4,20},{20... | collective-permute-start | bytes 1572872 | tf_op jit(solution)/shard_map/ppermute | solution.py:763
  490.0 3.7 collective-permute-start.26
  490.5 44.1 %collective-permute-start.27 = (f32[768]{0:T(1024)S(1)}, f32[768]{0:T(1024)S(1)}, u32[]{:S(2)}, u32[]{:S(2)}) collective-permute-start(f32[768]{0:T(1024)S(1)} %get-tuple-element.240), channel_id=1, source_target_pairs={{0,16},{16,0},{1,17},{17,1},{2,18},{18,2},{3,19},{19,3},{4,20},{20... | collective-permute-start | bytes 9224 | tf_op jit(solution)/shard_map/ppermute | solution.py:838
  493.7 40.9 %collective-permute-start.28 = (f32[768]{0:T(1024)S(1)}, f32[768]{0:T(1024)S(1)}, u32[]{:S(2)}, u32[]{:S(2)}) collective-permute-start(f32[768]{0:T(1024)S(1)} %get-tuple-element.239), channel_id=1, source_target_pairs={{0,18},{2,16},{16,2},{18,0},{1,19},{3,17},{17,3},{19,1},{4,22},{6,... | collective-permute-start | bytes 9224 | tf_op jit(solution)/shard_map/ppermute | solution.py:839
  544.7 34.3 %collective-permute-start.24 = (bf16[256,2048]{1,0:T(8,128)(2,1)}, bf16[256,2048]{1,0:T(8,128)(2,1)}, u32[]{:S(2)}, u32[]{:S(2)}) collective-permute-start(bf16[256,2048]{1,0:T(8,128)(2,1)} %get-tuple-element.208), channel_id=1, source_target_pairs={{0,8},{8,0},{1,9},{9,1},{2,10},{10,2},{3,11},{11,3},{4,12},{12,4},... | collective-permute-start | bytes 3145736 | tf_op jit(solution)/shard_map/ppermute | solution.py:860
  547.9 36.0 %collective-permute-start.25 = (bf16[256,2048]{1,0:T(8,128)(2,1)}, bf16[256,2048]{1,0:T(8,128)(2,1)}, u32[]{:S(2)}, u32[]{:S(2)}) collective-permute-start(bf16[256,2048]{1,0:T(8,128)(2,1)} %get-tuple-element.210), channel_id=1, source_target_pairs={{0,4},{4,0},{1,5},{5,1},{2,6},{6,2},{3,7},{7,3},{8,12},{12,8},{9,1... | collective-permute-start | bytes 3145736 | tf_op jit(solution)/shard_map/ppermute | solution.py:861
  551.5 36.4 %all-to-all-start.8 = ((bf16[8,64,512]{2,1,0:T(8,128)(2,1)}), bf16[8,64,512]{2,1,0:T(8,128)(2,1)}, u32[]{:S(2)}, u32[]{:S(2)}) async-start(bf16[8,64,512]{2,1,0:T(8,128)(2,1)} %bitcast.138), calls=%async_computation.8 | async-start | bytes 1048576 | tf_op jit(solution)/shard_map/all_to_all | solution.py:775
  (24 other events, 171.0 us)
Sparse Core Ops, SparseCore 0:
  12.0 136.9 all-gather.2

commit v3 on v2

--- a/solution.py
+++ b/solution.py
@@ -17,8 +17,8 @@
 TEAM = 8
 SLICE_FF = FF // TEAM
 CHUNKS = ((0, 256), None, (512, 1024), (256, 512))
+LOADS = ((0,), (1,), (2, 3))
 PACK_ROWS = 16
-FENCE = 20000
 LANES = 128
 
 eps_norm = 1e-05
@@ -39,7 +39,51 @@
 CROSS = ("col", "far")
 EVERY = ("far", "low", "row", "col", "core")
 SWAP = [(0, 1), (1, 0)]
-COST_UNIT = 115000000
+COST = {
+    'norm': 100,
+    'mlp1024': 20000,
+    'attn': 300,
+    'back': 10,
+    'far0': 20000,
+    'adam1': 90,
+    'adam0in': 40,
+    'adam0out': 10,
+    'adam1b': 40,
+    'out': 190,
+    'mlp512': 150,
+    'rows': 20000,
+    'back_row': 300,
+    'prep': 300,
+    'far2': 30,
+    'col1': 100,
+    'fin': 30,
+    'col0': 10,
+    'back_core': 10,
+}
+ORDER = (
+    'K0',
+    'K1',
+    'C0',
+    'K2',
+    'K3',
+    'C1',
+    'O',
+    'B',
+    'C3',
+    'F0',
+    'O1',
+    'B1',
+    'C2',
+    'F2',
+    'B2',
+    'A1',
+    'A0',
+    'O2',
+    'A2',
+    'A3',
+    'O3',
+    'B3',
+)
 ANYWHERE = pl.BlockSpec(memory_space=pl.ANY)
 
 
@@ -51,10 +95,10 @@
     return lax.optimization_barrier((value, *others))[0]
 
 
-def params(cost):
+def params(role):
     return dict(
         compiler_params=pltpu.CompilerParams(vmem_limit_bytes=VMEM_BYTES),
-        cost_estimate=pl.CostEstimate(flops=int(cost * COST_UNIT), bytes_accessed=1024, transcendentals=0),
+        cost_estimate=pl.CostEstimate(flops=int(COST.get(role, 1) * 1e8), bytes_accessed=1024, transcendentals=0),
     )
 
 
@@ -122,6 +166,24 @@
     return sum(1 if piece.ndim == 2 else piece.shape[0] for piece in pieces)
 
 
+def extra_rows(pieces, rows_dev):
+    count, (members, rows, width) = len(pieces), pieces[0].shape
+    more = rows - rows_dev
+
+    def kernel(*refs):
+        for k in range(count):
+            refs[-1][k] = refs[k][...]
+
+    return pl.pallas_call(
+        kernel,
+        grid=(1,),
+        in_specs=[blocks((members, more, width), lambda i: (0, rows_dev // more, 0))] * count,
+        out_specs=blocks((count, members, more, width), lambda i: (0, 0, 0, 0)),
+        out_shape=shaped((count, members, more, width), bf16),
+        **params("rows"),
+    )(*pieces)
+
+
 def member_copies(members_ref, team_ref, kind, buffer, sems):
     count, both, _ = team_ref.shape
     rows = both // 2
@@ -158,7 +220,7 @@
             out_specs=blocks((2 * slots, D), lambda i, *_: (0, 0)),
         ),
         out_shape=shaped((2 * slots, D), bf16),
-        **params(4),
+        **params("prep"),
     )(order, live, tokens, cotangent)
 
 
@@ -197,13 +259,13 @@
             scratch_shapes=[pltpu.VMEM((count * rows, D), bf16), pltpu.SemaphoreType.DMA((count,))],
         ),
         out_shape=[shaped((count * rows, D), bf16)] * 3,
-        **params(FENCE),
+        **params("norm"),
     )(members, team, gain_one, shift_one, gain_two, shift_two)
 
 
-def open_chunk(step, rows, rows_dev, members_ref, team_ref, w_refs, y_all, w_all, y_sems, w_sems):
+def open_chunk(step, rows, rows_dev, members_ref, team_ref, w_refs, begin, y_all, w_all, y_sems, w_sems):
     y_copies = member_copies(members_ref, team_ref, 1, y_all, y_sems)
-    w_copies = stacked_copies(w_refs, w_all, w_sems, rows_dev)
+    w_copies = stacked_copies(w_refs, w_all, w_sems, rows_dev, slice(begin, begin + w_all.shape[1]))
     slots = team_ref.shape[1] // 2
 
     @pl.when(step == 0)
@@ -255,16 +317,16 @@
     ]
 
 
-def mlp_chunk(members, team, a, w_pieces, b, rows_dev, rows=512):
-    total, width = a.shape[0], w_pieces[0].shape[-1]
-    cols = width // 2
+def mlp_chunk(members, team, a, w_pieces, begin, b, rows_dev, rows=512):
+    total, cols = a.shape[0], b.shape[1]
+    width = 2 * cols
     nw = len(w_pieces)
 
     def kernel(members_ref, team_ref, *refs):
         w_refs = refs[:nw]
         a_ref, b_ref, act_ref, dh_ref, keep_ref, send_ref, sum_ref, acc_ref, y_all, w_all, y_sems, w_sems = refs[nw:]
         step, last = pl.program_id(0), pl.num_programs(0) - 1
-        y = open_chunk(step, rows, rows_dev, members_ref, team_ref, w_refs, y_all, w_all, y_sems, w_sems)
+        y = open_chunk(step, rows, rows_dev, members_ref, team_ref, w_refs, begin, y_all, w_all, y_sems, w_sems)
         a = a_ref[...]
         act, slope = gelu_pair(dot(a, w_all[:, :cols]) + b_ref[...])
         act = act.astype(bf16)
@@ -287,7 +349,7 @@
             scratch_shapes=chunk_scratch(total, width, team.shape[0], copy_count(w_pieces)),
         ),
         out_shape=[shaped((total, cols), bf16)] * 2 + [shaped((D // 2, width), bf16)] * 2 + [shaped((1, cols), f32)],
-        **params(FENCE if width > D // 4 else 15),
+        **params(f"mlp{width}"),
     )(members, team, *w_pieces, a, b)
 
 
@@ -297,8 +359,8 @@
     return jnp.concatenate([part, values[:, LANES:]], axis=1)
 
 
-def attn_chunk(members, first, live, team, a, w_pieces, b, rotary, rows_dev, rows=512):
-    total, width = a.shape[0], w_pieces[0].shape[-1]
+def attn_chunk(members, first, live, team, a, w_pieces, begin, b, rotary, rows_dev, rows=512):
+    total, width = a.shape[0], 4 * HEAD
     nw = len(w_pieces)
     slots = BLK_DEV * BLOCK
     buffers = rows // slots
@@ -308,7 +370,7 @@
         a_ref, b_ref, cos_ref, low_ref, high_ref, att_ref, dm_ref, keep_ref, send_ref, sum_ref = refs[nw : nw + 10]
         acc_ref, y_all, w_all, y_sems, w_sems = refs[nw + 10 :]
         step, last = pl.program_id(0), pl.num_programs(0) - 1
-        y = open_chunk(step, rows, rows_dev, members_ref, team_ref, w_refs, y_all, w_all, y_sems, w_sems)
+        y = open_chunk(step, rows, rows_dev, members_ref, team_ref, w_refs, begin, y_all, w_all, y_sems, w_sems)
         a = a_ref[...]
         mixed = dot(a, w_all[:, : 3 * HEAD]) + b_ref[...]
         datt_all = dot(y, w_all[:, 3 * HEAD :]).astype(bf16)
@@ -317,7 +379,12 @@
         for k in range(buffers):
             buf = step * buffers + k
             part = slice(k * slots, (k + 1) * slots)
-            cosine, low_sine, high_sine = cos_ref[part], low_ref[part], high_ref[part]
+            apart = first_ref[buf, 1] == 1
+            tables = []
+            for ref in (cos_ref, low_ref, high_ref):
+                start = ref[:BLOCK]
+                tables.append(jnp.concatenate([start, jnp.where(apart, start, ref[BLOCK:])], axis=0))
+            cosine, low_sine, high_sine = tables
             queries = turn_lanes(mixed[part, :HEAD], cosine, low_sine, high_sine).astype(bf16)
             keys = turn_lanes(mixed[part, HEAD : 2 * HEAD], cosine, low_sine, high_sine).astype(bf16)
             values = mixed[part, 2 * HEAD :].astype(bf16)
@@ -350,14 +417,14 @@
         grid_spec=pltpu.PrefetchScalarGridSpec(
             num_scalar_prefetch=3,
             grid=(total // rows,),
-            in_specs=[ANYWHERE] * (1 + nw) + [moving(D), fixed(1, 3 * HEAD)] + [moving(LANES)] * 3,
+            in_specs=[ANYWHERE] * (1 + nw) + [moving(D), fixed(1, 3 * HEAD)] + [fixed(slots, LANES)] * 3,
             out_specs=[moving(HEAD), moving(3 * HEAD), fixed(D // 2, width), fixed(D // 2, width), fixed(1, 3 * HEAD)],
             scratch_shapes=chunk_scratch(total, width, team.shape[0], copy_count(w_pieces)),
         ),
         out_shape=[shaped((total, HEAD), bf16), shaped((total, 3 * HEAD), bf16)]
         + [shaped((D // 2, width), bf16)] * 2
         + [shaped((1, 3 * HEAD), f32)],
-        **params(FENCE),
+        **params("attn"),
     )(members, first, live, team, *w_pieces, a, b, *rotary)
 
 
@@ -429,7 +496,7 @@
         out_shape=shapes,
         scratch_shapes=[pltpu.VMEM((D, e - b), bf16) for b, e in places]
         + [pltpu.SemaphoreType.DMA((copy_count(group),)) for group in weights],
-        **params(19),
+        **params("out"),
     )(*[piece for group in weights for piece in group], *lefts)
 
 
@@ -477,11 +544,11 @@
         out_shape=shapes + [shaped((8, D), f32)],
         scratch_shapes=[pltpu.VMEM((D, e - b), bf16) for b, e in places]
         + [pltpu.SemaphoreType.DMA((copy_count(group),)) for group in weights],
-        **params(FENCE),
+        **params("back"),
     )(*[piece for group in weights for piece in group], *lefts, hat, gain_one, gain_two)
 
 
-def split_sum(left, right, steps):
+def split_sum(left, right, steps, role):
     rows, width = left.shape
     block = rows // 2 // steps
 
@@ -497,25 +564,56 @@
         in_specs=[low, high, low, high],
         out_specs=[low, low],
         out_shape=[shaped((rows // 2, width), f32), shaped((rows // 2, width), bf16)],
-        **params(4),
+        **params(role),
     )(left, left, right, right)
 
 
-def last_sum(kept, got, steps, cost):
-    rows, width = kept.shape
-
-    def kernel(l_ref, r_ref, out_ref):
-        out_ref[...] = (l_ref[...] + r_ref[...].astype(f32)).astype(bf16)
-
-    spec = blocks((rows // steps, width), lambda i: (i, 0))
+def last_sum(kept, got, role):
+    count, steps = len(kept), 2
+    rows = kept[0].shape[0]
+    widths = [v.shape[1] for v in kept]
+
+    def kernel(*refs):
+        begin = 0
+        for k in range(count):
+            here = slice(begin, begin + widths[k])
+            refs[-1][:, here] = (refs[k][...] + refs[count + k][...].astype(f32)).astype(bf16)
+            begin += widths[k]
+
+    spec = lambda width: blocks((rows // steps, width), lambda i: (i, 0))
     return pl.pallas_call(
         kernel,
         grid=(steps,),
-        in_specs=[spec, spec],
-        out_specs=spec,
-        out_shape=shaped((rows, width), bf16),
-        **params(cost),
-    )(kept, got)
+        in_specs=[spec(w) for w in widths] * 2,
+        out_specs=spec(sum(widths)),
+        out_shape=shaped((rows, sum(widths)), bf16),
+        **params(role),
+    )(*kept, *got)
+
+
+def last_sum_members(kept, got, extra, role):
+    count = len(kept)
+    members, more, width = extra.shape
+    rows = kept[0].shape[0] // members
+    widths = [v.shape[1] for v in kept]
+
+    def kernel(*refs):
+        begin = 0
+        for k in range(count):
+            here = slice(begin, begin + widths[k])
+            refs[-1][0, :rows, here] = (refs[k][...] + refs[count + k][...].astype(f32)).astype(bf16)
+            begin += widths[k]
+        refs[-1][0, rows:, :] = refs[-2][0]
+
+    spec = lambda w: blocks((rows, w), lambda i: (i, 0))
+    return pl.pallas_call(
+        kernel,
+        grid=(members,),
+        in_specs=[spec(w) for w in widths] * 2 + [blocks((1, more, width), lambda i: (i, 0, 0))],
+        out_specs=blocks((1, rows + more, width), lambda i: (i, 0, 0)),
+        out_shape=shaped((members, rows + more, width), bf16),
+        **params(role),
+    )(*kept, *got, extra)
 
 
 def finish_tokens(order, tokens, other, kept, got, back):
@@ -549,11 +647,11 @@
             scratch_shapes=[pltpu.VMEM((rows, D), f32)],
         ),
         out_shape=shaped((slots, D), bf16),
-        **params(4),
+        **params("fin"),
     )(order, tokens, other, kept, got)
 
 
-def adamw_columns(got, weight, first_m, second_m, section, unit, offset, sections, cost, held=None):
+def adamw_columns(got, weight, first_m, second_m, section, unit, offset, sections, role, held=None):
     rows, width = weight.shape
     span = TEAM * unit
     part = max(rows // 4, 16) if rows % 16 == 0 else rows
@@ -581,7 +679,7 @@
         out_specs=[full] * 4,
         out_shape=[shaped((rows, width), f32)] * 4,
         input_output_aliases={4 + k: k for k in range(len(extra))},
-        **params(cost),
+        **params(role),
     )(got, weight, first_m, second_m, *extra)
 
 
@@ -606,6 +704,7 @@
     first_vectors,
     second_vectors,
 ):
+    tokens_in = tokens
     far_size = lax.axis_size("far")
     paired = far_size == 2
     groups = 2 * far_size
@@ -658,52 +757,56 @@
         span = slice(TEAM * begin, TEAM * end)
         return jnp.concatenate([cut(w[:, span], 1)[:, 0].transpose(1, 0, 2) for w in (w_mlp_in, w_mlp_out)], axis=2)
 
-    owns, far_got = [], [None] * count
-    for index, chunk in enumerate(CHUNKS):
-        block = columns(chunk)
-        if index == 0 and paired:
-            width = block.shape[2]
-            extra = jnp.pad(payload, (0, PACK_ROWS * width - payload.shape[0])).reshape(1, PACK_ROWS, width)
-            block = jnp.concatenate([block, jnp.broadcast_to(extra, (TEAM, PACK_ROWS, width))], axis=1)
-        waits = owns[-1:]
-        if paired and index == 2:
-            far_got[0] = lax.ppermute(owns[0], "far", SWAP)
-            waits = waits + far_got[:1]
-        got = lax.all_to_all(after(block, *waits) if waits else block, NEAR, 0, 0, tiled=True)
-        owns.append(got if got.shape[1] != rows_dev else got.reshape(rows_team, got.shape[2]))
-
     if paired:
         both_send = prepare_tokens(to_local, block_live, tokens, cotangent)
     else:
         both_send = prepare_tokens(to_local, block_live, local_order(tokens), local_order(cotangent))
+    owns, far_got, load_of, begin_of = [], [None] * len(LOADS), {}, {}
+    for load, chunks in enumerate(LOADS):
+        parts, begin = [], 0
+        for index in chunks:
+            parts.append(columns(CHUNKS[index]))
+            load_of[index], begin_of[index] = load, begin
+            begin += parts[-1].shape[2]
+        block = jnp.concatenate(parts, axis=2) if len(parts) > 1 else parts[0]
+        if load == 0 and paired:
+            extra = jnp.pad(payload, (0, PACK_ROWS * begin - payload.shape[0])).reshape(1, PACK_ROWS, begin)
+            block = jnp.concatenate([block, jnp.broadcast_to(extra, (TEAM, PACK_ROWS, begin))], axis=1)
+        waits = owns[-1:]
+        if paired and load == 1:
+            far_got[0] = lax.ppermute(owns[0], "far", SWAP)
+        got = lax.all_to_all(after(block, *waits) if waits else block, NEAR, 0, 0, tiled=True)
+        owns.append(got if got.shape[1] != rows_dev else got.reshape(rows_team, got.shape[2]))
+
     team = lax.all_gather(both_send, NEAR, axis=0, tiled=False)
     members = jnp.array([4 * l + 2 * r + c for c in range(2) for r in range(2) for l in range(2)], jnp.int32) ^ me
 
-    w_chunks = []
-
-    def send_far(index, *waits):
-        far_got[index] = lax.ppermute(after(owns[index], far_got[index - 1], *waits), "far", SWAP)
-
-    def cross(index, *waits):
+    loads = []
+
+    def send_far(load, *waits):
+        far_got[load] = lax.ppermute(after(owns[load], *waits) if waits else owns[load], "far", SWAP)
+
+    def cross(load, *waits):
         if paired:
-            w_chunks[index][1] = far_got[index]
-            over = after(far_got[index], *waits) if waits else far_got[index]
-            w_chunks[index][3] = lax.ppermute(over, "col", SWAP)
+            loads[load][1] = far_got[load]
+            over = after(far_got[load], *waits) if waits else far_got[load]
+            loads[load][3] = lax.ppermute(over, "col", SWAP)
 
     if paired:
         for own in owns:
-            w_chunks.append([own, None, lax.ppermute(own, "col", SWAP), None])
-        send_far(1, owns[2])
-        send_far(2, owns[3])
+            loads.append([own, None, lax.ppermute(own, "col", SWAP), None])
+        send_far(1, far_got[0])
+        send_far(2, far_got[1])
     else:
         for own in owns:
-            w_chunks.append([lax.all_gather(own, CROSS, axis=0, tiled=True)])
+            loads.append([lax.all_gather(own, CROSS, axis=0, tiled=True)])
     cross(0)
     cross(1)
 
     length = piece + 2 * BLK_DEV
     if paired:
-        got = jnp.stack([part[:, rows_dev:].reshape(TEAM, -1)[:, :length] for part in (*w_chunks[0][:3], after(w_chunks[0][3], far_got[1]))])
+        parts = lax.optimization_barrier((*loads[0], owns[2], far_got[1]))[:4]
+        got = extra_rows(parts, rows_dev).reshape(4, TEAM, -1)[:, :, :length]
         mine = got[0]
         got = flips(got.reshape(2, 2, half, 2, length), 0, 1)
         everyone = got.transpose(1, 2, 0, 3, 4).reshape(4 * TEAM, length)
@@ -715,9 +818,7 @@
     vec_full = everyone[:, :piece].astype(f32).reshape(VEC)
     b_query, b_value, b_att, b_in, b_mlp, *norm_vectors = split_vectors(vec_full)
     gain_one, shift_one, gain_two, shift_two = (local_order(v)[None] for v in norm_vectors)
-    slot = jnp.arange(slot_total, dtype=jnp.int32)
-    position = slot[None, :] - BLOCK * jnp.repeat(first_table, BLOCK, axis=1)
-    rotary = rotary_rows(position.reshape(team_slots).astype(f32))
+    rotary = rotary_rows(jnp.arange(slot_total, dtype=jnp.int32).astype(f32))
     bias_q = lax.dynamic_slice(b_query, (me * HEAD,), (HEAD,))
     bias_v = lax.dynamic_slice(b_value, (me * HEAD,), (HEAD,))
     bias_qkv = jnp.concatenate([bias_q, jnp.zeros_like(bias_q), bias_v])[None]
@@ -731,20 +832,21 @@
 
     def run_chunk(index, *waits):
         chunk = CHUNKS[index]
+        pieces, offset = loads[load_of[index]], begin_of[index]
         ready = after(attn_in if chunk is None else mlp_in, *waits) if waits else (attn_in if chunk is None else mlp_in)
         if chunk is None:
             left_out, left_back, keep, send, total = attn_chunk(
-                members, first_table, live_table, team, ready, w_chunks[index], bias_qkv, rotary, rows_dev
+                members, first_table, live_table, team, ready, pieces, offset, bias_qkv, rotary, rows_dev
             )
-            places_out.append((3 * HEAD, 4 * HEAD))
-            places_back.append((0, 3 * HEAD))
+            places_out.append((offset + 3 * HEAD, offset + 4 * HEAD))
+            places_back.append((offset, offset + 3 * HEAD))
         else:
             begin, end = chunk
             left_out, left_back, keep, send, total = mlp_chunk(
-                members, team, ready, w_chunks[index], bias_in(begin, end), rows_dev
+                members, team, ready, pieces, offset, bias_in(begin, end), rows_dev
             )
-            places_out.append((end - begin, 2 * (end - begin)))
-            places_back.append((0, end - begin))
+            places_out.append((offset + end - begin, offset + 2 * (end - begin)))
+            places_back.append((offset, offset + end - begin))
         lefts_out.append(left_out)
         lefts_back.append(left_back)
         sums.append(total[0])
@@ -759,112 +861,162 @@
             term = jnp.concatenate([keep, got], axis=0)
             owned[index] = lax.psum_scatter(term, CROSS, scatter_dimension=0, tiled=True)
             return tokens[0]
-        kept, sent = split_sum(after(keep, *tokens), got, 2)
+        kept, sent = split_sum(after(keep, *tokens), got, 2, f"col{index}")
         grouped[index] = (kept, lax.ppermute(sent, "far", SWAP))
         return kept
 
-    def sum_far(index, *tokens, cost=2.5):
+    def sum_far(chunks, *tokens, extra=None):
         if not paired:
-            return tokens[0]
-        kept, got = grouped[index]
-        owned[index] = last_sum(after(kept, *tokens), got, 2, cost)
-        return owned[index]
-
-    def to_rows(index):
-        term = owned[index]
-        return lax.all_to_all(term.reshape(TEAM, rows_dev, term.shape[1]), NEAR, 0, 0, tiled=True)
+            return jnp.concatenate([owned[index] for index in chunks], axis=1)
+        kept = [grouped[index][0] for index in chunks]
+        kept[0] = after(kept[0], *tokens)
+        got = [grouped[index][1] for index in chunks]
+        role = f"far{chunks[0]}"
+        return last_sum(kept, got, role) if extra is None else last_sum_members(kept, got, extra, role)
+
+    def to_rows(term):
+        blocked = term if term.ndim == 3 else term.reshape(TEAM, rows_dev, term.shape[1])
+        return lax.all_to_all(blocked, NEAR, 0, 0, tiled=True)
 
     held = {}
 
-    def update(index, got, *tokens):
+    def update(index, got, start, *tokens):
         chunk = CHUNKS[index]
         got = after(got, *tokens)
         if chunk is None:
-            held["qkv"] = adamw_columns(got, w_qkv, first_qkv, second_qkv, 0, HEAD, 0, 3, FENCE)
-            held["att"] = adamw_columns(got, w_attn_out, first_attn_out, second_attn_out, 3, HEAD, 0, 1, 3)
-            return held["att"][0]
+            held["qkv"] = adamw_columns(got, w_qkv, first_qkv, second_qkv, start // HEAD, HEAD, 0, 3, "adam1")
+            held["att"] = adamw_columns(got, w_attn_out, first_attn_out, second_attn_out, start // HEAD + 3, HEAD, 0, 1, "adam1b")
+            return held["qkv"][0], held["att"][0]
         begin, end = chunk
         unit = end - begin
         for kind, name, arrays in ((0, "in", (w_mlp_in, first_mlp_in, second_mlp_in)), (1, "out", (w_mlp_out, first_mlp_out, second_mlp_out))):
-            held[name] = adamw_columns(got, *arrays, kind, unit, begin // unit, 1, 4, held.get(name))
-        return held["out"][0]
-
-    token = run_chunk(0)
-    cross(2, token)
-    if paired:
-        send_far(3, token)
-    token = run_chunk(1, token, *far_got[2:3] if paired else ())
-    cross(3, token)
-    token = sum_columns(0, token)
-    token = run_chunk(2, token, *far_got[3:4] if paired else ())
-    token = sum_far(0, token)
-    rows_zero = to_rows(0)
-    token = run_chunk(3, token)
-    token = sum_columns(1, token)
+            held[name] = adamw_columns(got, *arrays, start // unit + kind, unit, begin // unit, 1, f"adam{index}{name}", held.get(name))
+        return held["in"][0], held["out"][0]
+
+    w_of_chunk = [loads[load_of[index]] for index in range(count)]
     attn_index = CHUNKS.index(None)
-    lefts_back[0] = after(lefts_back[0], token, rows_zero)
-    back_send, back_keep, norm_sums = back_part(
-        hat, lefts_back, w_chunks, places_back, attn_index, gain_one, gain_two, rows_dev
-    )
-    lefts_out[0] = after(lefts_out[0], back_keep)
-    out_send, out_keep = out_part(lefts_out, w_chunks, places_out, rows_dev)
-
-    def own_step(pair, axis, steps, *tokens):
+    have = {}
+
+    def do_chunk(index, *waits):
+        done = run_chunk(index, *waits)
+        if index == 0:
+            cross(2, done)
+        return (done,)
+
+    def do_back(*waits):
+        lefts = [after(lefts_back[0], *waits), *lefts_back[1:]]
+        have["back_send"], have["back_keep"], have["norm_sums"] = back_part(
+            hat, lefts, w_of_chunk, places_back, attn_index, gain_one, gain_two, rows_dev
+        )
+        return (have["back_keep"],)
+
+    def do_out(*waits):
+        lefts = [after(lefts_out[0], *waits), *lefts_out[1:]]
+        have["out_send"], have["out_keep"] = out_part(lefts, w_of_chunk, places_out, rows_dev)
+        return (have["out_keep"],)
+
+    def own_step(pair, axis, steps, role, *waits):
         kept, sent = pair
-        return split_sum(after(kept, *tokens), lax.ppermute(sent, axis, SWAP), steps)
+        return split_sum(after(kept, *waits), lax.ppermute(sent, axis, SWAP), steps, role)
+
+    def do_own(name, stage, *waits):
+        if stage == "core":
+            pair = own_step((have[f"{name}_keep"], have[f"{name}_send"]), "core", 4, f"{name}_core", *waits)
+        else:
+            pair = own_step(have[f"{name}_pair"], stage, 2, f"{name}_{stage}", *waits)
+        have[f"{name}_pair"] = pair
+        return (pair[0],)
+
+    def do_far(chunks, *waits):
+        more = {}
+        if paired and chunks[0] == 2:
+            width = 2 * sum(CHUNKS[index][1] - CHUNKS[index][0] for index in chunks)
+            flat = after(vector_terms(), *waits).reshape(TEAM, groups * piece)
+            high = flat.astype(bf16)
+            split = jnp.concatenate([high, (flat - high.astype(f32)).astype(bf16)], axis=1)
+            split = jnp.pad(split, ((0, 0), (0, PACK_ROWS * width - split.shape[1])))
+            more = dict(extra=split.reshape(TEAM, PACK_ROWS, width))
+        owned_now = sum_far(chunks, *waits, **more)
+        have[f"rows{chunks[0]}"] = to_rows(owned_now)
+        return (owned_now,)
+
+    def do_finish(name, *waits):
+        kept, sent = have[f"{name}_pair"]
+        got = lax.ppermute(sent, "low" if name == "back" else "row", SWAP)
+        if not paired:
+            kept, got = own_order(kept), own_order(got)
+        other = seed_own if name == "back" else (b_att + b_mlp)[None]
+        have[name] = finish_tokens(to_own, after(tokens_in, *waits), other, kept, got, name == "back")
+        return (have[name],)
 
     alive = (jnp.arange(BLOCK, dtype=jnp.int32)[None, :] < block_live[:, None]).reshape(slot_total)
     seed_own = jnp.where(alive[:, None], cotangent, jnp.zeros_like(cotangent))
-    seed_sum = jnp.sum(seed_own.astype(f32), axis=0)
-
-    def place(values, width):
-        return lax.dynamic_update_slice(jnp.zeros((width,), f32), values, (me * values.shape[0],))
-
-    mlp_order = sorted((k for k in range(count) if CHUNKS[k] is not None), key=lambda k: CHUNKS[k][0])
-    local_vec = jnp.concatenate(
-        [
-            place(sums[attn_index][:HEAD], D),
-            place(sums[attn_index][2 * HEAD :], D),
-            seed_sum,
-            *[place(sums[k], TEAM * sums[k].shape[0]) for k in mlp_order],
-            seed_sum,
-            own_order(norm_sums[:4]).reshape(4 * D),
-        ]
-    )
-    vec_terms = local_vec.reshape(far_size, half, 2, 2, piece).transpose(1, 3, 0, 2, 4).reshape(TEAM, groups, piece)
-    vec_team = jnp.sum(lax.all_to_all(vec_terms, NEAR, 0, 0, tiled=True), axis=0)
+
+    def vector_terms():
+        norm_sums = have["norm_sums"]
+        seed_sum = jnp.sum(seed_own.astype(f32), axis=0)
+
+        def place(values, width):
+            return lax.dynamic_update_slice(jnp.zeros((width,), f32), values, (me * values.shape[0],))
+
+        mlp_order = sorted((k for k in range(count) if CHUNKS[k] is not None), key=lambda k: CHUNKS[k][0])
+        local_vec = jnp.concatenate(
+            [
+                place(sums[attn_index][:HEAD], D),
+                place(sums[attn_index][2 * HEAD :], D),
+                seed_sum,
+                *[place(sums[k], TEAM * sums[k].shape[0]) for k in mlp_order],
+                seed_sum,
+                own_order(norm_sums[:4]).reshape(4 * D),
+            ]
+        )
+        vec_terms = local_vec.reshape(far_size, half, 2, 2, piece).transpose(1, 3, 0, 2, 4).reshape(TEAM, groups, piece)
+
+        return vec_terms
+
+    actions = {
+        "K0": lambda *w: do_chunk(0, *w),
+        "K1": lambda *w: do_chunk(1, *w),
+        "K2": lambda *w: do_chunk(2, *w),
+        "K3": lambda *w: do_chunk(3, *w),
+        "C0": lambda *w: (sum_columns(0, *w),),
+        "C1": lambda *w: (sum_columns(1, *w),),
+        "C2": lambda *w: (sum_columns(2, *w),),
+        "C3": lambda *w: (sum_columns(3, *w),),
+        "B": do_back,
+        "O": do_out,
+        "B1": lambda *w: do_own("back", "core", *w),
+        "B2": lambda *w: do_own("back", "row", *w),
+        "B3": lambda *w: do_finish("back", *w),
+        "O1": lambda *w: do_own("out", "core", *w),
+        "O2": lambda *w: do_own("out", "low", *w),
+        "O3": lambda *w: do_finish("out", *w),
+        "F0": lambda *w: do_far((0, 1), *w),
+        "F2": lambda *w: do_far((2, 3), *w),
+        "A0": lambda *w: update(0, have["rows0"], 0, *w),
+        "A1": lambda *w: update(1, have["rows0"], 512, *w),
+        "A2": lambda *w: update(2, have["rows2"], 0, *w),
+        "A3": lambda *w: update(3, have["rows2"], 1024, *w),
+    }
+    waits = ()
+    for name in ORDER:
+        waits = actions[name](*waits)
+    out, grad_tokens, rows_high = have["out"], have["back"], have["rows2"]
+    if paired:
+        vec_got = rows_high[:, rows_dev:].reshape(TEAM, -1)[:, : 2 * groups * piece].astype(f32)
+        vec_team = jnp.sum(vec_got.reshape(2 * TEAM, groups, piece), axis=0)
+    else:
+        vec_team = jnp.sum(lax.all_to_all(vector_terms(), NEAR, 0, 0, tiled=True), axis=0)
     if paired:
         pick = lambda f, c: lax.dynamic_index_in_dim(vec_team, 2 * (far ^ f) + (column ^ c), 0, keepdims=False)
-        grad_vectors = pick(0, 0) + lax.ppermute(pick(0, 1), "col", SWAP) + lax.ppermute(pick(1, 0), "far", SWAP)
-        grad_vectors = grad_vectors + lax.ppermute(pick(1, 1), ("far", "col"), [(i, 3 - i) for i in range(4)])
+        over_col = lax.ppermute(pick(0, 1), "col", SWAP)
+        over_far = lax.ppermute(pick(1, 0), "far", SWAP)
+        over_both = lax.ppermute(pick(1, 1), ("far", "col"), [(i, 3 - i) for i in range(4)])
+        over_col, over_far, over_both, _ = lax.optimization_barrier((over_col, over_far, over_both, out))
+        grad_vectors = pick(0, 0) + over_col + over_far + over_both
     else:
         grad_vectors = jnp.sum(lax.all_to_all(vec_team, ("far", "col"), 0, 0, tiled=True), axis=0)
     new_vec, m_vec, u_vec = adamw_update(vectors, grad_vectors, first_vectors, second_vectors, vector_rate, 0.0)
-
-    token = sum_columns(2, out_keep)
-    token = sum_far(1, token, vec_team, cost=FENCE)
-    rows_one = to_rows(1)
-    back_pair = own_step((back_keep, back_send), "core", 4, token)
-    out_pair = own_step((out_keep, out_send), "core", 4, back_pair[0])
-    token = sum_columns(3, out_pair[0])
-    token = update(0, rows_zero, token)
-    token = update(1, rows_one, token)
-    token = sum_far(2, token)
-    rows_two = to_rows(2)
-    back_pair = own_step(back_pair, "row", 2, token)
-    out_pair = own_step(out_pair, "low", 2, back_pair[0])
-    token = sum_far(3, out_pair[0])
-    rows_three = to_rows(3)
-    token = update(2, rows_two, token)
-    ordered = (lambda v: v) if paired else own_order
-    back_got = lax.ppermute(back_pair[1], "low", SWAP)
-    out_got = lax.ppermute(out_pair[1], "row", SWAP)
-    grad_tokens = finish_tokens(to_own, after(tokens, token), seed_own, ordered(back_pair[0]), ordered(back_got), True)
-    bias_out = (b_att + b_mlp)[None]
-    out = finish_tokens(
-        to_own, after(tokens, grad_tokens), bias_out, ordered(out_pair[0]), ordered(out_got), False
-    )
-    update(3, rows_three, out)
     grad_qkv, new_qkv, m_qkv, u_qkv = held["qkv"]
     grad_attn_out, new_att, m_att, u_att = held["att"]
     grad_mlp_in, new_in, m_in, u_in = held["in"]

time: 609 us -> 585 us (0.961)
  starting transfers between devices: 80.9 us -> 56.8 us
  waiting for transfers between devices: 193 us -> 183 us
  local copies, waits for them, and re-layouts: 26.6 us -> 32.9 us
    ppermute x4, waiting for transfers between devices: 12.7 us -> 44.8 us  [sum_columns(): grouped[index] = (kept, lax.ppermute(sent, 'far', SWAP))]
    ppermute x15 -> x12, waiting for transfers between devices: 81.9 us -> 51.2 us  [the longest x2 42.5 us: send_far(): lax.ppermute(after(owns[load], *waits) if waits else owns[load], 'far', S...]
    all_to_all x4 -> x3, waiting for transfers between devices: 45.2 us -> 15.3 us  [body(): lax.all_to_all(after(block, *waits) if waits else block, NEAR, 0, 0, tile...]
    all_gather x1, waiting for transfers between devices: 0.01 us -> 23.8 us  [body(): team = lax.all_gather(both_send, NEAR, axis=0, tiled=False)]
    all_to_all x5 -> x2, starting transfers between devices: 20.8 us -> 7.48 us  [to_rows(): return lax.all_to_all(blocked, NEAR, 0, 0, tiled=True)]
    all_to_all x5 -> x2, waiting for transfers between devices: 0.01 us -> 9.62 us  [to_rows(): return lax.all_to_all(blocked, NEAR, 0, 0, tiled=True)]
    all_to_all x4 -> x3, starting transfers between devices: 21.1 us -> 13.1 us  [body(): lax.all_to_all(after(block, *waits) if waits else block, NEAR, 0, 0, tile...]
    ppermute x4, waiting for transfers between devices: 7.97 us -> 0.01 us  [run_chunk(): terms.append((keep, lax.ppermute(send, 'col', SWAP) if paired else send))]
  transfers between devices with their start and end apart: 39 -> 32, of which waited for: 12 -> 9; matrix products, arithmetic and copies ran while one was open for 7% -> 7% of each run, Pallas kernels for 42% -> 47%
where the time goes in v3:
time: 585 us; the launch traced here: 574 us
  Pallas kernels  270 us (46%)
  waiting for transfers between devices  183 us (31%)
  starting transfers between devices  56.8 us (10%)
  local copies, waits for them, and re-layouts  32.9 us (6%)
  other arithmetic  16.6 us (3%)
  between operations  15.2 us (3%)
    pallas_call x3, Pallas kernels, mlp_chunk(): pl.pallas_call(kernel, grid_spec=pltpu.PrefetchScalarGridSpec(num_scalar_...  70.7 us
    ppermute x4, waiting for transfers between devices, sum_columns(): grouped[index] = (kept, lax.ppermute(sent, 'far', SWAP))  44.8 us
    ppermute x2, waiting for transfers between devices, send_far(): lax.ppermute(after(owns[load], *waits) if waits else owns[load], 'far', S...  42.5 us
    pallas_call x8, Pallas kernels, adamw_columns(): pl.pallas_call(kernel, grid=(sections, rows // part), in_specs=[got_spec,...  39 us
    ppermute x1, waiting for transfers between devices, body(): far_got[0] = lax.ppermute(owns[0], 'far', SWAP)  37.8 us
    pallas_call x1, Pallas kernels, attn_chunk(): pl.pallas_call(kernel, grid_spec=pltpu.PrefetchScalarGridSpec(num_scalar_...  36.3 us
    pallas_call x8, Pallas kernels, split_sum(): pl.pallas_call(kernel, grid=(steps,), in_specs=[low, high, low, high], ou...  32.7 us
    pallas_call x1, Pallas kernels, back_part(): pl.pallas_call(kernel, grid=(TEAM,), in_specs=[ANYWHERE] * (count * per)...  32.4 us
  transfers between devices with their start and end apart: 32, of which 9 were waited for; matrix products, arithmetic and copies ran while one was open for 7% of the time, Pallas kernels for 47%

profile of v3, /device:TPU:0, one launch (start us, length us, event | category | flops | bytes accessed | tf_op | source)
XLA Modules:
  0.0 574.3 jit_solution(7727187281598642604)
XLA Ops:
  11.4 5.3 all-to-all-start
  23.7 3.3 all-to-all-done.refs_0_
  27.0 4.3 all-to-all-start.1
  33.7 12.0 %all-to-all-done.1 = bf16[8,64,1024]{2,1,0:T(8,128)(2,1)} async-done(((bf16[8,64,1024]{2,1,0:T(8,128)(2,1)}), bf16[8,64,1024]{2,1,0:T(8,128)(2,1)}, u32[]{:S(2)}, u32[]{:S(2)}) %all-to-all-start.1) | async-done | bytes 1048608 | tf_op jit(solution)/shard_map/all_to_all | solution.py:778
  45.7 3.6 all-to-all-start.2
  49.4 4.1 shard_map.363
  54.7 2.8 collective-permute-start
  58.2 37.8 %collective-permute-done.refs_1_ = bf16[8,80,512]{2,1,0:T(8,128)(2,1)S(1)} collective-permute-done((bf16[8,80,512]{2,1,0:T(8,128)(2,1)}, bf16[8,80,512]{2,1,0:T(8,128)(2,1)S(1)}, u32[]{:S(2)}, u32[]{:S(2)}) %collective-permute-start) | collective-permute-done | bytes 655392 | tf_op jit(solution)/shard_map/ppermute | solution.py:777
  96.0 3.3 collective-permute-start.1
  107.5 37.6 %collective-permute-done.1.refs_1_.refs_5_ = bf16[512,1024]{1,0:T(8,128)(2,1)} collective-permute-done((bf16[512,1024]{1,0:T(8,128)(2,1)}, bf16[512,1024]{1,0:T(8,128)(2,1)}, u32[]{:S(2)}, u32[]{:S(2)}) %collective-permute-start.1) | collective-permute-done | bytes 1048608 | tf_op jit(solution)/shard_map/ppermute | solution.py:787
  147.0 2.5 shard_map.364
  159.7 3.3 collective-permute-start.2
  165.1 23.8 %all-gather.3.cloned.1.call-done = bf16[4096,2048]{1,0:T(8,128)(2,1)} async-done(((bf16[512,2048]{1,0:T(8,128)(2,1)}), bf16[4096,2048]{1,0:T(8,128)(2,1)}) %all-gather.3.cloned.1.call-update) | async-done | bytes 16777232 | tf_op jit(solution)/shard_map/all_gather | solution.py:781
  188.9 14.2 %shard_map.365 = (bf16[2048,2048]{1,0:T(8,128)(2,1)}, bf16[2048,2048]{1,0:T(8,128)(2,1)}, bf16[2048,2048]{1,0:T(8,128)(2,1)}) custom-call(s32[8]{0:T(128)} %get-tuple-element.283.members_ref, bf16[8,512,2048]{2,1,0:T(8,128)(2,1)} %bitcast.157, f32[1,2048]{1,0:T(1,128)} %bitcast.140, f32[1,2048]{1,0:T(1,128)} %bitcast.143, f32[1,2048]{1,0:T(1,128)} %bitcast.138, ...), custom_call_target="tpu_custom_call" | custom-call | flops 10000000000 | bytes 1024 | tf_op jit(solution)/shard_map/pallas_call | solution.py:252
  203.1 19.9 %shard_map.366 = (bf16[2048,256]{1,0:T(8,128)(2,1)}, bf16[2048,256]{1,0:T(8,128)(2,1)}, bf16[1024,512]{1,0:T(8,128)(2,1)}, bf16[1024,512]{1,0:T(8,128)(2,1)}, f32[1,256]{1,0:T(1,128)}) custom-call(s32[8]{0:T(128)} %get-tuple-element.283.members_ref, bf16[8,512,2048]{2,1,0:T(8,128)(2,1)} %bitcast.158, bf16[8,80,512]{2,1,0:T(8,128)(2,1)} %all-to-all-done.refs_0_, ...), custom_call_target="tpu_custom_call" | custom-call | flops 15000000512 | bytes 1024 | tf_op jit(solution)/shard_map/pallas_call | solution.py:342
  224.7 5.0 collective-permute-done.2.refs_1_.refs_9_.refs_13_
  231.4 36.3 %shard_map.367 = (bf16[2048,256]{1,0:T(8,128)(2,1)}, bf16[2048,768]{1,0:T(8,128)(2,1)}, bf16[1024,1024]{1,0:T(8,128)(2,1)}, bf16[1024,1024]{1,0:T(8,128)(2,1)}, f32[1,768]{1,0:T(1,128)}) custom-call(s32[8]{0:T(128)} %get-tuple-element.283.members_ref, s32[8,2]{1,0:T(8,128)} %get-tuple-element.274.first_ref, s32[8,2]{1,0:T(8,128)} %get-tuple-element.273.live_ref, ...), custom_call_target="tpu_custom_call" | custom-call | flops 30000001024 | bytes 1024 | tf_op jit(solution)/shard_map/pallas_call | solution.py:415
  271.9 2.5 shard_map.368
  274.4 8.7 %collective-permute-done.6.refs_3_.refs_11_.refs_15_ = bf16[512,1536]{1,0:T(8,128)(2,1)S(1)} collective-permute-done((bf16[512,1536]{1,0:T(8,128)(2,1)}, bf16[512,1536]{1,0:T(8,128)(2,1)S(1)}, u32[]{:S(2)}, u32[]{:S(2)}) %collective-permute-start.6) | collective-permute-done | bytes 1572896 | tf_op jit(solution)/shard_map/ppermute | solution.py:793
  284.2 31.1 %shard_map.369 = (bf16[2048,512]{1,0:T(8,128)(2,1)}, bf16[2048,512]{1,0:T(8,128)(2,1)}, bf16[1024,1024]{1,0:T(8,128)(2,1)}, bf16[1024,1024]{1,0:T(8,128)(2,1)}, f32[1,512]{1,0:T(1,128)}) custom-call(s32[8]{0:T(128)} %get-tuple-element.283.members_ref, bf16[8,512,2048]{2,1,0:T(8,128)(2,1)} %bitcast.160, bf16[512,1536]{1,0:T(8,128)(2,1)} %bitcast.113, ...), custom_call_target="tpu_custom_call" | custom-call | flops 1999999991808 | bytes 1024 | tf_op jit(solution)/shard_map/pallas_call | solution.py:342
  315.3 19.7 %shard_map.370 = (bf16[2048,256]{1,0:T(8,128)(2,1)}, bf16[2048,256]{1,0:T(8,128)(2,1)}, bf16[1024,512]{1,0:T(8,128)(2,1)}, bf16[1024,512]{1,0:T(8,128)(2,1)}, f32[1,256]{1,0:T(1,128)}) custom-call(s32[8]{0:T(128)} %get-tuple-element.283.members_ref, bf16[8,512,2048]{2,1,0:T(8,128)(2,1)} %bitcast.161, bf16[512,1536]{1,0:T(8,128)(2,1)} %bitcast.114, ...), custom_call_target="tpu_custom_call" | custom-call | flops 15000000512 | bytes 1024 | tf_op jit(solution)/shard_map/pallas_call | solution.py:342
  340.1 3.5 shard_map.371
  343.5 19.6 %shard_map.372 = (bf16[1024,2048]{1,0:T(8,128)(2,1)}, bf16[1024,2048]{1,0:T(8,128)(2,1)}) custom-call(bf16[8,80,512]{2,1,0:T(8,128)(2,1)} %all-to-all-done.refs_0_, bf16[8,80,512]{2,1,0:T(8,128)(2,1)} %copy-done.12, bf16[8,80,512]{2,1,0:T(8,128)(2,1)} %collective-permute-done.4.refs_2_, bf16[8,80,512]{2,1,0:T(8,128)(2,1)} %collective-permute-done.5.refs_3_, ...), custom_call_target="tpu_custom_call" | custom-call | flops 19000000512 | bytes 1024 | tf_op jit(solution)/shard_map/pallas_call | solution.py:491
  363.1 32.4 %shard_map.373 = (bf16[1024,2048]{1,0:T(8,128)(2,1)}, bf16[1024,2048]{1,0:T(8,128)(2,1)}, f32[8,2048]{1,0:T(8,128)}) custom-call(bf16[8,80,512]{2,1,0:T(8,128)(2,1)} %all-to-all-done.refs_0_, bf16[8,80,512]{2,1,0:T(8,128)(2,1)} %copy-done.12, bf16[8,80,512]{2,1,0:T(8,128)(2,1)} %collective-permute-done.4.refs_2_, ...), custom_call_target="tpu_custom_call" | custom-call | flops 1000000000 | bytes 1024 | tf_op jit(solution)/shard_map/pallas_call | solution.py:537
  399.9 2.4 shard_map.374
  402.3 2.9 collective-permute-start.18
  406.2 3.3 shard_map.375
  409.5 3.6 all-to-all-start.4
  413.1 6.3 %shard_map.376 = (f32[512,2048]{1,0:T(8,128)}, bf16[512,2048]{1,0:T(8,128)(2,1)}) custom-call(bf16[1024,2048]{1,0:T(8,128)(2,1)} %get-tuple-element.179.l_low.l_high, bf16[1024,2048]{1,0:T(8,128)(2,1)} %get-tuple-element.179.l_low.l_high, bf16[1024,2048]{1,0:T(8,128)(2,1)} %collective-permute-done.14.r_low.r_high, ...), custom_call_target="tpu_custom_call" | custom-call | flops 100000000 | bytes 1024 | tf_op jit(solution)/shard_map/pallas_call | solution.py:561
  419.5 6.3 %shard_map.377 = (f32[512,2048]{1,0:T(8,128)}, bf16[512,2048]{1,0:T(8,128)(2,1)}) custom-call(bf16[1024,2048]{1,0:T(8,128)(2,1)} %get-tuple-element.182.l_low.l_high, bf16[1024,2048]{1,0:T(8,128)(2,1)} %get-tuple-element.182.l_low.l_high, bf16[1024,2048]{1,0:T(8,128)(2,1)} %collective-permute-done.15.r_low.r_high, ...), custom_call_target="tpu_custom_call" | custom-call | flops 1000000000 | bytes 1024 | tf_op jit(solution)/shard_map/pallas_call | solution.py:561
  425.8 3.5 shard_map.378
  433.7 44.8 %collective-permute-done.17.refs_2_ = bf16[512,1024]{1,0:T(8,128)(2,1)S(1)} collective-permute-done((bf16[512,1024]{1,0:T(8,128)(2,1)}, bf16[512,1024]{1,0:T(8,128)(2,1)S(1)}, u32[]{:S(2)}, u32[]{:S(2)}) %collective-permute-start.17) | collective-permute-done | bytes 1048608 | tf_op jit(solution)/shard_map/ppermute | solution.py:865
  479.5 6.2 %shard_map.379 = bf16[8,80,1536]{2,1,0:T(8,128)(2,1)} custom-call(f32[512,1024]{1,0:T(8,128)} %get-tuple-element.188.refs_0_, f32[512,512]{1,0:T(8,128)} %get-tuple-element.175.refs_1_, bf16[512,1024]{1,0:T(8,128)(2,1)} %copy-done.30, bf16[512,512]{1,0:T(8,128)(2,1)} %collective-permute-done.18.refs_3_, bf16[8,16,1536]{2,1,0:T(8,128)(2,1)} %bitcast.134), custom_call_target="tpu_custom_call" | custom-call | flops 3000000000 | bytes 1024 | tf_op jit(solution)/shard_map/pallas_call | solution.py:609
  485.7 3.9 all-to-all-start.3
  489.6 4.1 shard_map.380
  493.7 3.9 shard_map.382
  497.6 9.5 %shard_map.381 = (f32[64,6144]{1,0:T(8,128)}, f32[64,6144]{1,0:T(8,128)}, f32[64,6144]{1,0:T(8,128)}, f32[64,6144]{1,0:T(8,128)}) custom-call(bf16[8,64,1536]{2,1,0:T(8,128)(2,1)} %copy-done.6, f32[64,6144]{1,0:T(8,128)} %w_ref.8, f32[64,6144]{1,0:T(8,128)} %m_ref.8, f32[64,6144]{1,0:T(8,128)} %u_ref.8), custom_call_target="tpu_custom_call" | custom-call | flops 8999999488 | bytes 1024 | tf_op jit(solution)/shard_map/pallas_call | solution.py:675
  507.2 3.9 shard_map.384
  511.1 3.9 shard_map.383
  515.0 4.2 shard_map.385
  522.7 9.6 %all-to-all-done.3.g_ref = bf16[8,80,1536]{2,1,0:T(8,128)(2,1)S(1)} async-done(((bf16[8,80,1536]{2,1,0:T(8,128)(2,1)}), bf16[8,80,1536]{2,1,0:T(8,128)(2,1)S(1)}, u32[]{:S(2)}, u32[]{:S(2)}) %all-to-all-start.3) | async-done | bytes 1966112 | tf_op jit(solution)/shard_map/all_to_all | solution.py:879
  533.6 4.9 shard_map.387
  538.5 4.9 shard_map.386
  543.4 3.9 shard_map.389
  547.3 3.9 shard_map.388
  554.6 2.7 collective-permute-start.25
  557.3 3.9 shard_map.390
  561.2 5.1 shard_map.391
  (235 shorter events, 70.8 us)
Async XLA Ops:
  9.1 22.2 %copy-start.7 = (bf16[64,8192]{1,0:T(8,128)(2,1)}, bf16[64,8192]{1,0:T(8,128)(2,1)S(1)}, u32[]{:S(2)}) copy-start(bf16[64,8192]{1,0:T(8,128)(2,1)S(1)} %convert.11) | copy-start | bytes 3145732
  11.4 15.6 %all-to-all-start = ((bf16[8,80,512]{2,1,0:T(8,128)(2,1)}), bf16[8,80,512]{2,1,0:T(8,128)(2,1)}, u32[]{:S(2)}, u32[]{:S(2)}) async-start(bf16[8,80,512]{2,1,0:T(8,128)(2,1)} %pad_maximum_fusion.2), calls=%async_computation | async-start | bytes 1310720 | tf_op jit(solution)/shard_map/all_to_all | solution.py:778
  23.7 8.1 %copy-start.10 = (bf16[64,2048]{1,0:T(8,128)(2,1)S(1)}, bf16[64,2048]{1,0:T(8,128)(2,1)}, u32[]{:S(2)}) copy-start(bf16[64,2048]{1,0:T(8,128)(2,1)} %get-tuple-element.259) | copy-start | bytes 786436
  27.0 18.7 %all-to-all-start.1 = ((bf16[8,64,1024]{2,1,0:T(8,128)(2,1)}), bf16[8,64,1024]{2,1,0:T(8,128)(2,1)}, u32[]{:S(2)}, u32[]{:S(2)}) async-start(bf16[8,64,1024]{2,1,0:T(8,128)(2,1)} %pad_maximum_fusion.1), calls=%async_computation.1 | async-start | bytes 2097152 | tf_op jit(solution)/shard_map/all_to_all | solution.py:778
  45.7 101.2 %all-to-all-start.2 = ((bf16[8,64,1536]{2,1,0:T(8,128)(2,1)}), bf16[8,64,1536]{2,1,0:T(8,128)(2,1)S(1)}, u32[]{:S(2)}, u32[]{:S(2)}) async-start(bf16[8,64,1536]{2,1,0:T(8,128)(2,1)} %pad_maximum_fusion), calls=%async_computation.2 | async-start | bytes 3145728 | tf_op jit(solution)/shard_map/all_to_all | solution.py:778
  49.3 139.6 %all-gather.3.cloned.1.call-start = ((), (), s32[]{:S(2)}) async-start(), calls=%async_computation.5 | async-start | bytes 18874368 | tf_op jit(solution)/shard_map/all_gather | solution.py:781
  53.5 50.3 %copy-start.9 = (bf16[256,2048]{1,0:T(8,128)(2,1)S(1)}, bf16[256,2048]{1,0:T(8,128)(2,1)}, u32[]{:S(2)}) copy-start(bf16[256,2048]{1,0:T(8,128)(2,1)} %y_ref.1) | copy-start | bytes 3145732
  54.7 41.3 %collective-permute-start = (bf16[8,80,512]{2,1,0:T(8,128)(2,1)}, bf16[8,80,512]{2,1,0:T(8,128)(2,1)S(1)}, u32[]{:S(2)}, u32[]{:S(2)}) collective-permute-start(bf16[8,80,512]{2,1,0:T(8,128)(2,1)} %all-to-all-done.refs_0_), channel_id=1, source_target_pairs={{0,16},{16,0},{1,17},{17,1},{2,18},{18,2},{3,19},{19,3},{4,20},{20... | collective-permute-start | bytes 1966088 | tf_op jit(solution)/shard_map/ppermute | solution.py:777
  96.0 50.9 %copy-start.12 = (bf16[8,80,512]{2,1,0:T(8,128)(2,1)}, bf16[8,80,512]{2,1,0:T(8,128)(2,1)S(1)}, u32[]{:S(2)}) copy-start(bf16[8,80,512]{2,1,0:T(8,128)(2,1)S(1)} %collective-permute-done.refs_1_) | copy-start | bytes 1966084
  96.0 49.1 %collective-permute-start.1 = (bf16[512,1024]{1,0:T(8,128)(2,1)}, bf16[512,1024]{1,0:T(8,128)(2,1)}, u32[]{:S(2)}, u32[]{:S(2)}) collective-permute-start(bf16[512,1024]{1,0:T(8,128)(2,1)} %bitcast.9.refs_0_.refs_4_), channel_id=1, source_target_pairs={{0,16},{16,0},{1,17},{17,1},{2,18},{18,2},{3,19},{19,3},{4,20},{20... | collective-permute-start | bytes 3145736 | tf_op jit(solution)/shard_map/ppermute | solution.py:787
  99.8 47.1 %collective-permute-start.4 = (bf16[8,80,512]{2,1,0:T(8,128)(2,1)}, bf16[8,80,512]{2,1,0:T(8,128)(2,1)}, u32[]{:S(2)}, u32[]{:S(2)}) collective-permute-start(bf16[8,80,512]{2,1,0:T(8,128)(2,1)} %all-to-all-done.refs_0_), channel_id=1, source_target_pairs={{0,2},{2,0},{1,3},{3,1},{4,6},{6,4},{5,7},{7,5},{8,10},{10,8},{9,1... | collective-permute-start | bytes 1966088 | tf_op jit(solution)/shard_map/ppermute | solution.py:797
  101.7 45.3 %collective-permute-start.5 = (bf16[8,80,512]{2,1,0:T(8,128)(2,1)S(1)}, bf16[8,80,512]{2,1,0:T(8,128)(2,1)}, u32[]{:S(2)}, u32[]{:S(2)}) collective-permute-start(bf16[8,80,512]{2,1,0:T(8,128)(2,1)S(1)} %collective-permute-done.refs_1_), channel_id=1, source_target_pairs={{0,2},{2,0},{1,3},{3,1},{4,6},{6,4},{5,7},{7,5},{8,10},{10,8},{9,1... | collective-permute-start | bytes 1966088 | tf_op jit(solution)/shard_map/ppermute | solution.py:793
  105.7 125.7 %collective-permute-start.7 = (bf16[512,1024]{1,0:T(8,128)(2,1)}, bf16[512,1024]{1,0:T(8,128)(2,1)}, u32[]{:S(2)}, u32[]{:S(2)}) collective-permute-start(bf16[512,1024]{1,0:T(8,128)(2,1)} %bitcast.9.refs_0_.refs_4_), channel_id=1, source_target_pairs={{0,2},{2,0},{1,3},{3,1},{4,6},{6,4},{5,7},{7,5},{8,10},{10,8},{9,1... | collective-permute-start | bytes 3145736 | tf_op jit(solution)/shard_map/ppermute | solution.py:797
  145.1 86.3 %collective-permute-start.8 = (bf16[512,1024]{1,0:T(8,128)(2,1)}, bf16[512,1024]{1,0:T(8,128)(2,1)}, u32[]{:S(2)}, u32[]{:S(2)}) collective-permute-start(bf16[512,1024]{1,0:T(8,128)(2,1)} %collective-permute-done.1.refs_1_.refs_5_), channel_id=1, source_target_pairs={{0,2},{2,0},{1,3},{3,1},{4,6},{6,4},{5,7},{7,5},{8,10},{10,8},{9,1... | collective-permute-start | bytes 3145736 | tf_op jit(solution)/shard_map/ppermute | solution.py:793
  149.5 5.9 %copy-start.19 = (s32[8]{0:T(128)S(1)}, s32[8]{0:T(128)}, u32[]{:S(2)}) copy-start(s32[8]{0:T(128)} %get-tuple-element.285) | copy-start | bytes 100
  149.5 6.6 %copy-start.18 = (s32[8]{0:T(128)S(1)}, s32[8]{0:T(128)}, u32[]{:S(2)}) copy-start(s32[8]{0:T(128)} %get-tuple-element.284) | copy-start | bytes 100
  149.5 7.4 %copy-start.17 = (s32[8]{0:T(128)S(1)}, s32[8]{0:T(128)}, u32[]{:S(2)}) copy-start(s32[8]{0:T(128)} %get-tuple-element.287) | copy-start | bytes 100
  149.5 8.1 %copy-start.16 = (s32[8]{0:T(128)S(1)}, s32[8]{0:T(128)}, u32[]{:S(2)}) copy-start(s32[8]{0:T(128)} %get-tuple-element.286) | copy-start | bytes 100
  150.8 8.9 %copy-start.3 = (bf16[8,64,1536]{2,1,0:T(8,128)(2,1)S(1)}, bf16[8,64,1536]{2,1,0:T(8,128)(2,1)}, u32[]{:S(2)}) copy-start(bf16[8,64,1536]{2,1,0:T(8,128)(2,1)} %copy-done.2) | copy-start | bytes 4718596
  151.8 122.6 %collective-permute-start.3 = (bf16[512,1536]{1,0:T(8,128)(2,1)}, bf16[512,1536]{1,0:T(8,128)(2,1)S(1)}, u32[]{:S(2)}, u32[]{:S(2)}) collective-permute-start(bf16[512,1536]{1,0:T(8,128)(2,1)} %bitcast.112), channel_id=1, source_target_pairs={{0,2},{2,0},{1,3},{3,1},{4,6},{6,4},{5,7},{7,5},{8,10},{10,8},{9,1... | collective-permute-start | bytes 4718600 | tf_op jit(solution)/shard_map/ppermute | solution.py:797
  159.7 69.9 %collective-permute-start.2 = (bf16[512,1536]{1,0:T(8,128)(2,1)S(1)}, bf16[512,1536]{1,0:T(8,128)(2,1)}, u32[]{:S(2)}, u32[]{:S(2)}) collective-permute-start(bf16[512,1536]{1,0:T(8,128)(2,1)S(1)} %bitcast.119), channel_id=1, source_target_pairs={{0,16},{16,0},{1,17},{17,1},{2,18},{18,2},{3,19},{19,3},{4,20},{20... | collective-permute-start | bytes 4718600 | tf_op jit(solution)/shard_map/ppermute | solution.py:787
  223.1 48.8 %collective-permute-start.9 = (bf16[1024,512]{1,0:T(8,128)(2,1)}, bf16[1024,512]{1,0:T(8,128)(2,1)}, u32[]{:S(2)}, u32[]{:S(2)}) collective-permute-start(bf16[1024,512]{1,0:T(8,128)(2,1)} %get-tuple-element.148), channel_id=1, source_target_pairs={{0,2},{2,0},{1,3},{3,1},{4,6},{6,4},{5,7},{7,5},{8,10},{10,8},{9,1... | collective-permute-start | bytes 3145736 | tf_op jit(solution)/shard_map/ppermute | solution.py:853
  229.6 53.4 %collective-permute-start.6 = (bf16[512,1536]{1,0:T(8,128)(2,1)}, bf16[512,1536]{1,0:T(8,128)(2,1)S(1)}, u32[]{:S(2)}, u32[]{:S(2)}) collective-permute-start(bf16[512,1536]{1,0:T(8,128)(2,1)} %collective-permute-done.2.refs_1_.refs_9_.refs_13_), channel_id=1, source_target_pairs={{0,2},{2,0},{1,3},{3,1},{4,6},{6,4},{5,7},{7,5},{8,10},{10,8},{9,1... | collective-permute-start | bytes 4718600 | tf_op jit(solution)/shard_map/ppermute | solution.py:793
  231.4 37.8 %copy-start.25 = (f32[1,256]{1,0:T(1,128)S(1)}, f32[1,256]{1,0:T(1,128)}, u32[]{:S(2)}) copy-start(f32[1,256]{1,0:T(1,128)} %get-tuple-element.141) | copy-start | bytes 3076
  231.4 39.3 %copy-start.14 = (f32[2048]{0:T(1024)S(1)}, f32[2048]{0:T(1024)}, u32[]{:S(2)}) copy-start(f32[2048]{0:T(1024)} %get-tuple-element.252) | copy-start | bytes 24580
  267.7 72.4 %collective-permute-start.10 = (bf16[1024,1024]{1,0:T(8,128)(2,1)}, bf16[1024,1024]{1,0:T(8,128)(2,1)}, u32[]{:S(2)}, u32[]{:S(2)}) collective-permute-start(bf16[1024,1024]{1,0:T(8,128)(2,1)} %get-tuple-element.159), channel_id=1, source_target_pairs={{0,2},{2,0},{1,3},{3,1},{4,6},{6,4},{5,7},{7,5},{8,10},{10,8},{9,1... | collective-permute-start | bytes 6291464 | tf_op jit(solution)/shard_map/ppermute | solution.py:853
  274.3 127.9 %collective-permute-start.12 = (bf16[512,512]{1,0:T(8,128)(2,1)}, bf16[512,512]{1,0:T(8,128)(2,1)}, u32[]{:S(2)}, u32[]{:S(2)}) collective-permute-start(bf16[512,512]{1,0:T(8,128)(2,1)} %get-tuple-element.177), channel_id=1, source_target_pairs={{0,16},{16,0},{1,17},{17,1},{2,18},{18,2},{3,19},{19,3},{4,20},{20... | collective-permute-start | bytes 1572872 | tf_op jit(solution)/shard_map/ppermute | solution.py:865
  274.4 8.7 %copy-start.4 = (bf16[512,1536]{1,0:T(8,128)(2,1)}, bf16[512,1536]{1,0:T(8,128)(2,1)S(1)}, u32[]{:S(2)}) copy-start(bf16[512,1536]{1,0:T(8,128)(2,1)S(1)} %collective-permute-done.3.refs_2_.refs_10_.refs_14_) | copy-start | bytes 4718596
  315.3 22.7 %copy-start.24 = (f32[1,512]{1,0:T(1,128)S(1)}, f32[1,512]{1,0:T(1,128)}, u32[]{:S(2)}) copy-start(f32[1,512]{1,0:T(1,128)} %get-tuple-element.155) | copy-start | bytes 6148
  315.3 24.2 %copy-start.15 = (f32[2048]{0:T(1024)S(1)}, f32[2048]{0:T(1024)}, u32[]{:S(2)}) copy-start(f32[2048]{0:T(1024)} %get-tuple-element.252) | copy-start | bytes 24580
  335.0 63.8 %collective-permute-start.11 = (bf16[1024,512]{1,0:T(8,128)(2,1)}, bf16[1024,512]{1,0:T(8,128)(2,1)S(1)}, u32[]{:S(2)}, u32[]{:S(2)}) collective-permute-start(bf16[1024,512]{1,0:T(8,128)(2,1)} %get-tuple-element.174), channel_id=1, source_target_pairs={{0,2},{2,0},{1,3},{3,1},{4,6},{6,4},{5,7},{7,5},{8,10},{10,8},{9,1... | collective-permute-start | bytes 3145736 | tf_op jit(solution)/shard_map/ppermute | solution.py:853
  336.6 89.1 %collective-permute-start.16 = (bf16[1024,1024]{1,0:T(8,128)(2,1)}, bf16[1024,1024]{1,0:T(8,128)(2,1)}, u32[]{:S(2)}, u32[]{:S(2)}) collective-permute-start(bf16[1024,1024]{1,0:T(8,128)(2,1)} %get-tuple-element.186), channel_id=1, source_target_pairs={{0,2},{2,0},{1,3},{3,1},{4,6},{6,4},{5,7},{7,5},{8,10},{10,8},{9,1... | collective-permute-start | bytes 6291464 | tf_op jit(solution)/shard_map/ppermute | solution.py:853
  343.5 61.7 %collective-permute-start.13 = (bf16[512,1024]{1,0:T(8,128)(2,1)}, bf16[512,1024]{1,0:T(8,128)(2,1)S(1)}, u32[]{:S(2)}, u32[]{:S(2)}) collective-permute-start(bf16[512,1024]{1,0:T(8,128)(2,1)} %get-tuple-element.178), channel_id=1, source_target_pairs={{0,16},{16,0},{1,17},{17,1},{2,18},{18,2},{3,19},{19,3},{4,20},{20... | collective-permute-start | bytes 3145736 | tf_op jit(solution)/shard_map/ppermute | solution.py:865
  398.9 14.2 %collective-permute-start.14 = (bf16[1024,2048]{1,0:T(8,128)(2,1)}, bf16[1024,2048]{1,0:T(8,128)(2,1)}, u32[]{:S(2)}, u32[]{:S(2)}) collective-permute-start(bf16[1024,2048]{1,0:T(8,128)(2,1)} %get-tuple-element.180), channel_id=1, source_target_pairs={{0,1},{1,0},{2,3},{3,2},{4,5},{5,4},{6,7},{7,6},{8,9},{9,8},{10,11... | collective-permute-start | bytes 12582920 | tf_op jit(solution)/shard_map/ppermute | solution.py:920
  398.9 20.6 %collective-permute-start.15 = (bf16[1024,2048]{1,0:T(8,128)(2,1)}, bf16[1024,2048]{1,0:T(8,128)(2,1)}, u32[]{:S(2)}, u32[]{:S(2)}) collective-permute-start(bf16[1024,2048]{1,0:T(8,128)(2,1)} %get-tuple-element.183), channel_id=1, source_target_pairs={{0,1},{1,0},{2,3},{3,2},{4,5},{5,4},{6,7},{7,6},{8,9},{9,8},{10,11... | collective-permute-start | bytes 12582920 | tf_op jit(solution)/shard_map/ppermute | solution.py:920
  402.3 31.4 %collective-permute-start.18 = (bf16[512,512]{1,0:T(8,128)(2,1)}, bf16[512,512]{1,0:T(8,128)(2,1)}, u32[]{:S(2)}, u32[]{:S(2)}) collective-permute-start(bf16[512,512]{1,0:T(8,128)(2,1)} %get-tuple-element.190), channel_id=1, source_target_pairs={{0,16},{16,0},{1,17},{17,1},{2,18},{18,2},{3,19},{19,3},{4,20},{20... | collective-permute-start | bytes 1572872 | tf_op jit(solution)/shard_map/ppermute | solution.py:865
  409.5 76.2 %all-to-all-start.4 = ((bf16[8,64,1536]{2,1,0:T(8,128)(2,1)}), bf16[8,64,1536]{2,1,0:T(8,128)(2,1)S(1)}, u32[]{:S(2)}, u32[]{:S(2)}) async-start(bf16[8,64,1536]{2,1,0:T(8,128)(2,1)} %bitcast.125), calls=%async_computation.4 | async-start | bytes 3145728 | tf_op jit(solution)/shard_map/all_to_all | solution.py:879
  429.3 49.2 %collective-permute-start.17 = (bf16[512,1024]{1,0:T(8,128)(2,1)}, bf16[512,1024]{1,0:T(8,128)(2,1)S(1)}, u32[]{:S(2)}, u32[]{:S(2)}) collective-permute-start(bf16[512,1024]{1,0:T(8,128)(2,1)} %get-tuple-element.189), channel_id=1, source_target_pairs={{0,16},{16,0},{1,17},{17,1},{2,18},{18,2},{3,19},{19,3},{4,20},{20... | collective-permute-start | bytes 3145736 | tf_op jit(solution)/shard_map/ppermute | solution.py:865
  429.4 60.2 %collective-permute-start.19 = (bf16[512,2048]{1,0:T(8,128)(2,1)}, bf16[512,2048]{1,0:T(8,128)(2,1)}, u32[]{:S(2)}, u32[]{:S(2)}) collective-permute-start(bf16[512,2048]{1,0:T(8,128)(2,1)} %get-tuple-element.194), channel_id=1, source_target_pairs={{0,4},{4,0},{1,5},{5,1},{2,6},{6,2},{3,7},{7,3},{8,12},{12,8},{9,1... | collective-permute-start | bytes 6291464 | tf_op jit(solution)/shard_map/ppermute | solution.py:920
  432.2 82.8 %collective-permute-start.20 = (bf16[512,2048]{1,0:T(8,128)(2,1)}, bf16[512,2048]{1,0:T(8,128)(2,1)}, u32[]{:S(2)}, u32[]{:S(2)}) collective-permute-start(bf16[512,2048]{1,0:T(8,128)(2,1)} %get-tuple-element.203), channel_id=1, source_target_pairs={{0,8},{8,0},{1,9},{9,1},{2,10},{10,2},{3,11},{11,3},{4,12},{12,4},... | collective-permute-start | bytes 6291464 | tf_op jit(solution)/shard_map/ppermute | solution.py:920
  485.7 8.0 %copy-start.6 = (bf16[8,64,1536]{2,1,0:T(8,128)(2,1)}, bf16[8,64,1536]{2,1,0:T(8,128)(2,1)S(1)}, u32[]{:S(2)}) copy-start(bf16[8,64,1536]{2,1,0:T(8,128)(2,1)S(1)} %all-to-all-done.4.g_ref) | copy-start | bytes 4718596
  485.7 46.6 %all-to-all-start.3 = ((bf16[8,80,1536]{2,1,0:T(8,128)(2,1)}), bf16[8,80,1536]{2,1,0:T(8,128)(2,1)S(1)}, u32[]{:S(2)}, u32[]{:S(2)}) async-start(bf16[8,80,1536]{2,1,0:T(8,128)(2,1)} %shard_map.379), calls=%async_computation.3 | async-start | bytes 3932160 | tf_op jit(solution)/shard_map/all_to_all | solution.py:879
  515.0 6.1 %copy-start.28 = (bf16[256,2048]{1,0:T(8,128)(2,1)S(1)}, bf16[256,2048]{1,0:T(8,128)(2,1)}, u32[]{:S(2)}) copy-start(bf16[256,2048]{1,0:T(8,128)(2,1)} %get-tuple-element.226) | copy-start | bytes 3145732
  519.2 38.0 %collective-permute-start.21 = (bf16[256,2048]{1,0:T(8,128)(2,1)}, bf16[256,2048]{1,0:T(8,128)(2,1)}, u32[]{:S(2)}, u32[]{:S(2)}) collective-permute-start(bf16[256,2048]{1,0:T(8,128)(2,1)} %get-tuple-element.224), channel_id=1, source_target_pairs={{0,4},{4,0},{1,5},{5,1},{2,6},{6,2},{3,7},{7,3},{8,12},{12,8},{9,1... | collective-permute-start | bytes 3145736 | tf_op jit(solution)/shard_map/ppermute | solution.py:945
  521.2 40.0 %collective-permute-start.22 = (bf16[256,2048]{1,0:T(8,128)(2,1)S(1)}, bf16[256,2048]{1,0:T(8,128)(2,1)}, u32[]{:S(2)}, u32[]{:S(2)}) collective-permute-start(bf16[256,2048]{1,0:T(8,128)(2,1)S(1)} %copy-done.28), channel_id=1, source_target_pairs={{0,8},{8,0},{1,9},{9,1},{2,10},{10,2},{3,11},{11,3},{4,12},{12,4},... | collective-permute-start | bytes 3145736 | tf_op jit(solution)/shard_map/ppermute | solution.py:945
  552.8 13.5 %collective-permute-start.23 = (f32[768]{0:T(1024)S(1)}, f32[768]{0:T(1024)S(1)}, u32[]{:S(2)}, u32[]{:S(2)}) collective-permute-start(f32[768]{0:T(1024)S(1)} %get-tuple-element.245), channel_id=1, source_target_pairs={{0,2},{2,0},{1,3},{3,1},{4,6},{6,4},{5,7},{7,5},{8,10},{10,8},{9,1... | collective-permute-start | bytes 9224 | tf_op jit(solution)/shard_map/ppermute | solution.py:1012
  554.6 11.7 %collective-permute-start.24 = (f32[768]{0:T(1024)S(1)}, f32[768]{0:T(1024)S(1)}, u32[]{:S(2)}, u32[]{:S(2)}) collective-permute-start(f32[768]{0:T(1024)S(1)} %get-tuple-element.244), channel_id=1, source_target_pairs={{0,16},{16,0},{1,17},{17,1},{2,18},{18,2},{3,19},{19,3},{4,20},{20... | collective-permute-start | bytes 9224 | tf_op jit(solution)/shard_map/ppermute | solution.py:1013
  554.6 11.7 %collective-permute-start.25 = (f32[768]{0:T(1024)S(1)}, f32[768]{0:T(1024)S(1)}, u32[]{:S(2)}, u32[]{:S(2)}) collective-permute-start(f32[768]{0:T(1024)S(1)} %get-tuple-element.243), channel_id=1, source_target_pairs={{0,18},{2,16},{16,2},{18,0},{1,19},{3,17},{17,3},{19,1},{4,22},{6,... | collective-permute-start | bytes 9224 | tf_op jit(solution)/shard_map/ppermute | solution.py:1014
  (19 other events, 39.4 us)
Sparse Core Ops, SparseCore 0:
  53.7 135.1 all-gather.2

commit v4 on v3

--- a/solution.py
+++ b/solution.py
@@ -46,8 +46,7 @@
     'back': 10,
     'far0': 20000,
     'adam1': 90,
-    'adam0in': 40,
-    'adam0out': 10,
+    'adam0': 50,
     'adam1b': 40,
     'out': 190,
     'mlp512': 150,
@@ -184,17 +183,13 @@
     )(*pieces)
 
 
-def member_copies(members_ref, team_ref, kind, buffer, sems):
-    count, both, _ = team_ref.shape
-    rows = both // 2
-    return [
-        pltpu.make_async_copy(
-            team_ref.at[members_ref[k], kind * rows : (kind + 1) * rows],
-            buffer.at[k * rows : (k + 1) * rows],
-            sems.at[k],
-        )
-        for k in range(count)
-    ]
+def member_copies(members_ref, team_refs, kind, buffer, sems):
+    rows = team_refs[0].shape[1] // 2
+    copies = []
+    for k in range(TEAM):
+        source = team_refs[k % 2].at[members_ref[k], kind * rows : (kind + 1) * rows]
+        copies.append(pltpu.make_async_copy(source, buffer.at[k * rows : (k + 1) * rows], sems.at[k]))
+    return copies
 
 
 def prepare_tokens(order, live, tokens, cotangent):
@@ -225,12 +220,11 @@
 
 
 def norm_inputs(members, team, gain_one, shift_one, gain_two, shift_two):
-    count, both, _ = team.shape
-    rows = both // 2
-
-    def kernel(members_ref, team_ref, g1, s1, g2, s2, one_ref, two_ref, hat_ref, buffer, sems):
+    count, rows = TEAM, team[0].shape[1] // 2
+
+    def kernel(members_ref, near_ref, over_ref, g1, s1, g2, s2, one_ref, two_ref, hat_ref, buffer, sems):
         step = pl.program_id(0)
-        copies = member_copies(members_ref, team_ref, 0, buffer, sems)
+        copies = member_copies(members_ref, (near_ref, over_ref), 0, buffer, sems)
 
         @pl.when(step == 0)
         def _():
@@ -254,19 +248,19 @@
         grid_spec=pltpu.PrefetchScalarGridSpec(
             num_scalar_prefetch=1,
             grid=(count,),
-            in_specs=[ANYWHERE] + [line] * 4,
+            in_specs=[ANYWHERE] * 2 + [line] * 4,
             out_specs=[blocks((rows, D), lambda i, *_: (i, 0))] * 3,
             scratch_shapes=[pltpu.VMEM((count * rows, D), bf16), pltpu.SemaphoreType.DMA((count,))],
         ),
         out_shape=[shaped((count * rows, D), bf16)] * 3,
         **params("norm"),
-    )(members, team, gain_one, shift_one, gain_two, shift_two)
-
-
-def open_chunk(step, rows, rows_dev, members_ref, team_ref, w_refs, begin, y_all, w_all, y_sems, w_sems):
-    y_copies = member_copies(members_ref, team_ref, 1, y_all, y_sems)
+    )(members, *team, gain_one, shift_one, gain_two, shift_two)
+
+
+def open_chunk(step, rows, rows_dev, members_ref, team_refs, w_refs, begin, y_all, w_all, y_sems, w_sems):
+    y_copies = member_copies(members_ref, team_refs, 1, y_all, y_sems)
     w_copies = stacked_copies(w_refs, w_all, w_sems, rows_dev, slice(begin, begin + w_all.shape[1]))
-    slots = team_ref.shape[1] // 2
+    slots = team_refs[0].shape[1] // 2
 
     @pl.when(step == 0)
     def _():
@@ -322,11 +316,11 @@
     width = 2 * cols
     nw = len(w_pieces)
 
-    def kernel(members_ref, team_ref, *refs):
-        w_refs = refs[:nw]
-        a_ref, b_ref, act_ref, dh_ref, keep_ref, send_ref, sum_ref, acc_ref, y_all, w_all, y_sems, w_sems = refs[nw:]
+    def kernel(members_ref, *refs):
+        team_refs, w_refs, refs = refs[:2], refs[2 : 2 + nw], refs[2 + nw :]
+        a_ref, b_ref, act_ref, dh_ref, keep_ref, send_ref, sum_ref, acc_ref, y_all, w_all, y_sems, w_sems = refs
         step, last = pl.program_id(0), pl.num_programs(0) - 1
-        y = open_chunk(step, rows, rows_dev, members_ref, team_ref, w_refs, begin, y_all, w_all, y_sems, w_sems)
+        y = open_chunk(step, rows, rows_dev, members_ref, team_refs, w_refs, begin, y_all, w_all, y_sems, w_sems)
         a = a_ref[...]
         act, slope = gelu_pair(dot(a, w_all[:, :cols]) + b_ref[...])
         act = act.astype(bf16)
@@ -344,13 +338,13 @@
         grid_spec=pltpu.PrefetchScalarGridSpec(
             num_scalar_prefetch=1,
             grid=(total // rows,),
-            in_specs=[ANYWHERE] * (1 + nw) + [moving(D), fixed(1, cols)],
+            in_specs=[ANYWHERE] * (2 + nw) + [moving(D), fixed(1, cols)],
             out_specs=[moving(cols), moving(cols), fixed(D // 2, width), fixed(D // 2, width), fixed(1, cols)],
-            scratch_shapes=chunk_scratch(total, width, team.shape[0], copy_count(w_pieces)),
+            scratch_shapes=chunk_scratch(total, width, TEAM, copy_count(w_pieces)),
         ),
         out_shape=[shaped((total, cols), bf16)] * 2 + [shaped((D // 2, width), bf16)] * 2 + [shaped((1, cols), f32)],
         **params(f"mlp{width}"),
-    )(members, team, *w_pieces, a, b)
+    )(members, *team, *w_pieces, a, b)
 
 
 def turn_lanes(values, cosine, low_sine, high_sine):
@@ -365,12 +359,12 @@
     slots = BLK_DEV * BLOCK
     buffers = rows // slots
 
-    def kernel(members_ref, first_ref, live_ref, team_ref, *refs):
-        w_refs = refs[:nw]
-        a_ref, b_ref, cos_ref, low_ref, high_ref, att_ref, dm_ref, keep_ref, send_ref, sum_ref = refs[nw : nw + 10]
-        acc_ref, y_all, w_all, y_sems, w_sems = refs[nw + 10 :]
+    def kernel(members_ref, first_ref, live_ref, *refs):
+        team_refs, w_refs, refs = refs[:2], refs[2 : 2 + nw], refs[2 + nw :]
+        a_ref, b_ref, cos_ref, low_ref, high_ref, att_ref, dm_ref, keep_ref, send_ref, sum_ref = refs[:10]
+        acc_ref, y_all, w_all, y_sems, w_sems = refs[10:]
         step, last = pl.program_id(0), pl.num_programs(0) - 1
-        y = open_chunk(step, rows, rows_dev, members_ref, team_ref, w_refs, begin, y_all, w_all, y_sems, w_sems)
+        y = open_chunk(step, rows, rows_dev, members_ref, team_refs, w_refs, begin, y_all, w_all, y_sems, w_sems)
         a = a_ref[...]
         mixed = dot(a, w_all[:, : 3 * HEAD]) + b_ref[...]
         datt_all = dot(y, w_all[:, 3 * HEAD :]).astype(bf16)
@@ -417,15 +411,15 @@
         grid_spec=pltpu.PrefetchScalarGridSpec(
             num_scalar_prefetch=3,
             grid=(total // rows,),
-            in_specs=[ANYWHERE] * (1 + nw) + [moving(D), fixed(1, 3 * HEAD)] + [fixed(slots, LANES)] * 3,
+            in_specs=[ANYWHERE] * (2 + nw) + [moving(D), fixed(1, 3 * HEAD)] + [fixed(slots, LANES)] * 3,
             out_specs=[moving(HEAD), moving(3 * HEAD), fixed(D // 2, width), fixed(D // 2, width), fixed(1, 3 * HEAD)],
-            scratch_shapes=chunk_scratch(total, width, team.shape[0], copy_count(w_pieces)),
+            scratch_shapes=chunk_scratch(total, width, TEAM, copy_count(w_pieces)),
         ),
         out_shape=[shaped((total, HEAD), bf16), shaped((total, 3 * HEAD), bf16)]
         + [shaped((D // 2, width), bf16)] * 2
         + [shaped((1, 3 * HEAD), f32)],
         **params("attn"),
-    )(members, first, live, team, *w_pieces, a, b, *rotary)
+    )(members, first, live, *team, *w_pieces, a, b, *rotary)
 
 
 def token_block(i, low_first):
@@ -651,36 +645,42 @@
     )(order, tokens, other, kept, got)
 
 
-def adamw_columns(got, weight, first_m, second_m, section, unit, offset, sections, role, held=None):
-    rows, width = weight.shape
-    span = TEAM * unit
+def adamw_columns(got, matrices, unit, offset, sections, role, held=None):
+    rows = matrices[0][1].shape[0]
+    count, span = len(matrices), TEAM * unit
     part = max(rows // 4, 16) if rows % 16 == 0 else rows
-    got_spec = blocks((TEAM, part, unit), lambda k, i: (0, i, section + k))
     full = blocks((part, span), lambda k, i: (i, offset + k))
 
-    def kernel(g_ref, w_ref, m_ref, u_ref, *refs):
-        grad_ref, new_ref, mo_ref, uo_ref = refs[-4:]
-        for k in range(TEAM):
-            here = slice(k * unit, (k + 1) * unit)
-            grad = g_ref[k].astype(f32)
-            new, m_new, u_new = adamw_update(
-                w_ref[:, here], grad, m_ref[:, here], u_ref[:, here], learn_rate, decay_matrix
-            )
-            grad_ref[:, here] = grad
-            new_ref[:, here] = new
-            mo_ref[:, here] = m_new
-            uo_ref[:, here] = u_new
-
+    def kernel(*refs):
+        ins, outs = refs[: 4 * count], refs[-4 * count :]
+        for j in range(count):
+            g_ref, w_ref, m_ref, u_ref = ins[4 * j : 4 * j + 4]
+            grad_ref, new_ref, mo_ref, uo_ref = outs[4 * j : 4 * j + 4]
+            for k in range(TEAM):
+                here = slice(k * unit, (k + 1) * unit)
+                grad = g_ref[k].astype(f32)
+                new, m_new, u_new = adamw_update(
+                    w_ref[:, here], grad, m_ref[:, here], u_ref[:, here], learn_rate, decay_matrix
+                )
+                grad_ref[:, here] = grad
+                new_ref[:, here] = new
+                mo_ref[:, here] = m_new
+                uo_ref[:, here] = u_new
+
+    specs, args = [], []
+    for section, *arrays in matrices:
+        specs += [blocks((TEAM, part, unit), lambda k, i, s=section: (0, i, s + k)), full, full, full]
+        args += [got, *arrays]
     extra = list(held) if held is not None else []
     return pl.pallas_call(
         kernel,
         grid=(sections, rows // part),
-        in_specs=[got_spec, full, full, full] + [ANYWHERE] * len(extra),
-        out_specs=[full] * 4,
-        out_shape=[shaped((rows, width), f32)] * 4,
-        input_output_aliases={4 + k: k for k in range(len(extra))},
+        in_specs=specs + [ANYWHERE] * len(extra),
+        out_specs=[full] * (4 * count),
+        out_shape=[shaped(w.shape, f32) for _, w, _, _ in matrices for _ in range(4)],
+        input_output_aliases={4 * count + k: k for k in range(len(extra))},
         **params(role),
-    )(got, weight, first_m, second_m, *extra)
+    )(*args, *extra)
 
 
 def body(
@@ -761,6 +761,7 @@
         both_send = prepare_tokens(to_local, block_live, tokens, cotangent)
     else:
         both_send = prepare_tokens(to_local, block_live, local_order(tokens), local_order(cotangent))
+    both_low = lax.ppermute(both_send, "low", SWAP)
     owns, far_got, load_of, begin_of = [], [None] * len(LOADS), {}, {}
     for load, chunks in enumerate(LOADS):
         parts, begin = [], 0
@@ -772,14 +773,20 @@
         if load == 0 and paired:
             extra = jnp.pad(payload, (0, PACK_ROWS * begin - payload.shape[0])).reshape(1, PACK_ROWS, begin)
             block = jnp.concatenate([block, jnp.broadcast_to(extra, (TEAM, PACK_ROWS, begin))], axis=1)
-        waits = owns[-1:]
+        waits = owns[-1:] if load else [both_send]
         if paired and load == 1:
             far_got[0] = lax.ppermute(owns[0], "far", SWAP)
+        if paired and load == 2:
+            far_got[0] = lax.ppermute(owns[0], "far", SWAP)
+            both_low = after(both_low, owns[1], far_got[0])
+            waits = waits + [far_got[0]]
         got = lax.all_to_all(after(block, *waits) if waits else block, NEAR, 0, 0, tiled=True)
         owns.append(got if got.shape[1] != rows_dev else got.reshape(rows_team, got.shape[2]))
 
-    team = lax.all_gather(both_send, NEAR, axis=0, tiled=False)
-    members = jnp.array([4 * l + 2 * r + c for c in range(2) for r in range(2) for l in range(2)], jnp.int32) ^ me
+    team = [lax.all_gather(v, ("row", "core"), axis=0, tiled=False) for v in (both_send, both_low)]
+    order = jnp.array([4 * l + 2 * r + c for c in range(2) for r in range(2) for l in range(2)], jnp.int32)
+    near_members = order ^ me
+    members = near_members % 4
 
     loads = []
 
@@ -805,7 +812,7 @@
 
     length = piece + 2 * BLK_DEV
     if paired:
-        parts = lax.optimization_barrier((*loads[0], owns[2], far_got[1]))[:4]
+        parts = lax.optimization_barrier((*loads[0], owns[2], far_got[1], *team))[:4]
         got = extra_rows(parts, rows_dev).reshape(4, TEAM, -1)[:, :, :length]
         mine = got[0]
         got = flips(got.reshape(2, 2, half, 2, length), 0, 1)
@@ -813,7 +820,7 @@
     else:
         everyone = lax.all_gather(payload, EVERY, axis=0, tiled=False).reshape(-1, length)
         mine = lax.all_gather(payload, NEAR, axis=0, tiled=False).reshape(TEAM, length)
-    tables = mine[members, piece:].astype(f32).astype(jnp.int32)
+    tables = mine[near_members, piece:].astype(f32).astype(jnp.int32)
     first_table, live_table = tables[:, :BLK_DEV], tables[:, BLK_DEV:]
     vec_full = everyone[:, :piece].astype(f32).reshape(VEC)
     b_query, b_value, b_att, b_in, b_mlp, *norm_vectors = split_vectors(vec_full)
@@ -884,14 +891,21 @@
         chunk = CHUNKS[index]
         got = after(got, *tokens)
         if chunk is None:
-            held["qkv"] = adamw_columns(got, w_qkv, first_qkv, second_qkv, start // HEAD, HEAD, 0, 3, "adam1")
-            held["att"] = adamw_columns(got, w_attn_out, first_attn_out, second_attn_out, start // HEAD + 3, HEAD, 0, 1, "adam1b")
+            held["qkv"] = adamw_columns(
+                got, [(start // HEAD, w_qkv, first_qkv, second_qkv)], HEAD, 0, 3, "adam1"
+            )
+            held["att"] = adamw_columns(
+                got, [(start // HEAD + 3, w_attn_out, first_attn_out, second_attn_out)], HEAD, 0, 1, "adam1b"
+            )
             return held["qkv"][0], held["att"][0]
         begin, end = chunk
         unit = end - begin
-        for kind, name, arrays in ((0, "in", (w_mlp_in, first_mlp_in, second_mlp_in)), (1, "out", (w_mlp_out, first_mlp_out, second_mlp_out))):
-            held[name] = adamw_columns(got, *arrays, start // unit + kind, unit, begin // unit, 1, f"adam{index}{name}", held.get(name))
-        return held["in"][0], held["out"][0]
+        pair = [
+            (start // unit, w_mlp_in, first_mlp_in, second_mlp_in),
+            (start // unit + 1, w_mlp_out, first_mlp_out, second_mlp_out),
+        ]
+        held["mlp"] = adamw_columns(got, pair, unit, begin // unit, 1, f"adam{index}", held.get("mlp"))
+        return (held["mlp"][0],)
 
     w_of_chunk = [loads[load_of[index]] for index in range(count)]
     attn_index = CHUNKS.index(None)
@@ -1019,8 +1033,7 @@
     new_vec, m_vec, u_vec = adamw_update(vectors, grad_vectors, first_vectors, second_vectors, vector_rate, 0.0)
     grad_qkv, new_qkv, m_qkv, u_qkv = held["qkv"]
     grad_attn_out, new_att, m_att, u_att = held["att"]
-    grad_mlp_in, new_in, m_in, u_in = held["in"]
-    grad_mlp_out, new_out, m_out, u_out = held["out"]
+    grad_mlp_in, new_in, m_in, u_in, grad_mlp_out, new_out, m_out, u_out = held["mlp"]
     return (
         out,
         grad_tokens,

time: 585 us -> 579 us (0.990)
  Pallas kernels: 270 us -> 261 us
    ppermute x1, waiting for transfers between devices: 37.8 us -> 57.5 us  [body(): far_got[0] = lax.ppermute(owns[0], 'far', SWAP)]
    all_gather x1 -> x2, waiting for transfers between devices: 23.8 us -> 14.2 us  [body(): lax.all_gather(v, ('row', 'core'), axis=0, tiled=False)]
    all_to_all x3, waiting for transfers between devices: 15.3 us -> 6.23 us  [body(): lax.all_to_all(after(block, *waits) if waits else block, NEAR, 0, 0, tile...]
    pallas_call x8 -> x5, Pallas kernels: 39 us -> 30.3 us  [adamw_columns(): pl.pallas_call(kernel, grid=(sections, rows // part), in_specs=specs + [A...]
    ppermute x2, starting transfers between devices: 6.61 us -> 0.6 us  [send_far(): lax.ppermute(after(owns[load], *waits) if waits else owns[load], 'far', S...]
    unnamed x79 -> x77, local copies, waits for them, and re-layouts: 12.9 us -> 16.1 us
  transfers between devices with their start and end apart: 32 -> 34, of which waited for: 9 -> 9; matrix products, arithmetic and copies ran while one was open for 7% -> 7% of each run, Pallas kernels for 47% -> 45%
where the time goes in v4:
time: 579 us; the launch traced here: 569 us
  Pallas kernels  261 us (45%)
  waiting for transfers between devices  187 us (32%)
  starting transfers between devices  55.2 us (10%)
  local copies, waits for them, and re-layouts  35.1 us (6%)
  between operations  15.2 us (3%)
  other arithmetic  15 us (3%)
    pallas_call x3, Pallas kernels, mlp_chunk(): pl.pallas_call(kernel, grid_spec=pltpu.PrefetchScalarGridSpec(num_scalar_...  70.8 us
    ppermute x1, waiting for transfers between devices, body(): far_got[0] = lax.ppermute(owns[0], 'far', SWAP)  57.5 us
    ppermute x2, waiting for transfers between devices, send_far(): lax.ppermute(after(owns[load], *waits) if waits else owns[load], 'far', S...  48.2 us
    ppermute x4, waiting for transfers between devices, sum_columns(): grouped[index] = (kept, lax.ppermute(sent, 'far', SWAP))  44.4 us
    pallas_call x1, Pallas kernels, attn_chunk(): pl.pallas_call(kernel, grid_spec=pltpu.PrefetchScalarGridSpec(num_scalar_...  36.3 us
    pallas_call x8, Pallas kernels, split_sum(): pl.pallas_call(kernel, grid=(steps,), in_specs=[low, high, low, high], ou...  32.7 us
    pallas_call x1, Pallas kernels, back_part(): pl.pallas_call(kernel, grid=(TEAM,), in_specs=[ANYWHERE] * (count * per)...  32.4 us
    pallas_call x5, Pallas kernels, adamw_columns(): pl.pallas_call(kernel, grid=(sections, rows // part), in_specs=specs + [A...  30.3 us
  transfers between devices with their start and end apart: 34, of which 9 were waited for; matrix products, arithmetic and copies ran while one was open for 7% of the time, Pallas kernels for 45%

profile of v4, /device:TPU:0, one launch (start us, length us, event | category | flops | bytes accessed | tf_op | source)
XLA Modules:
  0.0 568.5 jit_solution(8517263023218836497)
XLA Ops:
  7.8 4.1 shard_map.363
  16.9 5.3 all-to-all-start
  22.1 2.0 collective-permute-start
  29.1 2.2 pad_maximum_fusion.1
  31.3 4.2 all-to-all-done.refs_0_.refs_2_
  35.5 4.2 all-to-all-start.1
  39.8 3.4 collective-permute-start.1
  43.2 57.5 %collective-permute-done.1.refs_1_.refs_3_ = bf16[8,80,512]{2,1,0:T(8,128)(2,1)S(1)} collective-permute-done((bf16[8,80,512]{2,1,0:T(8,128)(2,1)}, bf16[8,80,512]{2,1,0:T(8,128)(2,1)S(1)}, u32[]{:S(2)}, u32[]{:S(2)}) %collective-permute-start.1) | collective-permute-done | bytes 655392 | tf_op jit(solution)/shard_map/ppermute | solution.py:780
  100.7 2.0 all-to-all-done.1
  105.2 5.4 all-to-all-start.2
  116.8 1.9 convert_reduce_fusion
  120.5 40.6 %collective-permute-done.2.refs_3_.refs_5_ = bf16[512,1024]{1,0:T(8,128)(2,1)} collective-permute-done((bf16[512,1024]{1,0:T(8,128)(2,1)}, bf16[512,1024]{1,0:T(8,128)(2,1)}, u32[]{:S(2)}, u32[]{:S(2)}) %collective-permute-start.2) | collective-permute-done | bytes 1048608 | tf_op jit(solution)/shard_map/ppermute | solution.py:794
  163.2 14.2 %all-gather.7.cloned.1.call-done = bf16[2048,2048]{1,0:T(8,128)(2,1)} async-done(((bf16[512,2048]{1,0:T(8,128)(2,1)}), bf16[2048,2048]{1,0:T(8,128)(2,1)}) %all-gather.7.cloned.1.call-update) | async-done | bytes 8388624 | tf_op jit(solution)/shard_map/all_gather | solution.py:786
  177.4 1.9 shard_map.364
  184.2 14.2 %shard_map.365 = (bf16[2048,2048]{1,0:T(8,128)(2,1)}, bf16[2048,2048]{1,0:T(8,128)(2,1)}, bf16[2048,2048]{1,0:T(8,128)(2,1)}) custom-call(s32[8]{0:T(128)} %get-tuple-element.287.members_ref, bf16[4,512,2048]{2,1,0:T(8,128)(2,1)} %bitcast.150, bf16[4,512,2048]{2,1,0:T(8,128)(2,1)} %bitcast.155, f32[1,2048]{1,0:T(1,128)} %bitcast.133, f32[1,2048]{1,0:T(1,128)} %bitcast.136, ...), custom_call_target="tpu_custom_call" | custom-call | flops 10000000000 | bytes 1024 | tf_op jit(solution)/shard_map/pallas_call | solution.py:246
  198.5 20.1 %shard_map.366 = (bf16[2048,256]{1,0:T(8,128)(2,1)}, bf16[2048,256]{1,0:T(8,128)(2,1)}, bf16[1024,512]{1,0:T(8,128)(2,1)}, bf16[1024,512]{1,0:T(8,128)(2,1)}, f32[1,256]{1,0:T(1,128)}) custom-call(s32[8]{0:T(128)} %get-tuple-element.287.members_ref, bf16[4,512,2048]{2,1,0:T(8,128)(2,1)} %bitcast.151, bf16[4,512,2048]{2,1,0:T(8,128)(2,1)} %bitcast.156, ...), custom_call_target="tpu_custom_call" | custom-call | flops 15000000512 | bytes 1024 | tf_op jit(solution)/shard_map/pallas_call | solution.py:336
  224.5 7.6 %collective-permute-done.3.refs_3_.refs_9_.refs_13_ = bf16[512,1536]{1,0:T(8,128)(2,1)} collective-permute-done((bf16[512,1536]{1,0:T(8,128)(2,1)}, bf16[512,1536]{1,0:T(8,128)(2,1)}, u32[]{:S(2)}, u32[]{:S(2)}) %collective-permute-start.3) | collective-permute-done | bytes 1572896 | tf_op jit(solution)/shard_map/ppermute | solution.py:794
  234.6 36.3 %shard_map.367 = (bf16[2048,256]{1,0:T(8,128)(2,1)}, bf16[2048,768]{1,0:T(8,128)(2,1)}, bf16[1024,1024]{1,0:T(8,128)(2,1)}, bf16[1024,1024]{1,0:T(8,128)(2,1)}, f32[1,768]{1,0:T(1,128)}) custom-call(s32[8]{0:T(128)} %get-tuple-element.287.members_ref, s32[8,2]{1,0:T(8,128)} %get-tuple-element.278.first_ref, s32[8,2]{1,0:T(8,128)} %get-tuple-element.277.live_ref, ...), custom_call_target="tpu_custom_call" | custom-call | flops 30000001024 | bytes 1024 | tf_op jit(solution)/shard_map/pallas_call | solution.py:409
  276.7 2.4 shard_map.368
  279.2 3.8 collective-permute-done.7.refs_5_.refs_11_.refs_15_
  284.0 31.1 %shard_map.369 = (bf16[2048,512]{1,0:T(8,128)(2,1)}, bf16[2048,512]{1,0:T(8,128)(2,1)}, bf16[1024,1024]{1,0:T(8,128)(2,1)}, bf16[1024,1024]{1,0:T(8,128)(2,1)}, f32[1,512]{1,0:T(1,128)}) custom-call(s32[8]{0:T(128)} %get-tuple-element.287.members_ref, bf16[4,512,2048]{2,1,0:T(8,128)(2,1)} %bitcast.153, bf16[4,512,2048]{2,1,0:T(8,128)(2,1)} %bitcast.158, ...), custom_call_target="tpu_custom_call" | custom-call | flops 1999999991808 | bytes 1024 | tf_op jit(solution)/shard_map/pallas_call | solution.py:336
  315.2 19.7 %shard_map.370 = (bf16[2048,256]{1,0:T(8,128)(2,1)}, bf16[2048,256]{1,0:T(8,128)(2,1)}, bf16[1024,512]{1,0:T(8,128)(2,1)}, bf16[1024,512]{1,0:T(8,128)(2,1)}, f32[1,256]{1,0:T(1,128)}) custom-call(s32[8]{0:T(128)} %get-tuple-element.287.members_ref, bf16[4,512,2048]{2,1,0:T(8,128)(2,1)} %bitcast.154, bf16[4,512,2048]{2,1,0:T(8,128)(2,1)} %bitcast.159, ...), custom_call_target="tpu_custom_call" | custom-call | flops 15000000512 | bytes 1024 | tf_op jit(solution)/shard_map/pallas_call | solution.py:336
  339.9 3.5 shard_map.371
  343.8 19.6 %shard_map.372 = (bf16[1024,2048]{1,0:T(8,128)(2,1)}, bf16[1024,2048]{1,0:T(8,128)(2,1)}) custom-call(bf16[8,80,512]{2,1,0:T(8,128)(2,1)} %all-to-all-done.refs_0_.refs_2_, bf16[8,80,512]{2,1,0:T(8,128)(2,1)} %copy-done.10, bf16[8,80,512]{2,1,0:T(8,128)(2,1)} %copy-done.11, bf16[8,80,512]{2,1,0:T(8,128)(2,1)} %copy-done.12, ...), custom_call_target="tpu_custom_call" | custom-call | flops 19000000512 | bytes 1024 | tf_op jit(solution)/shard_map/pallas_call | solution.py:485
  363.4 32.4 %shard_map.373 = (bf16[1024,2048]{1,0:T(8,128)(2,1)}, bf16[1024,2048]{1,0:T(8,128)(2,1)}, f32[8,2048]{1,0:T(8,128)}) custom-call(bf16[8,80,512]{2,1,0:T(8,128)(2,1)} %all-to-all-done.refs_0_.refs_2_, bf16[8,80,512]{2,1,0:T(8,128)(2,1)} %copy-done.10, bf16[8,80,512]{2,1,0:T(8,128)(2,1)} %copy-done.11, bf16[8,80,512]{2,1,0:T(8,128)(2,1)} %copy-done.12, ...), custom_call_target="tpu_custom_call" | custom-call | flops 1000000000 | bytes 1024 | tf_op jit(solution)/shard_map/pallas_call | solution.py:531
  400.1 2.4 shard_map.374
  402.6 2.5 collective-permute-start.19
  406.1 3.3 shard_map.375
  409.4 3.6 all-to-all-start.4
  413.0 6.4 %shard_map.376 = (f32[512,2048]{1,0:T(8,128)}, bf16[512,2048]{1,0:T(8,128)(2,1)}) custom-call(bf16[1024,2048]{1,0:T(8,128)(2,1)} %get-tuple-element.183.l_low.l_high, bf16[1024,2048]{1,0:T(8,128)(2,1)} %get-tuple-element.183.l_low.l_high, bf16[1024,2048]{1,0:T(8,128)(2,1)} %collective-permute-done.15.r_low.r_high, ...), custom_call_target="tpu_custom_call" | custom-call | flops 100000000 | bytes 1024 | tf_op jit(solution)/shard_map/pallas_call | solution.py:555
  419.4 6.3 %shard_map.377 = (f32[512,2048]{1,0:T(8,128)}, bf16[512,2048]{1,0:T(8,128)(2,1)}) custom-call(bf16[1024,2048]{1,0:T(8,128)(2,1)} %get-tuple-element.186.l_low.l_high, bf16[1024,2048]{1,0:T(8,128)(2,1)} %get-tuple-element.186.l_low.l_high, bf16[1024,2048]{1,0:T(8,128)(2,1)} %collective-permute-done.16.r_low.r_high, ...), custom_call_target="tpu_custom_call" | custom-call | flops 1000000000 | bytes 1024 | tf_op jit(solution)/shard_map/pallas_call | solution.py:555
  425.7 3.5 shard_map.378
  429.7 1.9 collective-permute-start.20
  434.0 44.4 %collective-permute-done.18.refs_2_ = bf16[512,1024]{1,0:T(8,128)(2,1)S(1)} collective-permute-done((bf16[512,1024]{1,0:T(8,128)(2,1)}, bf16[512,1024]{1,0:T(8,128)(2,1)S(1)}, u32[]{:S(2)}, u32[]{:S(2)}) %collective-permute-start.18) | collective-permute-done | bytes 1048608 | tf_op jit(solution)/shard_map/ppermute | solution.py:872
  479.4 6.2 %shard_map.379 = bf16[8,80,1536]{2,1,0:T(8,128)(2,1)} custom-call(f32[512,1024]{1,0:T(8,128)} %get-tuple-element.192.refs_0_, f32[512,512]{1,0:T(8,128)} %get-tuple-element.179.refs_1_, bf16[512,1024]{1,0:T(8,128)(2,1)} %copy-done.30, bf16[512,512]{1,0:T(8,128)(2,1)} %collective-permute-done.19.refs_3_, bf16[8,16,1536]{2,1,0:T(8,128)(2,1)} %bitcast.127), custom_call_target="tpu_custom_call" | custom-call | flops 3000000000 | bytes 1024 | tf_op jit(solution)/shard_map/pallas_call | solution.py:603
  485.6 3.9 all-to-all-start.3
  489.5 4.1 shard_map.380
  493.6 3.9 shard_map.382
  497.5 9.5 %shard_map.381 = (f32[64,6144]{1,0:T(8,128)}, f32[64,6144]{1,0:T(8,128)}, f32[64,6144]{1,0:T(8,128)}, f32[64,6144]{1,0:T(8,128)}) custom-call(bf16[8,64,1536]{2,1,0:T(8,128)(2,1)} %copy-done.7, f32[64,6144]{1,0:T(8,128)} %refs_1_.5, f32[64,6144]{1,0:T(8,128)} %refs_2_.5, f32[64,6144]{1,0:T(8,128)} %refs_3_.5), custom_call_target="tpu_custom_call" | custom-call | flops 8999999488 | bytes 1024 | tf_op jit(solution)/shard_map/pallas_call | solution.py:675
  507.1 4.9 shard_map.383
  512.0 4.2 shard_map.384
  516.1 2.0 collective-permute-start.22
  519.6 12.6 %all-to-all-done.3.refs_0_.refs_4_ = bf16[8,80,1536]{2,1,0:T(8,128)(2,1)S(1)} async-done(((bf16[8,80,1536]{2,1,0:T(8,128)(2,1)}), bf16[8,80,1536]{2,1,0:T(8,128)(2,1)S(1)}, u32[]{:S(2)}, u32[]{:S(2)}) %all-to-all-start.3) | async-done | bytes 1966112 | tf_op jit(solution)/shard_map/all_to_all | solution.py:886
  533.4 7.1 %shard_map.385 = (f32[64,8192]{1,0:T(8,128)}, f32[64,8192]{1,0:T(8,128)}, f32[64,8192]{1,0:T(8,128)}, f32[64,8192]{1,0:T(8,128)}, f32[64,8192]{1,0:T(8,128)}, /*...) custom-call(bf16[8,80,1536]{2,1,0:T(8,128)(2,1)} %copy-done, ...), custom_call_target="tpu_custom_call", output_to_operand_aliasing={{0}: (8, {}), {1}: (9, {}), {2}: (10, {}), {3}: (11, {}), {... | custom-call | flops 100000000 | bytes 1024 | tf_op jit(solution)/shard_map/pallas_call | solution.py:675
  540.6 4.9 shard_map.386
  548.6 2.9 collective-permute-start.26
  551.4 3.9 shard_map.387
  555.4 5.1 shard_map.388
  (235 shorter events, 64.3 us)
Async XLA Ops:
  7.2 156.0 %all-gather.5.cloned.1.call-start = ((), (), s32[]{:S(2)}) async-start(), calls=%async_computation.5 | async-start | bytes 10485760 | tf_op jit(solution)/shard_map/all_gather | solution.py:786
  14.3 88.5 %copy-start.4 = (bf16[64,8192]{1,0:T(8,128)(2,1)}, bf16[64,8192]{1,0:T(8,128)(2,1)S(1)}, u32[]{:S(2)}) copy-start(bf16[64,8192]{1,0:T(8,128)(2,1)S(1)} %convert.11) | copy-start | bytes 3145732
  16.9 18.6 %all-to-all-start = ((bf16[8,80,512]{2,1,0:T(8,128)(2,1)}), bf16[8,80,512]{2,1,0:T(8,128)(2,1)}, u32[]{:S(2)}, u32[]{:S(2)}) async-start(bf16[8,80,512]{2,1,0:T(8,128)(2,1)} %pad_maximum_fusion.2), calls=%async_computation | async-start | bytes 1310720 | tf_op jit(solution)/shard_map/all_to_all | solution.py:783
  22.1 78.5 %collective-permute-start = (bf16[512,2048]{1,0:T(8,128)(2,1)}, bf16[512,2048]{1,0:T(8,128)(2,1)}, u32[]{:S(2)}, u32[]{:S(2)}) collective-permute-start(bf16[512,2048]{1,0:T(8,128)(2,1)} %shard_map.363), channel_id=1, source_target_pairs={{0,8},{8,0},{1,9},{9,1},{2,10},{10,2},{3,11},{11,3},{4,12},{12,4},... | collective-permute-start | bytes 6291464 | tf_op jit(solution)/shard_map/ppermute | solution.py:764
  35.5 67.2 %all-to-all-start.1 = ((bf16[8,64,1024]{2,1,0:T(8,128)(2,1)}), bf16[8,64,1024]{2,1,0:T(8,128)(2,1)}, u32[]{:S(2)}, u32[]{:S(2)}) async-start(bf16[8,64,1024]{2,1,0:T(8,128)(2,1)} %pad_maximum_fusion.1), calls=%async_computation.1 | async-start | bytes 2097152 | tf_op jit(solution)/shard_map/all_to_all | solution.py:783
  39.8 137.6 %all-gather.7.cloned.1.call-start = ((), (), s32[]{:S(2)}) async-start(), calls=%async_computation.6 | async-start | bytes 10485760 | tf_op jit(solution)/shard_map/all_gather | solution.py:786
  39.8 60.9 %collective-permute-start.1 = (bf16[8,80,512]{2,1,0:T(8,128)(2,1)}, bf16[8,80,512]{2,1,0:T(8,128)(2,1)S(1)}, u32[]{:S(2)}, u32[]{:S(2)}) collective-permute-start(bf16[8,80,512]{2,1,0:T(8,128)(2,1)} %all-to-all-done.refs_0_.refs_2_), channel_id=1, source_target_pairs={{0,16},{16,0},{1,17},{17,1},{2,18},{18,2},{3,19},{19,3},{4,20},{20... | collective-permute-start | bytes 1966088 | tf_op jit(solution)/shard_map/ppermute | solution.py:780
  100.7 14.0 %copy-start.10 = (bf16[8,80,512]{2,1,0:T(8,128)(2,1)}, bf16[8,80,512]{2,1,0:T(8,128)(2,1)S(1)}, u32[]{:S(2)}) copy-start(bf16[8,80,512]{2,1,0:T(8,128)(2,1)S(1)} %collective-permute-done.1.refs_1_.refs_3_) | copy-start | bytes 1966084
  105.2 11.6 %copy-start.8 = (bf16[256,2048]{1,0:T(8,128)(2,1)S(1)}, bf16[256,2048]{1,0:T(8,128)(2,1)}, u32[]{:S(2)}) copy-start(bf16[256,2048]{1,0:T(8,128)(2,1)} %y_ref.1) | copy-start | bytes 3145732
  105.2 57.4 %all-to-all-start.2 = ((bf16[8,64,1536]{2,1,0:T(8,128)(2,1)}), bf16[8,64,1536]{2,1,0:T(8,128)(2,1)}, u32[]{:S(2)}, u32[]{:S(2)}) async-start(bf16[8,64,1536]{2,1,0:T(8,128)(2,1)} %pad_maximum_fusion), calls=%async_computation.2 | async-start | bytes 3145728 | tf_op jit(solution)/shard_map/all_to_all | solution.py:783
  111.8 49.3 %collective-permute-start.2 = (bf16[512,1024]{1,0:T(8,128)(2,1)}, bf16[512,1024]{1,0:T(8,128)(2,1)}, u32[]{:S(2)}, u32[]{:S(2)}) collective-permute-start(bf16[512,1024]{1,0:T(8,128)(2,1)} %bitcast.5.refs_2_.refs_4_), channel_id=1, source_target_pairs={{0,16},{16,0},{1,17},{17,1},{2,18},{18,2},{3,19},{19,3},{4,20},{20... | collective-permute-start | bytes 3145736 | tf_op jit(solution)/shard_map/ppermute | solution.py:794
  112.9 50.2 %collective-permute-start.5 = (bf16[8,80,512]{2,1,0:T(8,128)(2,1)}, bf16[8,80,512]{2,1,0:T(8,128)(2,1)S(1)}, u32[]{:S(2)}, u32[]{:S(2)}) collective-permute-start(bf16[8,80,512]{2,1,0:T(8,128)(2,1)} %all-to-all-done.refs_0_.refs_2_), channel_id=1, source_target_pairs={{0,2},{2,0},{1,3},{3,1},{4,6},{6,4},{5,7},{7,5},{8,10},{10,8},{9,1... | collective-permute-start | bytes 1966088 | tf_op jit(solution)/shard_map/ppermute | solution.py:804
  114.7 48.5 %collective-permute-start.6 = (bf16[8,80,512]{2,1,0:T(8,128)(2,1)S(1)}, bf16[8,80,512]{2,1,0:T(8,128)(2,1)S(1)}, u32[]{:S(2)}, u32[]{:S(2)}) collective-permute-start(bf16[8,80,512]{2,1,0:T(8,128)(2,1)S(1)} %collective-permute-done.1.refs_1_.refs_3_), channel_id=1, source_target_pairs={{0,2},{2,0},{1,3},{3,1},{4,6},{6,4},{5,7},{7,5},{8,10},{10,8},{9,1... | collective-permute-start | bytes 1966088 | tf_op jit(solution)/shard_map/ppermute | solution.py:800
  118.7 115.8 %collective-permute-start.8 = (bf16[512,1024]{1,0:T(8,128)(2,1)}, bf16[512,1024]{1,0:T(8,128)(2,1)}, u32[]{:S(2)}, u32[]{:S(2)}) collective-permute-start(bf16[512,1024]{1,0:T(8,128)(2,1)} %bitcast.5.refs_2_.refs_4_), channel_id=1, source_target_pairs={{0,2},{2,0},{1,3},{3,1},{4,6},{6,4},{5,7},{7,5},{8,10},{10,8},{9,1... | collective-permute-start | bytes 3145736 | tf_op jit(solution)/shard_map/ppermute | solution.py:804
  161.1 73.5 %collective-permute-start.9 = (bf16[512,1024]{1,0:T(8,128)(2,1)}, bf16[512,1024]{1,0:T(8,128)(2,1)}, u32[]{:S(2)}, u32[]{:S(2)}) collective-permute-start(bf16[512,1024]{1,0:T(8,128)(2,1)} %collective-permute-done.2.refs_3_.refs_5_), channel_id=1, source_target_pairs={{0,2},{2,0},{1,3},{3,1},{4,6},{6,4},{5,7},{7,5},{8,10},{10,8},{9,1... | collective-permute-start | bytes 3145736 | tf_op jit(solution)/shard_map/ppermute | solution.py:800
  162.7 116.5 %collective-permute-start.4 = (bf16[512,1536]{1,0:T(8,128)(2,1)}, bf16[512,1536]{1,0:T(8,128)(2,1)}, u32[]{:S(2)}, u32[]{:S(2)}) collective-permute-start(bf16[512,1536]{1,0:T(8,128)(2,1)} %bitcast.11.refs_2_.refs_8_.refs_12_), channel_id=1, source_target_pairs={{0,2},{2,0},{1,3},{3,1},{4,6},{6,4},{5,7},{7,5},{8,10},{10,8},{9,1... | collective-permute-start | bytes 4718600 | tf_op jit(solution)/shard_map/ppermute | solution.py:804
  163.2 14.2 %copy-start.11 = (bf16[8,80,512]{2,1,0:T(8,128)(2,1)}, bf16[8,80,512]{2,1,0:T(8,128)(2,1)S(1)}, u32[]{:S(2)}) copy-start(bf16[8,80,512]{2,1,0:T(8,128)(2,1)S(1)} %collective-permute-done.5.refs_2_.refs_4_) | copy-start | bytes 1966084
  163.2 69.0 %collective-permute-start.3 = (bf16[512,1536]{1,0:T(8,128)(2,1)}, bf16[512,1536]{1,0:T(8,128)(2,1)}, u32[]{:S(2)}, u32[]{:S(2)}) collective-permute-start(bf16[512,1536]{1,0:T(8,128)(2,1)} %bitcast.11.refs_2_.refs_8_.refs_12_), channel_id=1, source_target_pairs={{0,16},{16,0},{1,17},{17,1},{2,18},{18,2},{3,19},{19,3},{4,20},{20... | collective-permute-start | bytes 4718600 | tf_op jit(solution)/shard_map/ppermute | solution.py:794
  163.2 14.2 %copy-start.12 = (bf16[8,80,512]{2,1,0:T(8,128)(2,1)}, bf16[8,80,512]{2,1,0:T(8,128)(2,1)S(1)}, u32[]{:S(2)}) copy-start(bf16[8,80,512]{2,1,0:T(8,128)(2,1)S(1)} %collective-permute-done.6.refs_3_.refs_5_) | copy-start | bytes 1966084
  198.5 20.1 %copy-start.19 = (s32[8]{0:T(128)S(1)}, s32[8]{0:T(128)}, u32[]{:S(2)}) copy-start(s32[8]{0:T(128)} %get-tuple-element.289) | copy-start | bytes 100
  198.5 20.9 %copy-start.18 = (s32[8]{0:T(128)S(1)}, s32[8]{0:T(128)}, u32[]{:S(2)}) copy-start(s32[8]{0:T(128)} %get-tuple-element.288) | copy-start | bytes 100
  198.5 21.6 %copy-start.17 = (s32[8]{0:T(128)S(1)}, s32[8]{0:T(128)}, u32[]{:S(2)}) copy-start(s32[8]{0:T(128)} %get-tuple-element.291) | copy-start | bytes 100
  198.5 22.4 %copy-start.16 = (s32[8]{0:T(128)S(1)}, s32[8]{0:T(128)}, u32[]{:S(2)}) copy-start(s32[8]{0:T(128)} %get-tuple-element.290) | copy-start | bytes 100
  223.0 52.7 %collective-permute-start.10 = (bf16[1024,512]{1,0:T(8,128)(2,1)}, bf16[1024,512]{1,0:T(8,128)(2,1)S(1)}, u32[]{:S(2)}, u32[]{:S(2)}) collective-permute-start(bf16[1024,512]{1,0:T(8,128)(2,1)} %get-tuple-element.152), channel_id=1, source_target_pairs={{0,2},{2,0},{1,3},{3,1},{4,6},{6,4},{5,7},{7,5},{8,10},{10,8},{9,1... | collective-permute-start | bytes 3145736 | tf_op jit(solution)/shard_map/ppermute | solution.py:860
  232.1 50.8 %collective-permute-start.7 = (bf16[512,1536]{1,0:T(8,128)(2,1)}, bf16[512,1536]{1,0:T(8,128)(2,1)S(1)}, u32[]{:S(2)}, u32[]{:S(2)}) collective-permute-start(bf16[512,1536]{1,0:T(8,128)(2,1)} %collective-permute-done.3.refs_3_.refs_9_.refs_13_), channel_id=1, source_target_pairs={{0,2},{2,0},{1,3},{3,1},{4,6},{6,4},{5,7},{7,5},{8,10},{10,8},{9,1... | collective-permute-start | bytes 4718600 | tf_op jit(solution)/shard_map/ppermute | solution.py:800
  234.6 38.5 %copy-start.25 = (f32[1,256]{1,0:T(1,128)S(1)}, f32[1,256]{1,0:T(1,128)}, u32[]{:S(2)}) copy-start(f32[1,256]{1,0:T(1,128)} %get-tuple-element.145) | copy-start | bytes 3076
  234.6 39.9 %copy-start.14 = (f32[2048]{0:T(1024)S(1)}, f32[2048]{0:T(1024)}, u32[]{:S(2)}) copy-start(f32[2048]{0:T(1024)} %get-tuple-element.256) | copy-start | bytes 24580
  271.6 68.4 %collective-permute-start.11 = (bf16[1024,1024]{1,0:T(8,128)(2,1)}, bf16[1024,1024]{1,0:T(8,128)(2,1)}, u32[]{:S(2)}, u32[]{:S(2)}) collective-permute-start(bf16[1024,1024]{1,0:T(8,128)(2,1)} %get-tuple-element.163), channel_id=1, source_target_pairs={{0,2},{2,0},{1,3},{3,1},{4,6},{6,4},{5,7},{7,5},{8,10},{10,8},{9,1... | collective-permute-start | bytes 6291464 | tf_op jit(solution)/shard_map/ppermute | solution.py:860
  279.1 123.4 %collective-permute-start.13 = (bf16[512,512]{1,0:T(8,128)(2,1)}, bf16[512,512]{1,0:T(8,128)(2,1)}, u32[]{:S(2)}, u32[]{:S(2)}) collective-permute-start(bf16[512,512]{1,0:T(8,128)(2,1)} %get-tuple-element.181), channel_id=1, source_target_pairs={{0,16},{16,0},{1,17},{17,1},{2,18},{18,2},{3,19},{19,3},{4,20},{20... | collective-permute-start | bytes 1572872 | tf_op jit(solution)/shard_map/ppermute | solution.py:872
  315.2 22.7 %copy-start.24 = (f32[1,512]{1,0:T(1,128)S(1)}, f32[1,512]{1,0:T(1,128)}, u32[]{:S(2)}) copy-start(f32[1,512]{1,0:T(1,128)} %get-tuple-element.159) | copy-start | bytes 6148
  315.2 24.1 %copy-start.15 = (f32[2048]{0:T(1024)S(1)}, f32[2048]{0:T(1024)}, u32[]{:S(2)}) copy-start(f32[2048]{0:T(1024)} %get-tuple-element.256) | copy-start | bytes 24580
  334.9 64.3 %collective-permute-start.12 = (bf16[1024,512]{1,0:T(8,128)(2,1)}, bf16[1024,512]{1,0:T(8,128)(2,1)S(1)}, u32[]{:S(2)}, u32[]{:S(2)}) collective-permute-start(bf16[1024,512]{1,0:T(8,128)(2,1)} %get-tuple-element.178), channel_id=1, source_target_pairs={{0,2},{2,0},{1,3},{3,1},{4,6},{6,4},{5,7},{7,5},{8,10},{10,8},{9,1... | collective-permute-start | bytes 3145736 | tf_op jit(solution)/shard_map/ppermute | solution.py:860
  336.5 89.2 %collective-permute-start.17 = (bf16[1024,1024]{1,0:T(8,128)(2,1)}, bf16[1024,1024]{1,0:T(8,128)(2,1)}, u32[]{:S(2)}, u32[]{:S(2)}) collective-permute-start(bf16[1024,1024]{1,0:T(8,128)(2,1)} %get-tuple-element.190), channel_id=1, source_target_pairs={{0,2},{2,0},{1,3},{3,1},{4,6},{6,4},{5,7},{7,5},{8,10},{10,8},{9,1... | collective-permute-start | bytes 6291464 | tf_op jit(solution)/shard_map/ppermute | solution.py:860
  343.4 61.7 %collective-permute-start.14 = (bf16[512,1024]{1,0:T(8,128)(2,1)}, bf16[512,1024]{1,0:T(8,128)(2,1)S(1)}, u32[]{:S(2)}, u32[]{:S(2)}) collective-permute-start(bf16[512,1024]{1,0:T(8,128)(2,1)} %get-tuple-element.182), channel_id=1, source_target_pairs={{0,16},{16,0},{1,17},{17,1},{2,18},{18,2},{3,19},{19,3},{4,20},{20... | collective-permute-start | bytes 3145736 | tf_op jit(solution)/shard_map/ppermute | solution.py:872
  399.2 13.8 %collective-permute-start.15 = (bf16[1024,2048]{1,0:T(8,128)(2,1)}, bf16[1024,2048]{1,0:T(8,128)(2,1)}, u32[]{:S(2)}, u32[]{:S(2)}) collective-permute-start(bf16[1024,2048]{1,0:T(8,128)(2,1)} %get-tuple-element.184), channel_id=1, source_target_pairs={{0,1},{1,0},{2,3},{3,2},{4,5},{5,4},{6,7},{7,6},{8,9},{9,8},{10,11... | collective-permute-start | bytes 12582920 | tf_op jit(solution)/shard_map/ppermute | solution.py:934
  399.2 20.2 %collective-permute-start.16 = (bf16[1024,2048]{1,0:T(8,128)(2,1)}, bf16[1024,2048]{1,0:T(8,128)(2,1)}, u32[]{:S(2)}, u32[]{:S(2)}) collective-permute-start(bf16[1024,2048]{1,0:T(8,128)(2,1)} %get-tuple-element.187), channel_id=1, source_target_pairs={{0,1},{1,0},{2,3},{3,2},{4,5},{5,4},{6,7},{7,6},{8,9},{9,8},{10,11... | collective-permute-start | bytes 12582920 | tf_op jit(solution)/shard_map/ppermute | solution.py:934
  402.6 31.4 %collective-permute-start.19 = (bf16[512,512]{1,0:T(8,128)(2,1)}, bf16[512,512]{1,0:T(8,128)(2,1)}, u32[]{:S(2)}, u32[]{:S(2)}) collective-permute-start(bf16[512,512]{1,0:T(8,128)(2,1)} %get-tuple-element.194), channel_id=1, source_target_pairs={{0,16},{16,0},{1,17},{17,1},{2,18},{18,2},{3,19},{19,3},{4,20},{20... | collective-permute-start | bytes 1572872 | tf_op jit(solution)/shard_map/ppermute | solution.py:872
  409.4 76.2 %all-to-all-start.4 = ((bf16[8,64,1536]{2,1,0:T(8,128)(2,1)}), bf16[8,64,1536]{2,1,0:T(8,128)(2,1)S(1)}, u32[]{:S(2)}, u32[]{:S(2)}) async-start(bf16[8,64,1536]{2,1,0:T(8,128)(2,1)} %bitcast.118), calls=%async_computation.4 | async-start | bytes 3145728 | tf_op jit(solution)/shard_map/all_to_all | solution.py:886
  429.2 49.2 %collective-permute-start.18 = (bf16[512,1024]{1,0:T(8,128)(2,1)}, bf16[512,1024]{1,0:T(8,128)(2,1)S(1)}, u32[]{:S(2)}, u32[]{:S(2)}) collective-permute-start(bf16[512,1024]{1,0:T(8,128)(2,1)} %get-tuple-element.193), channel_id=1, source_target_pairs={{0,16},{16,0},{1,17},{17,1},{2,18},{18,2},{3,19},{19,3},{4,20},{20... | collective-permute-start | bytes 3145736 | tf_op jit(solution)/shard_map/ppermute | solution.py:872
  429.7 59.8 %collective-permute-start.20 = (bf16[512,2048]{1,0:T(8,128)(2,1)}, bf16[512,2048]{1,0:T(8,128)(2,1)}, u32[]{:S(2)}, u32[]{:S(2)}) collective-permute-start(bf16[512,2048]{1,0:T(8,128)(2,1)} %get-tuple-element.198), channel_id=1, source_target_pairs={{0,4},{4,0},{1,5},{5,1},{2,6},{6,2},{3,7},{7,3},{8,12},{12,8},{9,1... | collective-permute-start | bytes 6291464 | tf_op jit(solution)/shard_map/ppermute | solution.py:934
  432.5 79.4 %collective-permute-start.21 = (bf16[512,2048]{1,0:T(8,128)(2,1)}, bf16[512,2048]{1,0:T(8,128)(2,1)}, u32[]{:S(2)}, u32[]{:S(2)}) collective-permute-start(bf16[512,2048]{1,0:T(8,128)(2,1)} %get-tuple-element.206), channel_id=1, source_target_pairs={{0,8},{8,0},{1,9},{9,1},{2,10},{10,2},{3,11},{11,3},{4,12},{12,4},... | collective-permute-start | bytes 6291464 | tf_op jit(solution)/shard_map/ppermute | solution.py:934
  485.6 8.0 %copy-start.7 = (bf16[8,64,1536]{2,1,0:T(8,128)(2,1)}, bf16[8,64,1536]{2,1,0:T(8,128)(2,1)S(1)}, u32[]{:S(2)}) copy-start(bf16[8,64,1536]{2,1,0:T(8,128)(2,1)S(1)} %all-to-all-done.4.refs_0_.refs_4_) | copy-start | bytes 4718596
  485.6 46.6 %all-to-all-start.3 = ((bf16[8,80,1536]{2,1,0:T(8,128)(2,1)}), bf16[8,80,1536]{2,1,0:T(8,128)(2,1)S(1)}, u32[]{:S(2)}, u32[]{:S(2)}) async-start(bf16[8,80,1536]{2,1,0:T(8,128)(2,1)} %shard_map.379), calls=%async_computation.3 | async-start | bytes 3932160 | tf_op jit(solution)/shard_map/all_to_all | solution.py:886
  516.1 35.3 %collective-permute-start.22 = (bf16[256,2048]{1,0:T(8,128)(2,1)}, bf16[256,2048]{1,0:T(8,128)(2,1)}, u32[]{:S(2)}, u32[]{:S(2)}) collective-permute-start(bf16[256,2048]{1,0:T(8,128)(2,1)} %get-tuple-element.227), channel_id=1, source_target_pairs={{0,4},{4,0},{1,5},{5,1},{2,6},{6,2},{3,7},{7,3},{8,12},{12,8},{9,1... | collective-permute-start | bytes 3145736 | tf_op jit(solution)/shard_map/ppermute | solution.py:959
  518.1 37.3 %collective-permute-start.23 = (bf16[256,2048]{1,0:T(8,128)(2,1)S(1)}, bf16[256,2048]{1,0:T(8,128)(2,1)}, u32[]{:S(2)}, u32[]{:S(2)}) collective-permute-start(bf16[256,2048]{1,0:T(8,128)(2,1)S(1)} %copy-done.28), channel_id=1, source_target_pairs={{0,8},{8,0},{1,9},{9,1},{2,10},{10,2},{3,11},{11,3},{4,12},{12,4},... | collective-permute-start | bytes 3145736 | tf_op jit(solution)/shard_map/ppermute | solution.py:959
  547.0 13.5 %collective-permute-start.24 = (f32[768]{0:T(1024)S(1)}, f32[768]{0:T(1024)S(1)}, u32[]{:S(2)}, u32[]{:S(2)}) collective-permute-start(f32[768]{0:T(1024)S(1)} %get-tuple-element.249), channel_id=1, source_target_pairs={{0,2},{2,0},{1,3},{3,1},{4,6},{6,4},{5,7},{7,5},{8,10},{10,8},{9,1... | collective-permute-start | bytes 9224 | tf_op jit(solution)/shard_map/ppermute | solution.py:1026
  548.6 11.9 %collective-permute-start.25 = (f32[768]{0:T(1024)S(1)}, f32[768]{0:T(1024)S(1)}, u32[]{:S(2)}, u32[]{:S(2)}) collective-permute-start(f32[768]{0:T(1024)S(1)} %get-tuple-element.248), channel_id=1, source_target_pairs={{0,16},{16,0},{1,17},{17,1},{2,18},{18,2},{3,19},{19,3},{4,20},{20... | collective-permute-start | bytes 9224 | tf_op jit(solution)/shard_map/ppermute | solution.py:1027
  548.6 11.9 %collective-permute-start.26 = (f32[768]{0:T(1024)S(1)}, f32[768]{0:T(1024)S(1)}, u32[]{:S(2)}, u32[]{:S(2)}) collective-permute-start(f32[768]{0:T(1024)S(1)} %get-tuple-element.247), channel_id=1, source_target_pairs={{0,18},{2,16},{16,2},{18,0},{1,19},{3,17},{17,3},{19,1},{4,22},{6,... | collective-permute-start | bytes 9224 | tf_op jit(solution)/shard_map/ppermute | solution.py:1028
  (20 other events, 50.2 us)
Sparse Core Ops, SparseCore 0:
  12.0 72.6 all-gather.4
  102.9 74.4 all-gather.6

commit v5 on v4

--- a/solution.py
+++ b/solution.py
@@ -563,7 +563,7 @@
 
 
 def last_sum(kept, got, role):
-    count, steps = len(kept), 2
+    count, steps = len(kept), 4
     rows = kept[0].shape[0]
     widths = [v.shape[1] for v in kept]
 
@@ -612,7 +612,7 @@
 
 def finish_tokens(order, tokens, other, kept, got, back):
     slots = tokens.shape[0]
-    steps = 2
+    steps = 4
     rows = slots // steps
 
     def kernel(order_ref, x_ref, other_ref, kept_ref, got_ref, out_ref, sum_ref):
@@ -868,7 +868,7 @@
             term = jnp.concatenate([keep, got], axis=0)
             owned[index] = lax.psum_scatter(term, CROSS, scatter_dimension=0, tiled=True)
             return tokens[0]
-        kept, sent = split_sum(after(keep, *tokens), got, 2, f"col{index}")
+        kept, sent = split_sum(after(keep, *tokens), got, 4, f"col{index}")
         grouped[index] = (kept, lax.ppermute(sent, "far", SWAP))
         return kept
 
@@ -935,9 +935,9 @@
 
     def do_own(name, stage, *waits):
         if stage == "core":
-            pair = own_step((have[f"{name}_keep"], have[f"{name}_send"]), "core", 4, f"{name}_core", *waits)
+            pair = own_step((have[f"{name}_keep"], have[f"{name}_send"]), "core", 8, f"{name}_core", *waits)
         else:
-            pair = own_step(have[f"{name}_pair"], stage, 2, f"{name}_{stage}", *waits)
+            pair = own_step(have[f"{name}_pair"], stage, 4, f"{name}_{stage}", *waits)
         have[f"{name}_pair"] = pair
         return (pair[0],)
 

time: 579 us -> 584 us (level)
  Pallas kernels: 261 us -> 273 us
  waiting for transfers between devices: 187 us -> 180 us
    pallas_call x8, Pallas kernels: 32.7 us -> 42 us  [split_sum(): pl.pallas_call(kernel, grid=(steps,), in_specs=[low, high, low, high], ou...]
  transfers between devices with their start and end apart: 34 -> 34, of which waited for: 9 -> 9; matrix products, arithmetic and copies ran while one was open for 7% -> 7% of each run, Pallas kernels for 45% -> 47%
where the time goes in v5:
time: 584 us; the launch traced here: 573 us
  Pallas kernels  273 us (47%)
  waiting for transfers between devices  180 us (31%)
  starting transfers between devices  54.8 us (9%)
  local copies, waits for them, and re-layouts  35.1 us (6%)
  between operations  15.2 us (3%)
  other arithmetic  15 us (3%)
    pallas_call x3, Pallas kernels, mlp_chunk(): pl.pallas_call(kernel, grid_spec=pltpu.PrefetchScalarGridSpec(num_scalar_...  70.9 us
    ppermute x1, waiting for transfers between devices, body(): far_got[0] = lax.ppermute(owns[0], 'far', SWAP)  57.5 us
    ppermute x2, waiting for transfers between devices, send_far(): lax.ppermute(after(owns[load], *waits) if waits else owns[load], 'far', S...  48.2 us
    ppermute x4, waiting for transfers between devices, sum_columns(): grouped[index] = (kept, lax.ppermute(sent, 'far', SWAP))  44.4 us
    pallas_call x8, Pallas kernels, split_sum(): pl.pallas_call(kernel, grid=(steps,), in_specs=[low, high, low, high], ou...  42 us
    pallas_call x1, Pallas kernels, attn_chunk(): pl.pallas_call(kernel, grid_spec=pltpu.PrefetchScalarGridSpec(num_scalar_...  36.3 us
    pallas_call x1, Pallas kernels, back_part(): pl.pallas_call(kernel, grid=(TEAM,), in_specs=[ANYWHERE] * (count * per)...  32.4 us
    pallas_call x5, Pallas kernels, adamw_columns(): pl.pallas_call(kernel, grid=(sections, rows // part), in_specs=specs + [A...  30.3 us
  transfers between devices with their start and end apart: 34, of which 9 were waited for; matrix products, arithmetic and copies ran while one was open for 7% of the time, Pallas kernels for 47%

profile of v5, /device:TPU:0, one launch (start us, length us, event | category | flops | bytes accessed | tf_op | source)
XLA Modules:
  0.0 573.1 jit_solution(7692887401274598101)
XLA Ops:
  7.8 4.1 shard_map.363
  16.9 5.3 all-to-all-start
  22.1 2.0 collective-permute-start
  29.1 2.2 pad_maximum_fusion.1
  31.3 4.2 all-to-all-done.refs_0_.refs_2_
  35.5 4.2 all-to-all-start.1
  39.8 3.4 collective-permute-start.1
  43.2 57.5 %collective-permute-done.1.refs_1_.refs_3_ = bf16[8,80,512]{2,1,0:T(8,128)(2,1)S(1)} collective-permute-done((bf16[8,80,512]{2,1,0:T(8,128)(2,1)}, bf16[8,80,512]{2,1,0:T(8,128)(2,1)S(1)}, u32[]{:S(2)}, u32[]{:S(2)}) %collective-permute-start.1) | collective-permute-done | bytes 655392 | tf_op jit(solution)/shard_map/ppermute | solution.py:780
  100.7 2.0 all-to-all-done.1
  105.2 5.4 all-to-all-start.2
  116.8 1.9 convert_reduce_fusion
  120.5 40.6 %collective-permute-done.2.refs_3_.refs_5_ = bf16[512,1024]{1,0:T(8,128)(2,1)} collective-permute-done((bf16[512,1024]{1,0:T(8,128)(2,1)}, bf16[512,1024]{1,0:T(8,128)(2,1)}, u32[]{:S(2)}, u32[]{:S(2)}) %collective-permute-start.2) | collective-permute-done | bytes 1048608 | tf_op jit(solution)/shard_map/ppermute | solution.py:794
  163.2 14.2 %all-gather.7.cloned.1.call-done = bf16[2048,2048]{1,0:T(8,128)(2,1)} async-done(((bf16[512,2048]{1,0:T(8,128)(2,1)}), bf16[2048,2048]{1,0:T(8,128)(2,1)}) %all-gather.7.cloned.1.call-update) | async-done | bytes 8388624 | tf_op jit(solution)/shard_map/all_gather | solution.py:786
  177.4 1.9 shard_map.364
  184.2 14.2 %shard_map.365 = (bf16[2048,2048]{1,0:T(8,128)(2,1)}, bf16[2048,2048]{1,0:T(8,128)(2,1)}, bf16[2048,2048]{1,0:T(8,128)(2,1)}) custom-call(s32[8]{0:T(128)} %get-tuple-element.287.members_ref, bf16[4,512,2048]{2,1,0:T(8,128)(2,1)} %bitcast.150, bf16[4,512,2048]{2,1,0:T(8,128)(2,1)} %bitcast.155, f32[1,2048]{1,0:T(1,128)} %bitcast.133, f32[1,2048]{1,0:T(1,128)} %bitcast.136, ...), custom_call_target="tpu_custom_call" | custom-call | flops 10000000000 | bytes 1024 | tf_op jit(solution)/shard_map/pallas_call | solution.py:246
  198.5 20.1 %shard_map.366 = (bf16[2048,256]{1,0:T(8,128)(2,1)}, bf16[2048,256]{1,0:T(8,128)(2,1)}, bf16[1024,512]{1,0:T(8,128)(2,1)}, bf16[1024,512]{1,0:T(8,128)(2,1)}, f32[1,256]{1,0:T(1,128)}) custom-call(s32[8]{0:T(128)} %get-tuple-element.287.members_ref, bf16[4,512,2048]{2,1,0:T(8,128)(2,1)} %bitcast.151, bf16[4,512,2048]{2,1,0:T(8,128)(2,1)} %bitcast.156, ...), custom_call_target="tpu_custom_call" | custom-call | flops 15000000512 | bytes 1024 | tf_op jit(solution)/shard_map/pallas_call | solution.py:336
  224.5 7.6 %collective-permute-done.3.refs_3_.refs_9_.refs_13_ = bf16[512,1536]{1,0:T(8,128)(2,1)} collective-permute-done((bf16[512,1536]{1,0:T(8,128)(2,1)}, bf16[512,1536]{1,0:T(8,128)(2,1)}, u32[]{:S(2)}, u32[]{:S(2)}) %collective-permute-start.3) | collective-permute-done | bytes 1572896 | tf_op jit(solution)/shard_map/ppermute | solution.py:794
  234.6 36.3 %shard_map.367 = (bf16[2048,256]{1,0:T(8,128)(2,1)}, bf16[2048,768]{1,0:T(8,128)(2,1)}, bf16[1024,1024]{1,0:T(8,128)(2,1)}, bf16[1024,1024]{1,0:T(8,128)(2,1)}, f32[1,768]{1,0:T(1,128)}) custom-call(s32[8]{0:T(128)} %get-tuple-element.287.members_ref, s32[8,2]{1,0:T(8,128)} %get-tuple-element.278.first_ref, s32[8,2]{1,0:T(8,128)} %get-tuple-element.277.live_ref, ...), custom_call_target="tpu_custom_call" | custom-call | flops 30000001024 | bytes 1024 | tf_op jit(solution)/shard_map/pallas_call | solution.py:409
  276.7 3.7 shard_map.368
  280.4 2.5 collective-permute-done.7.refs_5_.refs_11_.refs_15_
  284.0 31.1 %shard_map.369 = (bf16[2048,512]{1,0:T(8,128)(2,1)}, bf16[2048,512]{1,0:T(8,128)(2,1)}, bf16[1024,1024]{1,0:T(8,128)(2,1)}, bf16[1024,1024]{1,0:T(8,128)(2,1)}, f32[1,512]{1,0:T(1,128)}) custom-call(s32[8]{0:T(128)} %get-tuple-element.287.members_ref, bf16[4,512,2048]{2,1,0:T(8,128)(2,1)} %bitcast.153, bf16[4,512,2048]{2,1,0:T(8,128)(2,1)} %bitcast.158, ...), custom_call_target="tpu_custom_call" | custom-call | flops 1999999991808 | bytes 1024 | tf_op jit(solution)/shard_map/pallas_call | solution.py:336
  315.2 19.7 %shard_map.370 = (bf16[2048,256]{1,0:T(8,128)(2,1)}, bf16[2048,256]{1,0:T(8,128)(2,1)}, bf16[1024,512]{1,0:T(8,128)(2,1)}, bf16[1024,512]{1,0:T(8,128)(2,1)}, f32[1,256]{1,0:T(1,128)}) custom-call(s32[8]{0:T(128)} %get-tuple-element.287.members_ref, bf16[4,512,2048]{2,1,0:T(8,128)(2,1)} %bitcast.154, bf16[4,512,2048]{2,1,0:T(8,128)(2,1)} %bitcast.159, ...), custom_call_target="tpu_custom_call" | custom-call | flops 15000000512 | bytes 1024 | tf_op jit(solution)/shard_map/pallas_call | solution.py:336
  339.9 4.3 shard_map.371
  344.7 19.6 %shard_map.372 = (bf16[1024,2048]{1,0:T(8,128)(2,1)}, bf16[1024,2048]{1,0:T(8,128)(2,1)}) custom-call(bf16[8,80,512]{2,1,0:T(8,128)(2,1)} %all-to-all-done.refs_0_.refs_2_, bf16[8,80,512]{2,1,0:T(8,128)(2,1)} %copy-done.10, bf16[8,80,512]{2,1,0:T(8,128)(2,1)} %copy-done.11, bf16[8,80,512]{2,1,0:T(8,128)(2,1)} %copy-done.12, ...), custom_call_target="tpu_custom_call" | custom-call | flops 19000000512 | bytes 1024 | tf_op jit(solution)/shard_map/pallas_call | solution.py:485
  364.3 32.4 %shard_map.373 = (bf16[1024,2048]{1,0:T(8,128)(2,1)}, bf16[1024,2048]{1,0:T(8,128)(2,1)}, f32[8,2048]{1,0:T(8,128)}) custom-call(bf16[8,80,512]{2,1,0:T(8,128)(2,1)} %all-to-all-done.refs_0_.refs_2_, bf16[8,80,512]{2,1,0:T(8,128)(2,1)} %copy-done.10, bf16[8,80,512]{2,1,0:T(8,128)(2,1)} %copy-done.11, bf16[8,80,512]{2,1,0:T(8,128)(2,1)} %copy-done.12, ...), custom_call_target="tpu_custom_call" | custom-call | flops 1000000000 | bytes 1024 | tf_op jit(solution)/shard_map/pallas_call | solution.py:531
  401.0 3.7 shard_map.374
  404.7 2.5 collective-permute-start.19
  408.2 4.2 shard_map.375
  412.4 3.6 all-to-all-start.4
  416.0 8.1 %shard_map.376 = (f32[512,2048]{1,0:T(8,128)}, bf16[512,2048]{1,0:T(8,128)(2,1)}) custom-call(bf16[1024,2048]{1,0:T(8,128)(2,1)} %get-tuple-element.183.l_low.l_high, bf16[1024,2048]{1,0:T(8,128)(2,1)} %get-tuple-element.183.l_low.l_high, bf16[1024,2048]{1,0:T(8,128)(2,1)} %collective-permute-done.15.r_low.r_high, ...), custom_call_target="tpu_custom_call" | custom-call | flops 100000000 | bytes 1024 | tf_op jit(solution)/shard_map/pallas_call | solution.py:555
  424.1 8.1 %shard_map.377 = (f32[512,2048]{1,0:T(8,128)}, bf16[512,2048]{1,0:T(8,128)(2,1)}) custom-call(bf16[1024,2048]{1,0:T(8,128)(2,1)} %get-tuple-element.186.l_low.l_high, bf16[1024,2048]{1,0:T(8,128)(2,1)} %get-tuple-element.186.l_low.l_high, bf16[1024,2048]{1,0:T(8,128)(2,1)} %collective-permute-done.16.r_low.r_high, ...), custom_call_target="tpu_custom_call" | custom-call | flops 1000000000 | bytes 1024 | tf_op jit(solution)/shard_map/pallas_call | solution.py:555
  432.1 4.4 shard_map.378
  437.1 1.9 collective-permute-start.20
  441.3 44.4 %collective-permute-done.18.refs_2_ = bf16[512,1024]{1,0:T(8,128)(2,1)S(1)} collective-permute-done((bf16[512,1024]{1,0:T(8,128)(2,1)}, bf16[512,1024]{1,0:T(8,128)(2,1)S(1)}, u32[]{:S(2)}, u32[]{:S(2)}) %collective-permute-start.18) | collective-permute-done | bytes 1048608 | tf_op jit(solution)/shard_map/ppermute | solution.py:872
  486.7 6.2 %shard_map.379 = bf16[8,80,1536]{2,1,0:T(8,128)(2,1)} custom-call(f32[512,1024]{1,0:T(8,128)} %get-tuple-element.192.refs_0_, f32[512,512]{1,0:T(8,128)} %get-tuple-element.179.refs_1_, bf16[512,1024]{1,0:T(8,128)(2,1)} %copy-done.30, bf16[512,512]{1,0:T(8,128)(2,1)} %collective-permute-done.19.refs_3_, bf16[8,16,1536]{2,1,0:T(8,128)(2,1)} %bitcast.127), custom_call_target="tpu_custom_call" | custom-call | flops 3000000000 | bytes 1024 | tf_op jit(solution)/shard_map/pallas_call | solution.py:603
  492.9 3.6 all-to-all-start.3
  496.6 4.8 shard_map.380
  501.4 3.9 shard_map.382
  505.3 9.5 %shard_map.381 = (f32[64,6144]{1,0:T(8,128)}, f32[64,6144]{1,0:T(8,128)}, f32[64,6144]{1,0:T(8,128)}, f32[64,6144]{1,0:T(8,128)}) custom-call(bf16[8,64,1536]{2,1,0:T(8,128)(2,1)} %copy-done.7, f32[64,6144]{1,0:T(8,128)} %refs_1_.5, f32[64,6144]{1,0:T(8,128)} %refs_2_.5, f32[64,6144]{1,0:T(8,128)} %refs_3_.5), custom_call_target="tpu_custom_call" | custom-call | flops 8999999488 | bytes 1024 | tf_op jit(solution)/shard_map/pallas_call | solution.py:675
  514.9 4.9 shard_map.383
  519.8 4.9 shard_map.384
  524.7 1.9 collective-permute-start.22
  528.1 7.1 %all-to-all-done.3.refs_0_.refs_4_ = bf16[8,80,1536]{2,1,0:T(8,128)(2,1)S(1)} async-done(((bf16[8,80,1536]{2,1,0:T(8,128)(2,1)}), bf16[8,80,1536]{2,1,0:T(8,128)(2,1)S(1)}, u32[]{:S(2)}, u32[]{:S(2)}) %all-to-all-start.3) | async-done | bytes 1966112 | tf_op jit(solution)/shard_map/all_to_all | solution.py:886
  536.4 7.1 %shard_map.385 = (f32[64,8192]{1,0:T(8,128)}, f32[64,8192]{1,0:T(8,128)}, f32[64,8192]{1,0:T(8,128)}, f32[64,8192]{1,0:T(8,128)}, f32[64,8192]{1,0:T(8,128)}, /*...) custom-call(bf16[8,80,1536]{2,1,0:T(8,128)(2,1)} %copy-done, ...), custom_call_target="tpu_custom_call", output_to_operand_aliasing={{0}: (8, {}), {1}: (9, {}), {2}: (10, {}), {3}: (11, {}), {... | custom-call | flops 100000000 | bytes 1024 | tf_op jit(solution)/shard_map/pallas_call | solution.py:675
  543.5 4.9 shard_map.386
  551.5 2.9 collective-permute-start.26
  554.4 4.9 shard_map.387
  559.3 5.9 %shard_map.388 = bf16[256,2048]{1,0:T(8,128)(2,1)} custom-call(s32[16]{0:T(128)} %fusion.15.order_ref, bf16[256,2048]{1,0:T(8,128)(2,1)} %x_ref.3, bf16[256,2048]{1,0:T(8,128)(2,1)} %get-tuple-element.257.other_ref, f32[256,2048]{1,0:T(8,128)} %get-tuple-element.199.kept_ref, bf16[256,2048]{1,0:T(8,128)(2,1)} %collective-permute-done.23.got_ref), custom_call_target="tpu_custom_call" | custom-call | flops 3000000000 | bytes 1024 | tf_op jit(solution)/shard_map/pallas_call | solution.py:634
  (235 shorter events, 64.2 us)
Async XLA Ops:
  7.2 156.0 %all-gather.5.cloned.1.call-start = ((), (), s32[]{:S(2)}) async-start(), calls=%async_computation.5 | async-start | bytes 10485760 | tf_op jit(solution)/shard_map/all_gather | solution.py:786
  14.3 88.5 %copy-start.4 = (bf16[64,8192]{1,0:T(8,128)(2,1)}, bf16[64,8192]{1,0:T(8,128)(2,1)S(1)}, u32[]{:S(2)}) copy-start(bf16[64,8192]{1,0:T(8,128)(2,1)S(1)} %convert.11) | copy-start | bytes 3145732
  16.9 18.6 %all-to-all-start = ((bf16[8,80,512]{2,1,0:T(8,128)(2,1)}), bf16[8,80,512]{2,1,0:T(8,128)(2,1)}, u32[]{:S(2)}, u32[]{:S(2)}) async-start(bf16[8,80,512]{2,1,0:T(8,128)(2,1)} %pad_maximum_fusion.2), calls=%async_computation | async-start | bytes 1310720 | tf_op jit(solution)/shard_map/all_to_all | solution.py:783
  22.1 78.5 %collective-permute-start = (bf16[512,2048]{1,0:T(8,128)(2,1)}, bf16[512,2048]{1,0:T(8,128)(2,1)}, u32[]{:S(2)}, u32[]{:S(2)}) collective-permute-start(bf16[512,2048]{1,0:T(8,128)(2,1)} %shard_map.363), channel_id=1, source_target_pairs={{0,8},{8,0},{1,9},{9,1},{2,10},{10,2},{3,11},{11,3},{4,12},{12,4},... | collective-permute-start | bytes 6291464 | tf_op jit(solution)/shard_map/ppermute | solution.py:764
  35.5 67.2 %all-to-all-start.1 = ((bf16[8,64,1024]{2,1,0:T(8,128)(2,1)}), bf16[8,64,1024]{2,1,0:T(8,128)(2,1)}, u32[]{:S(2)}, u32[]{:S(2)}) async-start(bf16[8,64,1024]{2,1,0:T(8,128)(2,1)} %pad_maximum_fusion.1), calls=%async_computation.1 | async-start | bytes 2097152 | tf_op jit(solution)/shard_map/all_to_all | solution.py:783
  39.8 137.6 %all-gather.7.cloned.1.call-start = ((), (), s32[]{:S(2)}) async-start(), calls=%async_computation.6 | async-start | bytes 10485760 | tf_op jit(solution)/shard_map/all_gather | solution.py:786
  39.8 60.9 %collective-permute-start.1 = (bf16[8,80,512]{2,1,0:T(8,128)(2,1)}, bf16[8,80,512]{2,1,0:T(8,128)(2,1)S(1)}, u32[]{:S(2)}, u32[]{:S(2)}) collective-permute-start(bf16[8,80,512]{2,1,0:T(8,128)(2,1)} %all-to-all-done.refs_0_.refs_2_), channel_id=1, source_target_pairs={{0,16},{16,0},{1,17},{17,1},{2,18},{18,2},{3,19},{19,3},{4,20},{20... | collective-permute-start | bytes 1966088 | tf_op jit(solution)/shard_map/ppermute | solution.py:780
  100.7 14.0 %copy-start.10 = (bf16[8,80,512]{2,1,0:T(8,128)(2,1)}, bf16[8,80,512]{2,1,0:T(8,128)(2,1)S(1)}, u32[]{:S(2)}) copy-start(bf16[8,80,512]{2,1,0:T(8,128)(2,1)S(1)} %collective-permute-done.1.refs_1_.refs_3_) | copy-start | bytes 1966084
  105.2 11.6 %copy-start.8 = (bf16[256,2048]{1,0:T(8,128)(2,1)S(1)}, bf16[256,2048]{1,0:T(8,128)(2,1)}, u32[]{:S(2)}) copy-start(bf16[256,2048]{1,0:T(8,128)(2,1)} %y_ref.1) | copy-start | bytes 3145732
  105.2 57.4 %all-to-all-start.2 = ((bf16[8,64,1536]{2,1,0:T(8,128)(2,1)}), bf16[8,64,1536]{2,1,0:T(8,128)(2,1)}, u32[]{:S(2)}, u32[]{:S(2)}) async-start(bf16[8,64,1536]{2,1,0:T(8,128)(2,1)} %pad_maximum_fusion), calls=%async_computation.2 | async-start | bytes 3145728 | tf_op jit(solution)/shard_map/all_to_all | solution.py:783
  111.8 49.3 %collective-permute-start.2 = (bf16[512,1024]{1,0:T(8,128)(2,1)}, bf16[512,1024]{1,0:T(8,128)(2,1)}, u32[]{:S(2)}, u32[]{:S(2)}) collective-permute-start(bf16[512,1024]{1,0:T(8,128)(2,1)} %bitcast.5.refs_2_.refs_4_), channel_id=1, source_target_pairs={{0,16},{16,0},{1,17},{17,1},{2,18},{18,2},{3,19},{19,3},{4,20},{20... | collective-permute-start | bytes 3145736 | tf_op jit(solution)/shard_map/ppermute | solution.py:794
  112.9 50.2 %collective-permute-start.5 = (bf16[8,80,512]{2,1,0:T(8,128)(2,1)}, bf16[8,80,512]{2,1,0:T(8,128)(2,1)S(1)}, u32[]{:S(2)}, u32[]{:S(2)}) collective-permute-start(bf16[8,80,512]{2,1,0:T(8,128)(2,1)} %all-to-all-done.refs_0_.refs_2_), channel_id=1, source_target_pairs={{0,2},{2,0},{1,3},{3,1},{4,6},{6,4},{5,7},{7,5},{8,10},{10,8},{9,1... | collective-permute-start | bytes 1966088 | tf_op jit(solution)/shard_map/ppermute | solution.py:804
  114.7 48.5 %collective-permute-start.6 = (bf16[8,80,512]{2,1,0:T(8,128)(2,1)S(1)}, bf16[8,80,512]{2,1,0:T(8,128)(2,1)S(1)}, u32[]{:S(2)}, u32[]{:S(2)}) collective-permute-start(bf16[8,80,512]{2,1,0:T(8,128)(2,1)S(1)} %collective-permute-done.1.refs_1_.refs_3_), channel_id=1, source_target_pairs={{0,2},{2,0},{1,3},{3,1},{4,6},{6,4},{5,7},{7,5},{8,10},{10,8},{9,1... | collective-permute-start | bytes 1966088 | tf_op jit(solution)/shard_map/ppermute | solution.py:800
  118.7 115.8 %collective-permute-start.8 = (bf16[512,1024]{1,0:T(8,128)(2,1)}, bf16[512,1024]{1,0:T(8,128)(2,1)}, u32[]{:S(2)}, u32[]{:S(2)}) collective-permute-start(bf16[512,1024]{1,0:T(8,128)(2,1)} %bitcast.5.refs_2_.refs_4_), channel_id=1, source_target_pairs={{0,2},{2,0},{1,3},{3,1},{4,6},{6,4},{5,7},{7,5},{8,10},{10,8},{9,1... | collective-permute-start | bytes 3145736 | tf_op jit(solution)/shard_map/ppermute | solution.py:804
  161.1 73.5 %collective-permute-start.9 = (bf16[512,1024]{1,0:T(8,128)(2,1)}, bf16[512,1024]{1,0:T(8,128)(2,1)}, u32[]{:S(2)}, u32[]{:S(2)}) collective-permute-start(bf16[512,1024]{1,0:T(8,128)(2,1)} %collective-permute-done.2.refs_3_.refs_5_), channel_id=1, source_target_pairs={{0,2},{2,0},{1,3},{3,1},{4,6},{6,4},{5,7},{7,5},{8,10},{10,8},{9,1... | collective-permute-start | bytes 3145736 | tf_op jit(solution)/shard_map/ppermute | solution.py:800
  162.7 117.7 %collective-permute-start.4 = (bf16[512,1536]{1,0:T(8,128)(2,1)}, bf16[512,1536]{1,0:T(8,128)(2,1)}, u32[]{:S(2)}, u32[]{:S(2)}) collective-permute-start(bf16[512,1536]{1,0:T(8,128)(2,1)} %bitcast.11.refs_2_.refs_8_.refs_12_), channel_id=1, source_target_pairs={{0,2},{2,0},{1,3},{3,1},{4,6},{6,4},{5,7},{7,5},{8,10},{10,8},{9,1... | collective-permute-start | bytes 4718600 | tf_op jit(solution)/shard_map/ppermute | solution.py:804
  163.2 14.2 %copy-start.11 = (bf16[8,80,512]{2,1,0:T(8,128)(2,1)}, bf16[8,80,512]{2,1,0:T(8,128)(2,1)S(1)}, u32[]{:S(2)}) copy-start(bf16[8,80,512]{2,1,0:T(8,128)(2,1)S(1)} %collective-permute-done.5.refs_2_.refs_4_) | copy-start | bytes 1966084
  163.2 69.0 %collective-permute-start.3 = (bf16[512,1536]{1,0:T(8,128)(2,1)}, bf16[512,1536]{1,0:T(8,128)(2,1)}, u32[]{:S(2)}, u32[]{:S(2)}) collective-permute-start(bf16[512,1536]{1,0:T(8,128)(2,1)} %bitcast.11.refs_2_.refs_8_.refs_12_), channel_id=1, source_target_pairs={{0,16},{16,0},{1,17},{17,1},{2,18},{18,2},{3,19},{19,3},{4,20},{20... | collective-permute-start | bytes 4718600 | tf_op jit(solution)/shard_map/ppermute | solution.py:794
  163.2 14.2 %copy-start.12 = (bf16[8,80,512]{2,1,0:T(8,128)(2,1)}, bf16[8,80,512]{2,1,0:T(8,128)(2,1)S(1)}, u32[]{:S(2)}) copy-start(bf16[8,80,512]{2,1,0:T(8,128)(2,1)S(1)} %collective-permute-done.6.refs_3_.refs_5_) | copy-start | bytes 1966084
  198.5 20.1 %copy-start.19 = (s32[8]{0:T(128)S(1)}, s32[8]{0:T(128)}, u32[]{:S(2)}) copy-start(s32[8]{0:T(128)} %get-tuple-element.289) | copy-start | bytes 100
  198.5 20.9 %copy-start.18 = (s32[8]{0:T(128)S(1)}, s32[8]{0:T(128)}, u32[]{:S(2)}) copy-start(s32[8]{0:T(128)} %get-tuple-element.288) | copy-start | bytes 100
  198.5 21.6 %copy-start.17 = (s32[8]{0:T(128)S(1)}, s32[8]{0:T(128)}, u32[]{:S(2)}) copy-start(s32[8]{0:T(128)} %get-tuple-element.291) | copy-start | bytes 100
  198.5 22.4 %copy-start.16 = (s32[8]{0:T(128)S(1)}, s32[8]{0:T(128)}, u32[]{:S(2)}) copy-start(s32[8]{0:T(128)} %get-tuple-element.290) | copy-start | bytes 100
  223.0 52.7 %collective-permute-start.10 = (bf16[1024,512]{1,0:T(8,128)(2,1)}, bf16[1024,512]{1,0:T(8,128)(2,1)S(1)}, u32[]{:S(2)}, u32[]{:S(2)}) collective-permute-start(bf16[1024,512]{1,0:T(8,128)(2,1)} %get-tuple-element.152), channel_id=1, source_target_pairs={{0,2},{2,0},{1,3},{3,1},{4,6},{6,4},{5,7},{7,5},{8,10},{10,8},{9,1... | collective-permute-start | bytes 3145736 | tf_op jit(solution)/shard_map/ppermute | solution.py:860
  232.1 50.8 %collective-permute-start.7 = (bf16[512,1536]{1,0:T(8,128)(2,1)}, bf16[512,1536]{1,0:T(8,128)(2,1)S(1)}, u32[]{:S(2)}, u32[]{:S(2)}) collective-permute-start(bf16[512,1536]{1,0:T(8,128)(2,1)} %collective-permute-done.3.refs_3_.refs_9_.refs_13_), channel_id=1, source_target_pairs={{0,2},{2,0},{1,3},{3,1},{4,6},{6,4},{5,7},{7,5},{8,10},{10,8},{9,1... | collective-permute-start | bytes 4718600 | tf_op jit(solution)/shard_map/ppermute | solution.py:800
  234.6 38.5 %copy-start.25 = (f32[1,256]{1,0:T(1,128)S(1)}, f32[1,256]{1,0:T(1,128)}, u32[]{:S(2)}) copy-start(f32[1,256]{1,0:T(1,128)} %get-tuple-element.145) | copy-start | bytes 3076
  234.6 39.9 %copy-start.14 = (f32[2048]{0:T(1024)S(1)}, f32[2048]{0:T(1024)}, u32[]{:S(2)}) copy-start(f32[2048]{0:T(1024)} %get-tuple-element.256) | copy-start | bytes 24580
  271.6 68.4 %collective-permute-start.11 = (bf16[1024,1024]{1,0:T(8,128)(2,1)}, bf16[1024,1024]{1,0:T(8,128)(2,1)}, u32[]{:S(2)}, u32[]{:S(2)}) collective-permute-start(bf16[1024,1024]{1,0:T(8,128)(2,1)} %get-tuple-element.163), channel_id=1, source_target_pairs={{0,2},{2,0},{1,3},{3,1},{4,6},{6,4},{5,7},{7,5},{8,10},{10,8},{9,1... | collective-permute-start | bytes 6291464 | tf_op jit(solution)/shard_map/ppermute | solution.py:860
  280.4 124.3 %collective-permute-start.13 = (bf16[512,512]{1,0:T(8,128)(2,1)}, bf16[512,512]{1,0:T(8,128)(2,1)}, u32[]{:S(2)}, u32[]{:S(2)}) collective-permute-start(bf16[512,512]{1,0:T(8,128)(2,1)} %get-tuple-element.181), channel_id=1, source_target_pairs={{0,16},{16,0},{1,17},{17,1},{2,18},{18,2},{3,19},{19,3},{4,20},{20... | collective-permute-start | bytes 1572872 | tf_op jit(solution)/shard_map/ppermute | solution.py:872
  315.2 22.7 %copy-start.24 = (f32[1,512]{1,0:T(1,128)S(1)}, f32[1,512]{1,0:T(1,128)}, u32[]{:S(2)}) copy-start(f32[1,512]{1,0:T(1,128)} %get-tuple-element.159) | copy-start | bytes 6148
  315.2 24.1 %copy-start.15 = (f32[2048]{0:T(1024)S(1)}, f32[2048]{0:T(1024)}, u32[]{:S(2)}) copy-start(f32[2048]{0:T(1024)} %get-tuple-element.256) | copy-start | bytes 24580
  334.9 65.2 %collective-permute-start.12 = (bf16[1024,512]{1,0:T(8,128)(2,1)}, bf16[1024,512]{1,0:T(8,128)(2,1)S(1)}, u32[]{:S(2)}, u32[]{:S(2)}) collective-permute-start(bf16[1024,512]{1,0:T(8,128)(2,1)} %get-tuple-element.178), channel_id=1, source_target_pairs={{0,2},{2,0},{1,3},{3,1},{4,6},{6,4},{5,7},{7,5},{8,10},{10,8},{9,1... | collective-permute-start | bytes 3145736 | tf_op jit(solution)/shard_map/ppermute | solution.py:860
  336.5 95.7 %collective-permute-start.17 = (bf16[1024,1024]{1,0:T(8,128)(2,1)}, bf16[1024,1024]{1,0:T(8,128)(2,1)}, u32[]{:S(2)}, u32[]{:S(2)}) collective-permute-start(bf16[1024,1024]{1,0:T(8,128)(2,1)} %get-tuple-element.190), channel_id=1, source_target_pairs={{0,2},{2,0},{1,3},{3,1},{4,6},{6,4},{5,7},{7,5},{8,10},{10,8},{9,1... | collective-permute-start | bytes 6291464 | tf_op jit(solution)/shard_map/ppermute | solution.py:860
  344.3 63.0 %collective-permute-start.14 = (bf16[512,1024]{1,0:T(8,128)(2,1)}, bf16[512,1024]{1,0:T(8,128)(2,1)S(1)}, u32[]{:S(2)}, u32[]{:S(2)}) collective-permute-start(bf16[512,1024]{1,0:T(8,128)(2,1)} %get-tuple-element.182), channel_id=1, source_target_pairs={{0,16},{16,0},{1,17},{17,1},{2,18},{18,2},{3,19},{19,3},{4,20},{20... | collective-permute-start | bytes 3145736 | tf_op jit(solution)/shard_map/ppermute | solution.py:872
  400.0 15.9 %collective-permute-start.15 = (bf16[1024,2048]{1,0:T(8,128)(2,1)}, bf16[1024,2048]{1,0:T(8,128)(2,1)}, u32[]{:S(2)}, u32[]{:S(2)}) collective-permute-start(bf16[1024,2048]{1,0:T(8,128)(2,1)} %get-tuple-element.184), channel_id=1, source_target_pairs={{0,1},{1,0},{2,3},{3,2},{4,5},{5,4},{6,7},{7,6},{8,9},{9,8},{10,11... | collective-permute-start | bytes 12582920 | tf_op jit(solution)/shard_map/ppermute | solution.py:934
  400.0 24.0 %collective-permute-start.16 = (bf16[1024,2048]{1,0:T(8,128)(2,1)}, bf16[1024,2048]{1,0:T(8,128)(2,1)}, u32[]{:S(2)}, u32[]{:S(2)}) collective-permute-start(bf16[1024,2048]{1,0:T(8,128)(2,1)} %get-tuple-element.187), channel_id=1, source_target_pairs={{0,1},{1,0},{2,3},{3,2},{4,5},{5,4},{6,7},{7,6},{8,9},{9,8},{10,11... | collective-permute-start | bytes 12582920 | tf_op jit(solution)/shard_map/ppermute | solution.py:934
  404.7 36.6 %collective-permute-start.19 = (bf16[512,512]{1,0:T(8,128)(2,1)}, bf16[512,512]{1,0:T(8,128)(2,1)}, u32[]{:S(2)}, u32[]{:S(2)}) collective-permute-start(bf16[512,512]{1,0:T(8,128)(2,1)} %get-tuple-element.194), channel_id=1, source_target_pairs={{0,16},{16,0},{1,17},{17,1},{2,18},{18,2},{3,19},{19,3},{4,20},{20... | collective-permute-start | bytes 1572872 | tf_op jit(solution)/shard_map/ppermute | solution.py:872
  412.4 80.6 %all-to-all-start.4 = ((bf16[8,64,1536]{2,1,0:T(8,128)(2,1)}), bf16[8,64,1536]{2,1,0:T(8,128)(2,1)S(1)}, u32[]{:S(2)}, u32[]{:S(2)}) async-start(bf16[8,64,1536]{2,1,0:T(8,128)(2,1)} %bitcast.118), calls=%async_computation.4 | async-start | bytes 3145728 | tf_op jit(solution)/shard_map/all_to_all | solution.py:886
  436.5 49.2 %collective-permute-start.18 = (bf16[512,1024]{1,0:T(8,128)(2,1)}, bf16[512,1024]{1,0:T(8,128)(2,1)S(1)}, u32[]{:S(2)}, u32[]{:S(2)}) collective-permute-start(bf16[512,1024]{1,0:T(8,128)(2,1)} %get-tuple-element.193), channel_id=1, source_target_pairs={{0,16},{16,0},{1,17},{17,1},{2,18},{18,2},{3,19},{19,3},{4,20},{20... | collective-permute-start | bytes 3145736 | tf_op jit(solution)/shard_map/ppermute | solution.py:872
  437.1 59.5 %collective-permute-start.20 = (bf16[512,2048]{1,0:T(8,128)(2,1)}, bf16[512,2048]{1,0:T(8,128)(2,1)}, u32[]{:S(2)}, u32[]{:S(2)}) collective-permute-start(bf16[512,2048]{1,0:T(8,128)(2,1)} %get-tuple-element.198), channel_id=1, source_target_pairs={{0,4},{4,0},{1,5},{5,1},{2,6},{6,2},{3,7},{7,3},{8,12},{12,8},{9,1... | collective-permute-start | bytes 6291464 | tf_op jit(solution)/shard_map/ppermute | solution.py:934
  439.8 79.9 %collective-permute-start.21 = (bf16[512,2048]{1,0:T(8,128)(2,1)}, bf16[512,2048]{1,0:T(8,128)(2,1)}, u32[]{:S(2)}, u32[]{:S(2)}) collective-permute-start(bf16[512,2048]{1,0:T(8,128)(2,1)} %get-tuple-element.206), channel_id=1, source_target_pairs={{0,8},{8,0},{1,9},{9,1},{2,10},{10,2},{3,11},{11,3},{4,12},{12,4},... | collective-permute-start | bytes 6291464 | tf_op jit(solution)/shard_map/ppermute | solution.py:934
  492.9 8.5 %copy-start.7 = (bf16[8,64,1536]{2,1,0:T(8,128)(2,1)}, bf16[8,64,1536]{2,1,0:T(8,128)(2,1)S(1)}, u32[]{:S(2)}) copy-start(bf16[8,64,1536]{2,1,0:T(8,128)(2,1)S(1)} %all-to-all-done.4.refs_0_.refs_4_) | copy-start | bytes 4718596
  492.9 42.2 %all-to-all-start.3 = ((bf16[8,80,1536]{2,1,0:T(8,128)(2,1)}), bf16[8,80,1536]{2,1,0:T(8,128)(2,1)S(1)}, u32[]{:S(2)}, u32[]{:S(2)}) async-start(bf16[8,80,1536]{2,1,0:T(8,128)(2,1)} %shard_map.379), calls=%async_computation.3 | async-start | bytes 3932160 | tf_op jit(solution)/shard_map/all_to_all | solution.py:886
  524.7 29.7 %collective-permute-start.22 = (bf16[256,2048]{1,0:T(8,128)(2,1)}, bf16[256,2048]{1,0:T(8,128)(2,1)}, u32[]{:S(2)}, u32[]{:S(2)}) collective-permute-start(bf16[256,2048]{1,0:T(8,128)(2,1)} %get-tuple-element.227), channel_id=1, source_target_pairs={{0,4},{4,0},{1,5},{5,1},{2,6},{6,2},{3,7},{7,3},{8,12},{12,8},{9,1... | collective-permute-start | bytes 3145736 | tf_op jit(solution)/shard_map/ppermute | solution.py:959
  526.6 32.7 %collective-permute-start.23 = (bf16[256,2048]{1,0:T(8,128)(2,1)S(1)}, bf16[256,2048]{1,0:T(8,128)(2,1)}, u32[]{:S(2)}, u32[]{:S(2)}) collective-permute-start(bf16[256,2048]{1,0:T(8,128)(2,1)S(1)} %copy-done.28), channel_id=1, source_target_pairs={{0,8},{8,0},{1,9},{9,1},{2,10},{10,2},{3,11},{11,3},{4,12},{12,4},... | collective-permute-start | bytes 3145736 | tf_op jit(solution)/shard_map/ppermute | solution.py:959
  549.9 15.3 %collective-permute-start.24 = (f32[768]{0:T(1024)S(1)}, f32[768]{0:T(1024)S(1)}, u32[]{:S(2)}, u32[]{:S(2)}) collective-permute-start(f32[768]{0:T(1024)S(1)} %get-tuple-element.249), channel_id=1, source_target_pairs={{0,2},{2,0},{1,3},{3,1},{4,6},{6,4},{5,7},{7,5},{8,10},{10,8},{9,1... | collective-permute-start | bytes 9224 | tf_op jit(solution)/shard_map/ppermute | solution.py:1026
  551.5 13.7 %collective-permute-start.25 = (f32[768]{0:T(1024)S(1)}, f32[768]{0:T(1024)S(1)}, u32[]{:S(2)}, u32[]{:S(2)}) collective-permute-start(f32[768]{0:T(1024)S(1)} %get-tuple-element.248), channel_id=1, source_target_pairs={{0,16},{16,0},{1,17},{17,1},{2,18},{18,2},{3,19},{19,3},{4,20},{20... | collective-permute-start | bytes 9224 | tf_op jit(solution)/shard_map/ppermute | solution.py:1027
  551.5 13.7 %collective-permute-start.26 = (f32[768]{0:T(1024)S(1)}, f32[768]{0:T(1024)S(1)}, u32[]{:S(2)}, u32[]{:S(2)}) collective-permute-start(f32[768]{0:T(1024)S(1)} %get-tuple-element.247), channel_id=1, source_target_pairs={{0,18},{2,16},{16,2},{18,0},{1,19},{3,17},{17,3},{19,1},{4,22},{6,... | collective-permute-start | bytes 9224 | tf_op jit(solution)/shard_map/ppermute | solution.py:1028
  (20 other events, 54.1 us)
Sparse Core Ops, SparseCore 0:
  12.0 72.6 all-gather.4
  102.9 74.4 all-gather.6
